TPU v7x, 32 devices: a whole 2x2x4 slice. The times are simulated.
32 devices in a mesh: dp: 32 (over z, y, x, core).
Axes of the slice: x: 2, y: 2, z: 4, core: 2. Of those that a mesh axis runs over, the one named last changes fastest.
Arguments:
- targets: bfloat16 [32768, 512], P('dp')
- memory: bfloat16 [32768, 512], P('dp'), may hold values from -6 to 6
- target_ids: int32 [32768], P('dp'), may hold values from 0 to 7, as said below
- memory_ids: int32 [32768], P('dp'), may hold values from 0 to 7, as said below
- cotangent: bfloat16 [32768, 512], P('dp'), may hold values from -6 to 6
- params: float32 [4203008], P('dp')
- first_moment: float32 [4203008], P('dp')
- second_moment: float32 [4203008], P('dp')
Outputs:
- layer_out: bfloat16 [32768, 512], P('dp')
- input_grad: bfloat16 [32768, 512], P('dp')
- memory_grad: bfloat16 [32768, 512], P('dp')
- grad_norm: float32 [], replicated
- param_grad: float32 [4203008], P('dp')
- vector_grad: float32 [8704], replicated
- new_params: float32 [4203008], P('dp')
- new_first: float32 [4203008], P('dp')
- new_second: float32 [4203008], P('dp')
- params_low: bfloat16 [4203008], P('dp')
Inputs may be any that keep to these rules, and one draw needn't show every extreme that they name: `target_ids`: within each sequence of 1024 target tokens the ids start at 0 and rise by 0 or 1 from token to token; the same sequence's memory tokens carry exactly the same set of ids in the same way. `memory_ids`: within each sequence of 1024 memory tokens the ids start at 0 and rise by 0 or 1 from token to token, with the same set of ids as the sequence's target tokens.
All inputs are finite; a program needn't handle non-finite values.
Results may differ from a plain program's by a relative error of at most 0.018.
The roundings to bfloat16 on the way count: a program that leaves them out, or rounds other values in their place, can miss the bound.
Values may be sent and summed in bfloat16 or wider, within the bound.
No kernel may reach another device: no remote copies, remote signals or barrier semaphores. Data moves between devices by JAX's collectives and lax.ppermute only.
A program may use at most 192 MiB of HBM per device.

v0:
```python
import functools
import jax
import jax.numpy as jnp
from jax import lax
from jax.experimental import pallas as pl
from jax.experimental.pallas import tpu as pltpu
from jax.sharding import PartitionSpec as P

D = 512
FF = 2048
HEADS = 8
LEN = 1024
STEP = 10
ROWS = 256
BLOCKS = LEN // ROWS
LANES = 128
PAIRS = D // LANES
MASK_LANE = 32
EARLY_PAIRS = 3

eps_norm = 1e-05
beta_one = 0.9
beta_two = 0.999
adam_eps = 1e-08
step_rate = 0.05
weight_decay = 0.01
clip_limit = 1.0
masked_value = -1e30
log2_e = 1.4426950408889634
query_scale = 0.125 * log2_e
key_scale = 1.0 / log2_e

BF = jnp.bfloat16
F32 = jnp.float32
VMEM_BYTES = 60 * 1024 * 1024


def nn(a, b):
    return jnp.dot(a, b, preferred_element_type=F32)


def nt(a, b):
    return lax.dot_general(a, b, (((1,), (1,)), ((), ())), preferred_element_type=F32)


def tn(a, b):
    return lax.dot_general(a, b, (((0,), (0,)), ((), ())), preferred_element_type=F32)


def layer_norm(resid):
    center = resid - jnp.mean(resid, axis=1, keepdims=True)
    inv_std = lax.rsqrt(jnp.mean(center * center, axis=1, keepdims=True) + eps_norm)
    return center * inv_std, inv_std


def norm_back(grad, normed, inv_std, gain):
    scaled = grad * gain
    return inv_std * (
        scaled
        - jnp.mean(scaled, axis=1, keepdims=True)
        - normed * jnp.mean(scaled * normed, axis=1, keepdims=True)
    )


def half_row(parity):
    lane = lax.broadcasted_iota(jnp.int32, (1, LANES), 1)
    inside = (lane // 64) == parity
    return jnp.where(inside, 1.0, 0.0).astype(BF)


def lane_row(first, count):
    lane = lax.broadcasted_iota(jnp.int32, (1, LANES), 1)
    inside = (lane >= first) & (lane < first + count)
    return jnp.where(inside, 1.0, 0.0).astype(BF)


def causal_bias(transposed):
    row = lax.broadcasted_iota(jnp.int32, (ROWS, ROWS), 0)
    col = lax.broadcasted_iota(jnp.int32, (ROWS, ROWS), 1)
    ok = (row <= col) if transposed else (col <= row)
    return jnp.where(ok, 0.0, masked_value)


def attend_forward(q_ref, k_ref, v_ref, qa_ref, ka_ref, o_ref, qal_ref, causal):
    lane = lax.broadcasted_iota(jnp.int32, (ROWS, LANES), 1)
    low = lane < 64
    bias = causal_bias(False) if causal else None
    for qb in range(BLOCKS):
        rows = pl.ds(qb * ROWS, ROWS)
        keys = (qb + 1) * ROWS if causal else LEN
        qa = qa_ref[rows, :]

        def one_pair(pair, lse_parts):
            lanes = pl.ds(pl.multiple_of(pair * LANES, LANES), LANES)
            q_pair = q_ref[rows, lanes]
            k_cat = jnp.concatenate([k_ref[:keys, lanes], ka_ref[:keys, :]], axis=1)
            v_pair = v_ref[:keys, lanes]
            outs = []
            for parity in range(2):
                half = half_row(parity)
                head = pair * 2 + parity
                q_cat = jnp.concatenate([q_pair * half, qa], axis=1)
                scores = nt(q_cat, k_cat)
                if causal:
                    diag = scores[:, keys - ROWS :] + bias
                    scores = (
                        jnp.concatenate([scores[:, : keys - ROWS], diag], axis=1) if qb else diag
                    )
                top = jnp.max(scores, axis=1, keepdims=True)
                probs = jnp.exp2(scores - top).astype(BF)
                mixed = nn(probs, v_pair * half + (1.0 - half).astype(BF))
                turned = pltpu.roll(mixed, 64, 1)
                outs.append(mixed / turned)
                total = turned if parity == 0 else mixed
                lse = -(top + jnp.log2(total))
                first = lse.astype(BF).astype(F32)
                rest = lse - first
                second = rest.astype(BF).astype(F32)
                base = head * 3
                lse_parts = jnp.where(lane == base, first, lse_parts)
                lse_parts = jnp.where(lane == base + 1, second, lse_parts)
                lse_parts = jnp.where(lane == base + 2, rest - second, lse_parts)
            o_ref[rows, lanes] = jnp.where(low, outs[0], outs[1]).astype(BF)
            return lse_parts

        lse_parts = lax.fori_loop(0, PAIRS, one_pair, jnp.zeros((ROWS, LANES), F32))
        qal_ref[rows, :] = (qa.astype(F32) + lse_parts).astype(BF)


def attend_backward(
    q_ref, k_ref, v_ref, do_ref, qal_ref, del_ref, ka_ref, dq_ref, dk_ref, dv_ref, p_ref, s_ref, causal,
    span=(0, PAIRS),
):
    bias = causal_bias(True) if causal else None

    def one_pair(pair, carry):
        lanes = pl.ds(pl.multiple_of(pair * LANES, LANES), LANES)
        k_pair = k_ref[:, lanes]
        k_turn = k_pair.T
        v_pair = v_ref[:, lanes]
        dq_parts = [[], []]
        for parity in range(2):
            head = pair * 2 + parity
            half = half_row(parity)
            k_cat = jnp.concatenate([k_pair * half, ka_ref[...] + lane_row(head * 3, 3)], axis=1)
            ones = jnp.broadcast_to(lane_row(head * 2, 2), (LEN, LANES))
            v_cat = jnp.concatenate([v_pair * half, ones], axis=1)
            for qb in range(BLOCKS):
                rows = pl.ds(qb * ROWS, ROWS)
                keys = (qb + 1) * ROWS if causal else LEN
                q_cat = jnp.concatenate([q_ref[rows, lanes], qal_ref[rows, :]], axis=1)
                do_cat = jnp.concatenate([do_ref[rows, lanes], del_ref[rows, :]], axis=1)
                scores = nt(k_cat[:keys], q_cat)
                if causal:
                    diag = scores[keys - ROWS :] + bias
                    scores = jnp.concatenate([scores[: keys - ROWS], diag], axis=0) if qb else diag
                probs = jnp.exp2(scores)
                p_ref[parity, :keys, rows] = probs.astype(BF)
                grads = (probs * nt(v_cat[:keys], do_cat)).astype(BF)
                s_ref[parity, :keys, rows] = grads
                dq_parts[parity].append(
                    nn(k_turn[parity * 64 : parity * 64 + 64, :keys], grads)
                )
        for qb in range(BLOCKS):
            rows = pl.ds(qb * ROWS, ROWS)
            dq = jnp.concatenate([dq_parts[0][qb], dq_parts[1][qb]], axis=0) * 0.125
            dq_ref[rows, lanes] = dq.T.astype(BF)
        for kb in range(BLOCKS):
            rows = pl.ds(kb * ROWS, ROWS)
            first = kb * ROWS if causal else 0
            tail = pl.ds(first, LEN - first)
            do_pair = do_ref[tail, lanes]
            q_pair = q_ref[tail, lanes]
            dv = nn(p_ref[0, rows, tail], do_pair * half_row(0))
            dv = dv + nn(p_ref[1, rows, tail], do_pair * half_row(1))
            dv_ref[rows, lanes] = dv.astype(BF)
            dk = nn(s_ref[0, rows, tail], q_pair * half_row(0))
            dk = dk + nn(s_ref[1, rows, tail], q_pair * half_row(1))
            dk_ref[rows, lanes] = (dk * key_scale).astype(BF)
        return carry

    lax.fori_loop(span[0], span[1], one_pair, 0)


def mix_gradient(g_ref, w_out, o_ref, do_ref, del_ref):
    lane = lax.broadcasted_iota(jnp.int32, (ROWS, LANES), 1)
    even = lane % 2 == 0
    col = lax.broadcasted_iota(jnp.int32, (D, LANES), 0) // 64
    pick = jnp.where(lax.broadcasted_iota(jnp.int32, (D, LANES), 1) // 2 == col, -1.0, 0.0).astype(BF)
    for qb in range(BLOCKS):
        rows = pl.ds(qb * ROWS, ROWS)
        do = nt(g_ref[rows, :], w_out).astype(BF)
        do_ref[rows, :] = do
        prod = do.astype(F32) * o_ref[rows, :].astype(F32)
        high = prod.astype(BF)
        inner = nn(high, pick) + nn((prod - high.astype(F32)).astype(BF), pick)
        first = inner.astype(BF).astype(F32)
        del_ref[rows, :] = jnp.where(even, first, inner - first).astype(BF)


def vec_row(vec_ref, index):
    return vec_ref[index : index + 1, :]


def fetch(all_ref, block, w_ref, sem):
    copy = pltpu.make_async_copy(all_ref.at[pl.ds(8 * block, 8)], w_ref, sem)
    copy.start()
    return copy


def square(w_ref, matrix):
    return w_ref[2 * matrix : 2 * matrix + 2].reshape(D, D)


def put_square(mine_ref, other_ref, core, matrix, turned_ref, grad):
    for ref, half in ((mine_ref, core), (other_ref, 1 - core)):
        rows = turned_ref[pl.ds(pl.multiple_of(half * ROWS, ROWS), ROWS), :]
        ref[matrix, :ROWS, :] = nn(rows, grad).astype(BF)


def put_square_tn(mine_ref, other_ref, core, matrix, left_ref, grad):
    for ref, half in ((mine_ref, core), (other_ref, 1 - core)):
        cols = left_ref[:, pl.ds(pl.multiple_of(half * ROWS, ROWS), ROWS)]
        ref[matrix, :ROWS, :] = tn(cols, grad).astype(BF)


def self_forward_kernel(
    core_ref, own_ref, other_ref, x_ref, vec_ref, qa_ref, ka_ref,
    q_ref, k_ref, v_ref, o_ref, qal_ref, n_ref, r_ref,
    w_ref, sems,
):
    core, place_xy = core_ref[0], core_ref[1]
    copies = []
    for matrix in range(4):
        for half, source in enumerate((own_ref, other_ref)):
            place = 2 * matrix + (core if half == 0 else 1 - core)
            copies.append(
                pltpu.make_async_copy(
                    source.at[matrix ^ place_xy, pl.ds(0, ROWS)], w_ref.at[place], sems.at[2 * matrix + half]
                )
            )
    for copy in copies:
        copy.start()
    for copy in copies[:6]:
        copy.wait()
    for qb in range(BLOCKS):
        rows = pl.ds(qb * ROWS, ROWS)
        x = x_ref[rows, :]
        q_ref[rows, :] = ((nn(x, square(w_ref, 0)) + vec_row(vec_ref, 6)) * query_scale).astype(BF)
        k_ref[rows, :] = nn(x, square(w_ref, 1)).astype(BF)
        v_ref[rows, :] = (nn(x, square(w_ref, 2)) + vec_row(vec_ref, 7)).astype(BF)
    attend_forward(q_ref, k_ref, v_ref, qa_ref, ka_ref, o_ref, qal_ref, True)
    for copy in copies[6:]:
        copy.wait()
    for qb in range(BLOCKS):
        rows = pl.ds(qb * ROWS, ROWS)
        resid = x_ref[rows, :].astype(F32) + nn(o_ref[rows, :], square(w_ref, 3)) + vec_row(vec_ref, 8)
        normed, inv_std = layer_norm(resid)
        n_ref[rows, :] = normed
        r_ref[rows, :] = jnp.broadcast_to(inv_std, (ROWS, LANES))


def cross_forward_kernel(
    all_ref, n1_ref, m_ref, vec_ref, qa_ref, ka_ref,
    q_ref, k_ref, v_ref, o_ref, qal_ref, n_ref, r_ref,
    w_ref, sem,
):
    fetch(all_ref, 1, w_ref, sem).wait()
    for qb in range(BLOCKS):
        rows = pl.ds(qb * ROWS, ROWS)
        h = (n1_ref[rows, :] * vec_row(vec_ref, 0) + vec_row(vec_ref, 1)).astype(BF)
        m = m_ref[rows, :]
        q_ref[rows, :] = ((nn(h, square(w_ref, 0)) + vec_row(vec_ref, 9)) * query_scale).astype(BF)
        k_ref[rows, :] = nn(m, square(w_ref, 1)).astype(BF)
        v_ref[rows, :] = (nn(m, square(w_ref, 2)) + vec_row(vec_ref, 10)).astype(BF)
    attend_forward(q_ref, k_ref, v_ref, qa_ref, ka_ref, o_ref, qal_ref, False)
    for qb in range(BLOCKS):
        rows = pl.ds(qb * ROWS, ROWS)
        h = n1_ref[rows, :] * vec_row(vec_ref, 0) + vec_row(vec_ref, 1)
        resid = h + nn(o_ref[rows, :], square(w_ref, 3)) + vec_row(vec_ref, 11)
        normed, inv_std = layer_norm(resid)
        n_ref[rows, :] = normed
        r_ref[rows, :] = jnp.broadcast_to(inv_std, (ROWS, LANES))


def col_sum(x):
    return jnp.sum(x.astype(F32), axis=0, keepdims=True)


def ffn_kernel(
    core_ref, all_ref, n2_ref, r2_ref, cot_ref, vec_ref,
    out_ref, mine_ref, other_ref, dr_ref, vg_ref,
    w1_ref, w2_ref, u_ref, da_ref, h_ref, dz_ref, f_ref, ht_ref, sem1, sem2,
):
    copy1 = fetch(all_ref, 2, w1_ref, sem1)
    copy2 = fetch(all_ref, 3, w2_ref, sem2)
    copy1.wait()
    copy2.wait()

    def w1_block(j):
        return w1_ref[:, 64 * j : 64 * j + 64].reshape(D, D)

    def w2_block(j):
        return square(w2_ref, j)

    vg_ref[...] = jnp.zeros_like(vg_ref)

    def one_tile(tile, carry):
        rows = pl.ds(pl.multiple_of(tile * ROWS, ROWS), ROWS)
        n2 = n2_ref[rows, :]
        h2 = n2 * vec_row(vec_ref, 2) + vec_row(vec_ref, 3)
        h2_low = h2.astype(BF)
        h_ref[rows, :] = h2_low
        resid = h2 + vec_row(vec_ref, 16)
        for j in range(4):
            a = nn(h2_low, w1_block(j)) + vec_row(vec_ref, 12 + j)
            s = 0.5 * jnp.tanh(0.5 * a) + 0.5
            u = (a * s).astype(BF)
            u_ref[rows, j * D : (j + 1) * D] = u
            f_ref[:, j * D : (j + 1) * D] = s * (1.0 + a * (1.0 - s))
            resid = resid + nn(u, w2_block(j))
        n3, inv3 = layer_norm(resid)
        gain3 = vec_row(vec_ref, 4)
        out_ref[rows, :] = (n3 * gain3 + vec_row(vec_ref, 5)).astype(BF)
        cot = cot_ref[rows, :].astype(F32)
        dr3 = norm_back(cot, n3, inv3, gain3)
        dz = dr3.astype(BF)
        dz_ref[rows, :] = dz
        vg_ref[4:5, :] += col_sum(cot * n3)
        vg_ref[5:6, :] += col_sum(cot)
        vg_ref[16:17, :] += col_sum(dz)
        dh = dr3
        for j in range(4):
            da = (nt(dz, w2_block(j)) * f_ref[:, j * D : (j + 1) * D]).astype(BF)
            da_ref[rows, j * D : (j + 1) * D] = da
            vg_ref[12 + j : 13 + j, :] += col_sum(da)
            dh = dh + nt(da, w1_block(j))
        vg_ref[2:3, :] += col_sum(dh * n2)
        vg_ref[3:4, :] += col_sum(dh)
        dr2 = norm_back(dh, n2, r2_ref[rows, 0:1], vec_row(vec_ref, 2))
        dr_ref[rows, :] = dr2
        vg_ref[11:12, :] += col_sum(dr2.astype(BF))
        return carry

    lax.fori_loop(0, BLOCKS, one_tile, 0)
    core = core_ref[0]
    ht_ref[...] = jnp.swapaxes(h_ref[...].T.reshape(4, 2, 64, LEN), 0, 1).reshape(2, ROWS, LEN)
    for j in range(4):
        da = da_ref[:, j * D : (j + 1) * D]
        dz = dz_ref[...]
        for ref, half in ((mine_ref, core), (other_ref, 1 - core)):
            dw1 = nn(ht_ref[half], da).astype(BF)
            ref[:, 64 * j : 64 * j + 64, :] = dw1.reshape(4, 64, D)
            cols = pl.ds(pl.multiple_of(j * D + half * ROWS, ROWS), ROWS)
            ref[j, ROWS:, :] = tn(u_ref[:, cols], dz).astype(BF)


def cross_backward_kernel(
    core_ref, all_ref, dr2_ref, vec_ref, q_ref, k_ref, v_ref, o_ref, qal_ref, ka_ref, n1_ref, r1_ref, mt_ref, vf_ref,
    mine_ref, other_ref, mg_ref, dr1_ref,
    g_ref, do_ref, del_ref, dq_ref, dk_ref, dv_ref, p_ref, s_ref, h_ref, w_ref, vg_ref, sem,
):
    core = core_ref[0]
    copy = fetch(all_ref, 1, w_ref, sem)
    for qb in range(BLOCKS):
        rows = pl.ds(qb * ROWS, ROWS)
        g_ref[rows, :] = dr2_ref[rows, :].astype(BF)
        h_ref[rows, :] = (n1_ref[rows, :] * vec_row(vec_ref, 0) + vec_row(vec_ref, 1)).astype(BF)
    copy.wait()
    mix_gradient(g_ref, square(w_ref, 3), o_ref, do_ref, del_ref)
    put_square_tn(mine_ref, other_ref, core, 3, o_ref, g_ref[...])
    attend_backward(
        q_ref, k_ref, v_ref, do_ref, qal_ref, del_ref, ka_ref, dq_ref, dk_ref, dv_ref, p_ref, s_ref, False
    )
    put_square_tn(mine_ref, other_ref, core, 0, h_ref, dq_ref[...])
    put_square(mine_ref, other_ref, core, 1, mt_ref, dk_ref[...])
    put_square(mine_ref, other_ref, core, 2, mt_ref, dv_ref[...])
    vg_ref[...] = vf_ref[...]
    for qb in range(BLOCKS):
        rows = pl.ds(qb * ROWS, ROWS)
        dq = dq_ref[rows, :]
        dk = dk_ref[rows, :]
        dv = dv_ref[rows, :]
        mg_ref[rows, :] = (nt(dk, square(w_ref, 1)) + nt(dv, square(w_ref, 2))).astype(BF)
        vg_ref[9:10, :] += col_sum(dq)
        vg_ref[10:11, :] += col_sum(dv)
        dh = dr2_ref[rows, :] + nt(dq, square(w_ref, 0))
        n1 = n1_ref[rows, :]
        vg_ref[0:1, :] += col_sum(dh * n1)
        vg_ref[1:2, :] += col_sum(dh)
        dr1 = norm_back(dh, n1, r1_ref[rows, 0:1], vec_row(vec_ref, 0))
        dr1_ref[rows, :] = dr1
        vg_ref[8:9, :] += col_sum(dr1.astype(BF))
    blank = jnp.zeros((12, D), F32)
    for ref, half in ((mine_ref, core), (other_ref, 1 - core)):
        for xy in range(4):
            low, high = vg_ref[8 * xy : 8 * xy + 4, :], vg_ref[8 * xy + 4 : 8 * xy + 8, :]
            rows = jnp.where(half == 0, low, high)
            ref[xy, ROWS:, :] = jnp.concatenate([rows, blank], axis=0).astype(BF)


def self_backward_start_kernel(
    all_ref, dr1_ref, q_ref, k_ref, v_ref, o_ref, qal_ref, ka_ref,
    do_ref, del_ref, dq_ref, dk_ref, dv_ref,
    g_ref, p_ref, s_ref, w_ref, sem,
):
    copy = fetch(all_ref, 0, w_ref, sem)
    for qb in range(BLOCKS):
        rows = pl.ds(qb * ROWS, ROWS)
        g_ref[rows, :] = dr1_ref[rows, :].astype(BF)
    copy.wait()
    mix_gradient(g_ref, square(w_ref, 3), o_ref, do_ref, del_ref)
    attend_backward(
        q_ref, k_ref, v_ref, do_ref, qal_ref, del_ref, ka_ref, dq_ref, dk_ref, dv_ref, p_ref, s_ref, True,
        (0, EARLY_PAIRS),
    )


def self_backward_end_kernel(
    core_ref, all_ref, dr1_ref, q_ref, k_ref, v_ref, o_ref, qal_ref, ka_ref, xt_ref,
    do_ref, del_ref, dqe_ref, dke_ref, dve_ref,
    mine_ref, other_ref, ig_ref,
    g_ref, dq_ref, dk_ref, dv_ref, p_ref, s_ref, w_ref, late_ref, sem,
):
    core = core_ref[0]
    copy = fetch(all_ref, 0, w_ref, sem)
    for qb in range(BLOCKS):
        rows = pl.ds(qb * ROWS, ROWS)
        g_ref[rows, :] = dr1_ref[rows, :].astype(BF)
    early = EARLY_PAIRS * LANES
    for ref, source in ((dq_ref, dqe_ref), (dk_ref, dke_ref), (dv_ref, dve_ref)):
        ref[:, :early] = source[:, :early]
    attend_backward(
        q_ref, k_ref, v_ref, do_ref, qal_ref, del_ref, ka_ref, dq_ref, dk_ref, dv_ref, p_ref, s_ref, True,
        (EARLY_PAIRS, PAIRS),
    )
    copy.wait()
    put_square_tn(mine_ref, other_ref, core, 3, o_ref, g_ref[...])
    put_square(mine_ref, other_ref, core, 0, xt_ref, dq_ref[...])
    put_square(mine_ref, other_ref, core, 1, xt_ref, dk_ref[...])
    put_square(mine_ref, other_ref, core, 2, xt_ref, dv_ref[...])
    late_ref[...] = jnp.zeros_like(late_ref)
    for qb in range(BLOCKS):
        rows = pl.ds(qb * ROWS, ROWS)
        dq = dq_ref[rows, :]
        dk = dk_ref[rows, :]
        dv = dv_ref[rows, :]
        ig_ref[rows, :] = (
            dr1_ref[rows, :]
            + nt(dq, square(w_ref, 0))
            + nt(dk, square(w_ref, 1))
            + nt(dv, square(w_ref, 2))
        ).astype(BF)
        late_ref[0:1, :] += col_sum(dq)
        late_ref[1:2, :] += col_sum(dv)
    for ref, half in ((mine_ref, core), (other_ref, 1 - core)):
        for xy in range(4):
            place = pl.multiple_of((2 * (xy % 2) + half) * LANES, LANES)
            piece = late_ref[xy // 2 : xy // 2 + 1, pl.ds(place, LANES)]
            ref[xy, ROWS:, :] = jnp.zeros((16, D), BF)
            ref[xy, ROWS:, :LANES] = jnp.broadcast_to(piece, (16, LANES)).astype(BF)


def call(kernel, outs, scratch, flops, args, remote=(), sems=1):
    sds = [jax.ShapeDtypeStruct(shape, dtype) for shape, dtype in outs]
    moved = sum(a.size * a.dtype.itemsize for a in args)
    spaces = {"a": pl.ANY, "s": pltpu.SMEM, "v": pltpu.VMEM}
    kinds = dict(remote)
    memory = [pltpu.VMEM(shape, dtype) for shape, dtype in scratch]
    memory += [pltpu.SemaphoreType.DMA] * sems if sems < 8 else [pltpu.SemaphoreType.DMA((sems,))]
    return pl.pallas_call(
        kernel,
        out_shape=sds,
        in_specs=[
            pl.BlockSpec(memory_space=spaces[kinds.get(i, "v")]) for i in range(len(args))
        ],
        scratch_shapes=memory,
        compiler_params=pltpu.CompilerParams(vmem_limit_bytes=VMEM_BYTES),
        cost_estimate=pl.CostEstimate(flops=flops, bytes_accessed=moved, transcendentals=0),
    )(*args)


TOK = (LEN, D)
STAT = (LEN, LANES)
OCT = (8, ROWS, D)
unit = 2 * LEN * D * D
FORWARD_OUTS = [(TOK, BF)] * 4 + [(STAT, BF), (TOK, F32), (STAT, F32)]
HALVES = ((4, ROWS + 16, D), BF)
TOKB = (TOK, BF)
PROBS = ((2, LEN, LEN), BF)


def self_forward(*args):
    kinds = ((0, "s"), (1, "a"), (2, "a"))
    return call(self_forward_kernel, FORWARD_OUTS, [(OCT, BF)], 20 * unit, args, kinds, 8)


def cross_forward(*args):
    return call(cross_forward_kernel, FORWARD_OUTS, [(OCT, BF)], 25 * unit, args, ((0, "a"),))


KINDS = ((0, "s"), (1, "a"))


def ffn(*args):
    outs = [TOKB, ((4, 2 * ROWS, D), BF), ((4, 2 * ROWS, D), BF), (TOK, F32), ((32, D), F32)]
    scratch = [(OCT, BF), (OCT, BF), ((LEN, FF), BF), ((LEN, FF), BF), TOKB, TOKB]
    scratch += [((ROWS, FF), F32), ((2, ROWS, LEN), BF)]
    return call(ffn_kernel, outs, scratch, 26 * unit, args, KINDS, 2)


def cross_backward(*args):
    outs = [HALVES, HALVES, TOKB, (TOK, F32)]
    scratch = [TOKB, TOKB, (STAT, BF), TOKB, TOKB, TOKB, PROBS, PROBS, TOKB, (OCT, BF), ((32, D), F32)]
    return call(cross_backward_kernel, outs, scratch, 50 * unit, args, KINDS)


def self_backward_start(*args):
    outs = [TOKB, (STAT, BF), TOKB, TOKB, TOKB]
    scratch = [TOKB, PROBS, PROBS, (OCT, BF)]
    return call(self_backward_start_kernel, outs, scratch, 25 * unit, args, ((0, "a"),))


def self_backward_end(*args):
    outs = [HALVES, HALVES, TOKB]
    scratch = [TOKB, TOKB, TOKB, TOKB, PROBS, PROBS, (OCT, BF), ((8, D), F32)]
    return call(self_backward_end_kernel, outs, scratch, 2 * unit, args, KINDS)


SQUARES = 8 * D * D
VEC_ROWS = 17
VEC_LEN = VEC_ROWS * D


def groups_xy():
    return [[z * 8 + c * 2 + core for c in range(4)] for z in range(4) for core in range(2)]


def groups_z():
    return [[z * 8 + p for z in range(4)] for p in range(8)]


def swap(x, bit):
    return lax.ppermute(x, "dp", [(i, i ^ bit) for i in range(32)])


def turn_w1(chunk, here, out_first):
    if out_first:
        alt = chunk.reshape(64, 4, D).transpose(1, 0, 2).reshape(ROWS, D)
    else:
        alt = chunk.reshape(4, 64, D).transpose(1, 0, 2).reshape(ROWS, D)
    return jnp.where(here, alt, chunk)


def gather_first(buf, index):
    z = index // 8
    far = lax.ppermute(buf, "dp", [(p, 16 + p) for p in range(8)])
    held = jnp.where(z == 2, far, buf)
    near = lax.ppermute(held, "dp", [(z0 * 8 + p, z0 * 8 + 8 + p) for z0 in (0, 2) for p in range(8)])
    held = jnp.where(z % 2 == 1, near, held)
    side, up = swap(held, 2), swap(held, 4)
    half = held.shape[0] // 2
    corner = [swap(up[:half], 2), swap(side[half:], 4)]
    own = jnp.concatenate([held, side, up] + corner).reshape((4,) + held.shape)
    other = swap(own, 1)
    place = index % 8 // 2
    source = jnp.where(
        index % 2 == 0,
        lax.dynamic_index_in_dim(own, place, 0, keepdims=False)[ROWS:],
        lax.dynamic_index_in_dim(other, place, 0, keepdims=False)[ROWS:],
    )
    return own, other, source.astype(F32)


def gather_blocks(params, index):
    low = params.astype(BF)
    share = low.shape[0]
    shift = share - ROWS * D
    prev = lax.ppermute(low[share - VEC_LEN :], "dp", [(i, (i + 1) % 32) for i in range(32)])
    flat = lax.dynamic_slice(jnp.concatenate([prev, low]), (VEC_LEN - shift * index,), (ROWS * D,))
    chunk = turn_w1(flat.reshape(ROWS, D), index // 8 == 2, True)
    everything = lax.all_gather(chunk, "dp", axis=0)
    vec = jnp.pad(prev.reshape(VEC_ROWS, D), ((0, 15), (0, 0)))
    own, other, vec = gather_first(jnp.concatenate([chunk, vec]), index)
    return own, other, everything.reshape(32, ROWS, D), vec


def gather_plain(params, index):
    flat = lax.all_gather(params.astype(BF), "dp", axis=0, tiled=True)
    end = SQUARES + D * FF
    w1 = flat[SQUARES:end].reshape(8, 64, 4, D).transpose(0, 2, 1, 3).reshape(8, ROWS, D)
    mats = flat[:SQUARES].reshape(16, ROWS, D)
    w2 = flat[end : end + D * FF].reshape(8, ROWS, D)
    vec = flat[end + D * FF :].reshape(VEC_ROWS, D).astype(F32)
    pairs = mats[:8].reshape(4, 2, ROWS, D)
    own = lax.dynamic_index_in_dim(pairs, index % 2, 1, keepdims=False)
    other = lax.dynamic_index_in_dim(pairs, 1 - index % 2, 1, keepdims=False)
    return own, other, jnp.concatenate([mats, w1, w2]), jnp.pad(vec, ((0, 15), (0, 0)))


def plane_sum(mine, other):
    pair = (mine.astype(F32) + swap(other, 1).astype(F32)).astype(BF)
    parts = lax.all_to_all(pair, "dp", 0, 0, tiled=True, axis_index_groups=groups_xy())
    return jnp.sum(parts.astype(F32), axis=0).astype(BF)


def column_sum(part_c, part_f):
    rows = ROWS + 16
    blocks = jnp.stack([jnp.zeros((ROWS, D), BF), part_c[:ROWS], part_f[:ROWS], part_f[ROWS:]])
    extra = jnp.pad(part_c[ROWS : ROWS + 4].reshape(4, 1, D), ((0, 0), (0, 15), (0, 0)))
    stack = jnp.concatenate([blocks, extra], axis=1).reshape(4 * rows, D)
    return lax.psum_scatter(
        stack, "dp", scatter_dimension=0, tiled=True, axis_index_groups=groups_z()
    ).astype(F32)


def finish_blocks(mine, other, rest, index):
    z = index // 8
    part = plane_sum(mine, other)
    sent = [lax.ppermute(part, "dp", [(8 * k + p, p) for p in range(8)]) for k in (1, 2, 3)]
    own = part.astype(F32)
    for piece in sent:
        own = own + piece.astype(F32)
    chunk = jnp.where(z == 0, own[:ROWS], rest[:ROWS])
    flat = turn_w1(chunk, z == 2, False).reshape(ROWS * D)
    after = lax.ppermute(flat[:VEC_LEN], "dp", [(i + 1, i) for i in range(31)])
    pieces = jnp.concatenate(
        [
            rest[ROWS].reshape(4, LANES),
            own[ROWS : ROWS + 1, :LANES],
            jnp.full((3, LANES), jnp.sum(chunk * chunk)),
        ]
    )
    pieces = jnp.broadcast_to(pieces[None], (32, 8, LANES))
    pieces = lax.all_to_all(pieces, "dp", 0, 0, tiled=True)
    vec = pieces[:, :4].reshape(4, 8, D).transpose(1, 0, 2).reshape(32, D)
    late = jnp.pad(pieces[:8, 4].reshape(2, D), ((6, 9), (0, 0)))
    vec = (vec[:VEC_ROWS] + late).reshape(VEC_LEN)
    square = jnp.sum(pieces[:, 5, 0]) + jnp.sum(vec * vec)
    after = jnp.where(index == 31, vec, after)
    share = lax.dynamic_slice(jnp.concatenate([flat, after]), (272 * index,), (ROWS * D + 272,))
    return share, vec, square


def share_plain(pairs, index, share_len):
    def joined(mine, other):
        low = jnp.where(index % 2 == 0, mine, other).astype(F32)
        return jnp.stack([low, jnp.where(index % 2 == 0, other, mine).astype(F32)], axis=1)

    self_g, cross_g, ffn_g = (joined(*pair) for pair in pairs)
    dw1 = ffn_g[:, :, :ROWS].reshape(8, 4, 64, D).transpose(0, 2, 1, 3)
    vec = cross_g[:, :, ROWS : ROWS + 4].reshape(32, D)
    late = jnp.pad(self_g[:, :, ROWS, :LANES].reshape(2, D), ((6, 9), (0, 0)))
    vec = vec[:VEC_ROWS] + late
    parts = (self_g[:, :, :ROWS], cross_g[:, :, :ROWS], dw1, ffn_g[:, :, ROWS:], vec)
    flat = lax.psum(jnp.concatenate([g.reshape(-1) for g in parts]), "dp")
    share = lax.dynamic_slice(flat, (index * share_len,), (share_len,))
    return share, flat[-VEC_LEN:], jnp.sum(flat * flat)


def shards(count, targets, memory, target_ids, memory_ids, cotangent, params, first_moment, second_moment):
    index = lax.axis_index("dp")
    blocked = count == 32
    gather = gather_blocks if blocked else gather_plain
    own, other, weights, vec = gather(params, index)
    place = jnp.where(blocked, index % 8 // 2, 0)
    core = jnp.stack([index % 2, place]).astype(jnp.int32)
    lane = jnp.arange(LANES)[None, :] - MASK_LANE
    live = (lane >= 0) & (lane < 8)
    same_t = lane == target_ids[:, None]
    same_m = lane == memory_ids[:, None]
    qa = jnp.where(live & ~same_t, masked_value, 0.0).astype(BF)
    ka_self = jnp.where(same_t, 1.0, 0.0).astype(BF)
    ka_cross = jnp.where(same_m, 1.0, 0.0).astype(BF)
    memory_turn, targets_turn = memory.T, targets.T
    qa, ka_self, ka_cross, memory_turn, targets_turn, vec = lax.optimization_barrier(
        (qa, ka_self, ka_cross, memory_turn, targets_turn, vec)
    )
    qs, ks, vs, os, qal_s, n1, r1 = self_forward(
        core, own, other, targets, vec, qa, ka_self
    )
    qc, kc, vc, oc, qal_c, n2, r2 = cross_forward(
        weights, n1, memory, vec, qa, ka_cross
    )
    out, mine_f, other_f, dr2, vg_f = ffn(core, weights, n2, r2, cotangent, vec)
    mine_c, other_c, memory_grad, dr1 = cross_backward(
        core, weights, dr2, vec, qc, kc, vc, oc, qal_c, ka_cross, n1, r1, memory_turn, vg_f
    )
    if blocked:
        part_f = plane_sum(mine_f, other_f)
        part_f, mine_c, other_c, dr1 = lax.optimization_barrier((part_f, mine_c, other_c, dr1))
        part_c = plane_sum(mine_c, other_c)
    early = self_backward_start(weights, dr1, qs, ks, vs, os, qal_s, ka_self)
    if blocked:
        part_c, early = lax.optimization_barrier((part_c, early))
        rest = column_sum(part_c, part_f)
    mine_s, other_s, input_grad = self_backward_end(
        core, weights, dr1, qs, ks, vs, os, qal_s, ka_self, targets_turn, *early
    )
    if blocked:
        grad, vec_total, square = finish_blocks(mine_s, other_s, rest, index)
    else:
        pairs = ((mine_s, other_s), (mine_c, other_c), (mine_f, other_f))
        grad, vec_total, square = share_plain(pairs, index, params.shape[0])
    norm_value = jnp.sqrt(square)
    factor = jnp.minimum(1.0, clip_limit / (norm_value + 1e-06))
    clipped = grad * factor
    new_first = beta_one * first_moment + (1.0 - beta_one) * clipped
    new_second = beta_two * second_moment + (1.0 - beta_two) * clipped * clipped
    first_hat = new_first / (1.0 - beta_one**STEP)
    second_hat = new_second / (1.0 - beta_two**STEP)
    new_params = params - step_rate * (
        first_hat / (jnp.sqrt(second_hat) + adam_eps) + weight_decay * params
    )
    return (
        out,
        input_grad,
        memory_grad,
        norm_value,
        grad,
        vec_total,
        new_params,
        new_first,
        new_second,
        new_params.astype(BF),
    )


def solution(mesh):
    rows, flat = P("dp", None), P("dp")
    return jax.shard_map(
        functools.partial(shards, mesh.shape["dp"]),
        mesh=mesh,
        in_specs=(rows, rows, flat, flat, rows, flat, flat, flat),
        out_specs=(rows, rows, rows, P(), flat, P(), flat, flat, flat, flat),
        check_vma=False,
    )
```

profile of v0, /device:TPU:0, one launch (start us, length us, event | category | flops | bytes accessed | tf_op | source)
XLA Modules:
  0.0 324.2 jit_solution(5138203586375258740)
XLA Ops:
  8.8 7.4 %collective-permute-done = bf16[8704]{0:T(1024)(128)(2,1)S(1)} collective-permute-done((bf16[8704]{0:T(1024)(128)(2,1)S(1)}, bf16[8704]{0:T(1024)(128)(2,1)S(1)}, u32[]{:S(2)}, u32[]{:S(2)}) %collective-permute-start) | collective-permute-done | bytes 17440 | tf_op jit(solution)/shard_map/ppermute | solution.py:579
  17.9 3.1 collective-permute-start.1
  21.0 7.3 %collective-permute-done.1 = bf16[288,512]{1,0:T(8,128)(2,1)S(1)} collective-permute-done((bf16[288,512]{1,0:T(8,128)(2,1)S(1)}, bf16[288,512]{1,0:T(8,128)(2,1)S(1)}, u32[]{:S(2)}, u32[]{:S(2)}) %collective-permute-start.1) | collective-permute-done | bytes 294944 | tf_op jit(solution)/shard_map/ppermute | solution.py:557
  29.7 7.4 %collective-permute-done.2 = bf16[288,512]{1,0:T(8,128)(2,1)S(1)} collective-permute-done((bf16[288,512]{1,0:T(8,128)(2,1)S(1)}, bf16[288,512]{1,0:T(8,128)(2,1)S(1)}, u32[]{:S(2)}, u32[]{:S(2)}) %collective-permute-start.2) | collective-permute-done | bytes 294944 | tf_op jit(solution)/shard_map/ppermute | solution.py:559
  38.5 1.6 collective-permute-start.3
  40.1 3.9 %collective-permute-done.4 = bf16[288,512]{1,0:T(8,128)(2,1)S(1)} collective-permute-done((bf16[288,512]{1,0:T(8,128)(2,1)S(1)}, bf16[288,512]{1,0:T(8,128)(2,1)S(1)}, u32[]{:S(2)}, u32[]{:S(2)}) %collective-permute-start.4) | collective-permute-done | bytes 294944 | tf_op jit(solution)/shard_map/ppermute | solution.py:544
  44.0 2.4 collective-permute-start.5
  46.4 3.4 %collective-permute-done.3 = bf16[288,512]{1,0:T(8,128)(2,1)S(1)} collective-permute-done((bf16[288,512]{1,0:T(8,128)(2,1)S(1)}, bf16[288,512]{1,0:T(8,128)(2,1)S(1)}, u32[]{:S(2)}, u32[]{:S(2)}) %collective-permute-start.3) | collective-permute-done | bytes 294944 | tf_op jit(solution)/shard_map/ppermute | solution.py:544
  50.0 4.7 %collective-permute-done.5 = bf16[144,512]{1,0:T(8,128)(2,1)S(1)} collective-permute-done((bf16[144,512]{1,0:T(8,128)(2,1)S(1)}, bf16[144,512]{1,0:T(8,128)(2,1)S(1)}, u32[]{:S(2)}, u32[]{:S(2)}) %collective-permute-start.5) | collective-permute-done | bytes 147488 | tf_op jit(solution)/shard_map/ppermute | solution.py:544
  55.2 1.7 copy.65
  61.4 23.8 %shard_map.159 = (bf16[1024,512]{1,0:T(8,128)(2,1)}, bf16[1024,512]{1,0:T(8,128)(2,1)}, bf16[1024,512]{1,0:T(8,128)(2,1)}, bf16[1024,512]{1,0:T(8,128)(2,1)}, bf...) custom-call(s32[2]{0:T(128)} %pad_add_fusion.core_ref, bf16[4,288,512]{2,1,0:T(8,128)(2,1)} %bitcast.43, ...), custom_call_target="tpu_custom_call" | custom-call | flops 10737418240 | bytes 3997704 | tf_op jit(solution)/shard_map/pallas_call | solution.py:471
  85.2 13.9 %all-gather.2.cloned.1.call-done.all_ref = bf16[32,256,512]{2,1,0:T(8,128)(2,1)} async-done(((bf16[1,256,512]{2,1,0:T(8,128)(2,1)}), bf16[32,256,512]{2,1,0:T(8,128)(2,1)}) %all-gather.2.cloned.1.call-update) | async-done | bytes 8388624 | tf_op jit(solution)/shard_map/all_gather | solution.py:582
  99.2 28.1 %shard_map.160 = (bf16[1024,512]{1,0:T(8,128)(2,1)}, bf16[1024,512]{1,0:T(8,128)(2,1)}, bf16[1024,512]{1,0:T(8,128)(2,1)}, bf16[1024,512]{1,0:T(8,128)(2,1)}, bf...) custom-call(bf16[32,256,512]{2,1,0:T(8,128)(2,1)} %all-gather.2.cloned.1.call-done.all_ref, ...), custom_call_target="tpu_custom_call" | custom-call | flops 13421772800 | bytes 12124160 | tf_op jit(solution)/shard_map/pallas_call | solution.py:471
  127.3 25.9 %shard_map.161 = (bf16[1024,512]{1,0:T(8,128)(2,1)}, bf16[4,512,512]{2,1,0:T(8,128)(2,1)}, bf16[4,512,512]{2,1,0:T(8,128)(2,1)}, f32[1024,512]{1,0:T(8,128)}, f32[32,512]{1,0:T(8,128)}) custom-call(s32[2]{0:T(128)} %pad_add_fusion.core_ref, bf16[32,256,512]{2,1,0:T(8,128)(2,1)} %all-gather.2.cloned.1.call-done.all_ref, ...), custom_call_target="tpu_custom_call" | custom-call | flops 13958643712 | bytes 12124168 | tf_op jit(solution)/shard_map/pallas_call | solution.py:471
  153.6 4.1 %collective-permute-done.8 = bf16[4,512,512]{2,1,0:T(8,128)(2,1)S(1)} collective-permute-done((bf16[4,512,512]{2,1,0:T(8,128)(2,1)}, bf16[4,512,512]{2,1,0:T(8,128)(2,1)S(1)}, u32[]{:S(2)}, u32[]{:S(2)}) %collective-permute-start.8) | collective-permute-done | bytes 2097184 | tf_op jit(solution)/shard_map/ppermute | solution.py:544
  157.7 3.5 %add_convert_fusion = bf16[4,512,512]{2,1,0:T(8,128)(2,1)} fusion(bf16[4,512,512]{2,1,0:T(8,128)(2,1)S(1)} %collective-permute-done.8, bf16[4,512,512]{2,1,0:T(8,128)(2,1)} %get-tuple-element.65), kind=kLoop, calls=%fused_computation | loop fusion | flops 4194304 | bytes 6291456 | tf_op jit(solution)/shard_map/convert_element_type | solution.py:602
  161.2 3.8 %all-to-all-start = ((bf16[4,512,512]{2,1,0:T(8,128)(2,1)}), bf16[4,512,512]{2,1,0:T(8,128)(2,1)S(1)}, u32[]{:S(2)}, u32[]{:S(2)}) async-start(bf16[4,512,512]{2,1,0:T(8,128)(2,1)} %add_convert_fusion), calls=%async_computation | async-start | bytes 4194304 | tf_op jit(solution)/shard_map/all_to_all | solution.py:603
  164.9 39.7 %shard_map.162 = (bf16[4,272,512]{2,1,0:T(8,128)(2,1)}, bf16[4,272,512]{2,1,0:T(8,128)(2,1)}, bf16[1024,512]{1,0:T(8,128)(2,1)}, f32[1024,512]{1,0:T(8,128)}) custom-call(s32[2]{0:T(128)} %pad_add_fusion.core_ref, bf16[32,256,512]{2,1,0:T(8,128)(2,1)} %all-gather.2.cloned.1.call-done.all_ref, f32[1024,512]{1,0:T(8,128)} %get-tuple-element.67.dr2_ref, ...), custom_call_target="tpu_custom_call" | custom-call | flops 26843545600 | bytes 19005448 | tf_op jit(solution)/shard_map/pallas_call | solution.py:471
  205.7 2.6 collective-permute-done.9
  208.3 2.6 add_convert_fusion.2
  210.9 4.1 %all-to-all-start.1 = ((bf16[4,272,512]{2,1,0:T(8,128)(2,1)}), bf16[4,272,512]{2,1,0:T(8,128)(2,1)S(1)}, u32[]{:S(2)}, u32[]{:S(2)}) async-start(bf16[4,272,512]{2,1,0:T(8,128)(2,1)} %add_convert_fusion.2), calls=%async_computation.1 | async-start | bytes 2228224 | tf_op jit(solution)/shard_map/all_to_all | solution.py:603
  215.0 21.0 %shard_map.163 = (bf16[1024,512]{1,0:T(8,128)(2,1)}, bf16[1024,128]{1,0:T(8,128)(2,1)}, bf16[1024,512]{1,0:T(8,128)(2,1)}, bf16[1024,512]{1,0:T(8,128)(2,1)}, bf16[1024,512]{1,0:T(8,128)(2,1)}) custom-call(bf16[32,256,512]{2,1,0:T(8,128)(2,1)} %all-gather.2.cloned.1.call-done.all_ref, f32[1024,512]{1,0:T(8,128)} %get-tuple-element.79.dr1_ref, ...), custom_call_target="tpu_custom_call" | custom-call | flops 13421772800 | bytes 15204352 | tf_op jit(solution)/shard_map/pallas_call | solution.py:471
  236.3 14.8 %shard_map.164 = (bf16[4,272,512]{2,1,0:T(8,128)(2,1)}, bf16[4,272,512]{2,1,0:T(8,128)(2,1)}, bf16[1024,512]{1,0:T(8,128)(2,1)}) custom-call(s32[2]{0:T(128)} %pad_add_fusion.core_ref, bf16[32,256,512]{2,1,0:T(8,128)(2,1)} %all-gather.2.cloned.1.call-done.all_ref, f32[1024,512]{1,0:T(8,128)} %get-tuple-element.79.dr1_ref, ...), custom_call_target="tpu_custom_call" | custom-call | flops 1073741824 | bytes 20709384 | tf_op jit(solution)/shard_map/pallas_call | solution.py:471
  252.5 1.6 collective-permute-done.10
  254.5 19.3 %all_to_all.20 = bf16[4,272,512]{2,1,0:T(8,128)(2,1)S(1)} all-to-all(bf16[4,272,512]{2,1,0:T(8,128)(2,1)S(1)} %add_convert_fusion.1), channel_id=1, replica_groups={{0,2,4,6},{1,3,5,7},{8,10,12,14},{9,11,13,15},{16,18,20,22},{17,19,21,2..., dimensions={0} | all-to-all | bytes 2228224 | tf_op jit(solution)/shard_map/all_to_all | solution.py:603
  277.9 3.5 %reduce-scatter.2.cloned.1.call-done = bf16[272,512]{1,0:T(8,128)(2,1)} async-done(((bf16[1088,512]{1,0:T(8,128)(2,1)}), bf16[272,512]{1,0:T(8,128)(2,1)}) %reduce-scatter.2.cloned.1.call-update) | async-done | bytes 278544 | tf_op jit(solution)/shard_map/reduce_scatter | solution.py:612
  283.1 3.5 %collective-permute-done.13 = bf16[272,512]{1,0:T(8,128)(2,1)S(1)} collective-permute-done((bf16[272,512]{1,0:T(8,128)(2,1)S(1)}, bf16[272,512]{1,0:T(8,128)(2,1)S(1)}, u32[]{:S(2)}, u32[]{:S(2)}) %collective-permute-start.13) | collective-permute-done | bytes 278560 | tf_op jit(solution)/shard_map/ppermute | solution.py:620
  286.6 5.2 %collective-permute-done.12 = bf16[272,512]{1,0:T(8,128)(2,1)S(1)} collective-permute-done((bf16[272,512]{1,0:T(8,128)(2,1)S(1)}, bf16[272,512]{1,0:T(8,128)(2,1)S(1)}, u32[]{:S(2)}, u32[]{:S(2)}) %collective-permute-start.12) | collective-permute-done | bytes 278560 | tf_op jit(solution)/shard_map/ppermute | solution.py:620
  291.8 5.9 %collective-permute-done.11 = bf16[272,512]{1,0:T(8,128)(2,1)S(1)} collective-permute-done((bf16[272,512]{1,0:T(8,128)(2,1)S(1)}, bf16[272,512]{1,0:T(8,128)(2,1)S(1)}, u32[]{:S(2)}, u32[]{:S(2)}) %collective-permute-start.11) | collective-permute-done | bytes 278560 | tf_op jit(solution)/shard_map/ppermute | solution.py:620
  300.1 2.6 all-to-all-start.3
  305.0 6.0 %all-to-all-done.3 = f32[32,8,128]{2,1,0:T(8,128)S(1)} async-done(((f32[32,8,128]{2,1,0:T(8,128)}), f32[32,8,128]{2,1,0:T(8,128)S(1)}, u32[]{:S(2)}, u32[]{:S(2)}) %all-to-all-start.3) | async-done | bytes 131104 | tf_op jit(solution)/shard_map/all_to_all | solution.py:635
  313.8 2.1 fusion.11
  (102 shorter events, 26.4 us)
Async XLA Ops:
  7.2 92.0 %all-gather.2.cloned.1.call-start = ((), (), s32[]{:S(2)}) async-start(), calls=%async_computation.5 | async-start | bytes 8650752 | tf_op jit(solution)/shard_map/all_gather | solution.py:582
  8.4 7.8 %collective-permute-start = (bf16[8704]{0:T(1024)(128)(2,1)S(1)}, bf16[8704]{0:T(1024)(128)(2,1)S(1)}, u32[]{:S(2)}, u32[]{:S(2)}) collective-permute-start(bf16[8704]{0:T(1024)(128)(2,1)S(1)} %slice.78), channel_id=1, source_target_pairs={{0,1},{1,2},{2,3},{3,4},{4,5},{5,6},{6,7},{7,8},{8,9},{9,10},{10,1... | collective-permute-start | bytes 52232 | tf_op jit(solution)/shard_map/ppermute | solution.py:579
  17.9 10.4 %collective-permute-start.1 = (bf16[288,512]{1,0:T(8,128)(2,1)S(1)}, bf16[288,512]{1,0:T(8,128)(2,1)S(1)}, u32[]{:S(2)}, u32[]{:S(2)}) collective-permute-start(bf16[288,512]{1,0:T(8,128)(2,1)S(1)} %fusion.7), channel_id=1, source_target_pairs={{0,16},{1,17},{2,18},{3,19},{4,20},{5,21},{6,22},{7,23}} | collective-permute-start | bytes 884744 | tf_op jit(solution)/shard_map/ppermute | solution.py:557
  28.4 8.7 %collective-permute-start.2 = (bf16[288,512]{1,0:T(8,128)(2,1)S(1)}, bf16[288,512]{1,0:T(8,128)(2,1)S(1)}, u32[]{:S(2)}, u32[]{:S(2)}) collective-permute-start(bf16[288,512]{1,0:T(8,128)(2,1)S(1)} %broadcast_select_fusion), channel_id=1, source_target_pairs={{0,8},{1,9},{2,10},{3,11},{4,12},{5,13},{6,14},{7,15},{16,24},{17,... | collective-permute-start | bytes 884744 | tf_op jit(solution)/shard_map/ppermute | solution.py:559
  37.2 18.0 %copy-start.3 = (bf16[1024,512]{1,0:T(8,128)(2,1)S(1)}, bf16[1024,512]{1,0:T(8,128)(2,1)}, u32[]{:S(2)}) copy-start(bf16[1024,512]{1,0:T(8,128)(2,1)} %m_ref.1) | copy-start | bytes 3145732
  37.2 6.8 %collective-permute-start.4 = (bf16[288,512]{1,0:T(8,128)(2,1)S(1)}, bf16[288,512]{1,0:T(8,128)(2,1)S(1)}, u32[]{:S(2)}, u32[]{:S(2)}) collective-permute-start(bf16[288,512]{1,0:T(8,128)(2,1)S(1)} %get-tuple-element.114), channel_id=1, source_target_pairs={{0,4},{1,5},{2,6},{3,7},{4,0},{5,1},{6,2},{7,3},{8,12},{9,13},{10,... | collective-permute-start | bytes 884744 | tf_op jit(solution)/shard_map/ppermute | solution.py:544
  38.5 11.3 %collective-permute-start.3 = (bf16[288,512]{1,0:T(8,128)(2,1)S(1)}, bf16[288,512]{1,0:T(8,128)(2,1)S(1)}, u32[]{:S(2)}, u32[]{:S(2)}) collective-permute-start(bf16[288,512]{1,0:T(8,128)(2,1)S(1)} %get-tuple-element.114), channel_id=1, source_target_pairs={{0,2},{1,3},{2,0},{3,1},{4,6},{5,7},{6,4},{7,5},{8,10},{9,11},{10,... | collective-permute-start | bytes 884744 | tf_op jit(solution)/shard_map/ppermute | solution.py:544
  44.0 10.6 %collective-permute-start.5 = (bf16[144,512]{1,0:T(8,128)(2,1)S(1)}, bf16[144,512]{1,0:T(8,128)(2,1)S(1)}, u32[]{:S(2)}, u32[]{:S(2)}) collective-permute-start(bf16[144,512]{1,0:T(8,128)(2,1)S(1)} %slice.79), channel_id=1, source_target_pairs={{0,2},{1,3},{2,0},{3,1},{4,6},{5,7},{6,4},{7,5},{8,10},{9,11},{10,... | collective-permute-start | bytes 442376 | tf_op jit(solution)/shard_map/ppermute | solution.py:544
  49.8 5.2 %collective-permute-start.6 = (bf16[144,512]{1,0:T(8,128)(2,1)S(1)}, bf16[144,512]{1,0:T(8,128)(2,1)S(1)}, u32[]{:S(2)}, u32[]{:S(2)}) collective-permute-start(bf16[144,512]{1,0:T(8,128)(2,1)S(1)} %slice.80), channel_id=1, source_target_pairs={{0,4},{1,5},{2,6},{3,7},{4,0},{5,1},{6,2},{7,3},{8,12},{9,13},{10,... | collective-permute-start | bytes 442376 | tf_op jit(solution)/shard_map/ppermute | solution.py:544
  54.7 2.2 copy-start.2
  55.1 5.0 %copy-start.7 = (bf16[1152,512]{1,0:T(8,128)(2,1)}, bf16[1152,512]{1,0:T(8,128)(2,1)S(1)}, u32[]{:S(2)}) copy-start(bf16[1152,512]{1,0:T(8,128)(2,1)S(1)} %constant_dynamic-update-slice_fusion) | copy-start | bytes 3538948
  55.1 5.0 %collective-permute-start.7 = (bf16[4,288,512]{2,1,0:T(8,128)(2,1)S(1)}, bf16[4,288,512]{2,1,0:T(8,128)(2,1)}, u32[]{:S(2)}, u32[]{:S(2)}) collective-permute-start(bf16[4,288,512]{2,1,0:T(8,128)(2,1)S(1)} %bitcast.41), channel_id=1, source_target_pairs={{0,1},{1,0},{2,3},{3,2},{4,5},{5,4},{6,7},{7,6},{8,9},{9,8},{10,11... | collective-permute-start | bytes 3538952 | tf_op jit(solution)/shard_map/ppermute | solution.py:544
  56.9 2.0 copy-start.8
  56.9 2.0 copy-start.9
  153.2 4.4 %collective-permute-start.8 = (bf16[4,512,512]{2,1,0:T(8,128)(2,1)}, bf16[4,512,512]{2,1,0:T(8,128)(2,1)S(1)}, u32[]{:S(2)}, u32[]{:S(2)}) collective-permute-start(bf16[4,512,512]{2,1,0:T(8,128)(2,1)} %get-tuple-element.66), channel_id=1, source_target_pairs={{0,1},{1,0},{2,3},{3,2},{4,5},{5,4},{6,7},{7,6},{8,9},{9,8},{10,11... | collective-permute-start | bytes 6291464 | tf_op jit(solution)/shard_map/ppermute | solution.py:544
  161.2 43.5 %all-to-all-start = ((bf16[4,512,512]{2,1,0:T(8,128)(2,1)}), bf16[4,512,512]{2,1,0:T(8,128)(2,1)S(1)}, u32[]{:S(2)}, u32[]{:S(2)}) async-start(bf16[4,512,512]{2,1,0:T(8,128)(2,1)} %add_convert_fusion), calls=%async_computation | async-start | bytes 4194304 | tf_op jit(solution)/shard_map/all_to_all | solution.py:603
  205.3 3.0 collective-permute-start.9
  210.9 25.1 %all-to-all-start.1 = ((bf16[4,272,512]{2,1,0:T(8,128)(2,1)}), bf16[4,272,512]{2,1,0:T(8,128)(2,1)S(1)}, u32[]{:S(2)}, u32[]{:S(2)}) async-start(bf16[4,272,512]{2,1,0:T(8,128)(2,1)} %add_convert_fusion.2), calls=%async_computation.1 | async-start | bytes 2228224 | tf_op jit(solution)/shard_map/all_to_all | solution.py:603
  215.0 66.4 %reduce-scatter.2.cloned.1.call-start = ((), (), s32[]{:S(2)}) async-start(), calls=%async_computation.6 | async-start | bytes 1392640 | tf_op jit(solution)/shard_map/reduce_scatter | solution.py:612
  251.1 3.0 collective-permute-start.10
  251.2 2.9 copy-start.1
  274.0 12.6 %collective-permute-start.13 = (bf16[272,512]{1,0:T(8,128)(2,1)S(1)}, bf16[272,512]{1,0:T(8,128)(2,1)S(1)}, u32[]{:S(2)}, u32[]{:S(2)}) collective-permute-start(bf16[272,512]{1,0:T(8,128)(2,1)S(1)} %reduce_sum.65), channel_id=1, source_target_pairs={{24,0},{25,1},{26,2},{27,3},{28,4},{29,5},{30,6},{31,7}} | collective-permute-start | bytes 835592 | tf_op jit(solution)/shard_map/ppermute | solution.py:620
  275.3 16.5 %collective-permute-start.12 = (bf16[272,512]{1,0:T(8,128)(2,1)S(1)}, bf16[272,512]{1,0:T(8,128)(2,1)S(1)}, u32[]{:S(2)}, u32[]{:S(2)}) collective-permute-start(bf16[272,512]{1,0:T(8,128)(2,1)S(1)} %reduce_sum.65), channel_id=1, source_target_pairs={{16,0},{17,1},{18,2},{19,3},{20,4},{21,5},{22,6},{23,7}} | collective-permute-start | bytes 835592 | tf_op jit(solution)/shard_map/ppermute | solution.py:620
  276.6 21.1 %collective-permute-start.11 = (bf16[272,512]{1,0:T(8,128)(2,1)S(1)}, bf16[272,512]{1,0:T(8,128)(2,1)S(1)}, u32[]{:S(2)}, u32[]{:S(2)}) collective-permute-start(bf16[272,512]{1,0:T(8,128)(2,1)S(1)} %reduce_sum.65), channel_id=1, source_target_pairs={{8,0},{9,1},{10,2},{11,3},{12,4},{13,5},{14,6},{15,7}} | collective-permute-start | bytes 835592 | tf_op jit(solution)/shard_map/ppermute | solution.py:620
  300.1 10.8 %all-to-all-start.3 = ((f32[32,8,128]{2,1,0:T(8,128)}), f32[32,8,128]{2,1,0:T(8,128)S(1)}, u32[]{:S(2)}, u32[]{:S(2)}) async-start(f32[32,8,128]{2,1,0:T(8,128)} %broadcast_in_dim.30), calls=%async_computation.4 | async-start | bytes 262144 | tf_op jit(solution)/shard_map/all_to_all | solution.py:635
  303.3 10.5 %copy-start = (f32[131344]{0:T(1024)S(1)}, f32[131344]{0:T(1024)}, u32[]{:S(2)}) copy-start(f32[131344]{0:T(1024)} %param.13) | copy-start | bytes 1576132
  303.4 10.5 %copy-start.4 = (f32[131344]{0:T(1024)S(1)}, f32[131344]{0:T(1024)}, u32[]{:S(2)}) copy-start(f32[131344]{0:T(1024)} %param.14) | copy-start | bytes 1576132
  303.4 10.5 %copy-start.5 = (f32[131344]{0:T(1024)S(1)}, f32[131344]{0:T(1024)}, u32[]{:S(2)}) copy-start(f32[131344]{0:T(1024)} %param.15) | copy-start | bytes 1576132
  303.4 10.4 %collective-permute-start.14 = (f32[8704]{0:T(1024)S(1)}, f32[8704]{0:T(1024)S(1)}, u32[]{:S(2)}, u32[]{:S(2)}) collective-permute-start(f32[8704]{0:T(1024)S(1)} %slice.77), channel_id=1, source_target_pairs={{1,0},{2,1},{3,2},{4,3},{5,4},{6,5},{7,6},{8,7},{9,8},{10,9},{11,1... | collective-permute-start | bytes 104456 | tf_op jit(solution)/shard_map/ppermute | solution.py:626
  313.8 2.2 copy-start.6
Sparse Core Ops, SparseCore 0:
  17.7 81.4 all-gather.1
  252.7 28.6 reduce-scatter.1
where the time goes:
time: 327 us; the launch traced here: 324 us
  Pallas kernels  153 us (47%)
  waiting for transfers between devices  80.7 us (25%)
  starting transfers between devices  26.9 us (8%)
  other arithmetic  19.9 us (6%)
  blocking collectives  19.3 us (6%)
  between operations  17.4 us (5%)
  local copies, waits for them, and re-layouts  6.68 us (2%)
    pallas_call x6, Pallas kernels, call(): pl.pallas_call(kernel, out_shape=sds, in_specs=[pl.BlockSpec(memory_space...  153 us
    ppermute x8, waiting for transfers between devices, swap(): return lax.ppermute(x, 'dp', [(i, i ^ bit) for i in range(32)])  20.6 us
    all_to_all x1, blocking collectives, plane_sum(): lax.all_to_all(pair, 'dp', 0, 0, tiled=True, axis_index_groups=groups_xy())  19.3 us
    ppermute x3, waiting for transfers between devices, finish_blocks(): lax.ppermute(part, 'dp', [(8 * k + p, p) for p in range(8)])  14.6 us
    all_gather x1, waiting for transfers between devices, gather_blocks(): everything = lax.all_gather(chunk, 'dp', axis=0)  13.9 us
    all_to_all x2, starting transfers between devices, plane_sum(): lax.all_to_all(pair, 'dp', 0, 0, tiled=True, axis_index_groups=groups_xy())  7.92 us
    ppermute x1, waiting for transfers between devices, gather_first(): lax.ppermute(held, 'dp', [(z0 * 8 + p, z0 * 8 + 8 + p) for z0 in (0, 2) f...  7.4 us
    ppermute x1, waiting for transfers between devices, gather_blocks(): lax.ppermute(low[share - VEC_LEN:], 'dp', [(i, (i + 1) % 32) for i in ran...  7.36 us
  transfers between devices with their start and end apart: 20, of which 16 were waited for; matrix products, arithmetic and copies ran while one was open for 4% of the time, Pallas kernels for 26%

commit v1 on v0

v1 whole, which is shorter than its diff:
```python
import functools
import jax
import jax.numpy as jnp
from jax import lax
from jax.experimental import pallas as pl
from jax.experimental.pallas import tpu as pltpu
from jax.sharding import PartitionSpec as P

D = 512
FF = 2048
HEADS = 8
LEN = 1024
STEP = 10
ROWS = 256
BLOCKS = LEN // ROWS
LANES = 128
PAIRS = D // LANES
MASK_LANE = 32
EARLY_PAIRS = 3
FIRST_ROWS = ROWS + 32

eps_norm = 1e-05
beta_one = 0.9
beta_two = 0.999
adam_eps = 1e-08
step_rate = 0.05
weight_decay = 0.01
clip_limit = 1.0
masked_value = -1e30
log2_e = 1.4426950408889634
query_scale = 0.125 * log2_e
key_scale = 1.0 / log2_e

BF = jnp.bfloat16
F32 = jnp.float32
VMEM_BYTES = 60 * 1024 * 1024


def nn(a, b):
    return jnp.dot(a, b, preferred_element_type=F32)


def nt(a, b):
    return lax.dot_general(a, b, (((1,), (1,)), ((), ())), preferred_element_type=F32)


def tn(a, b):
    return lax.dot_general(a, b, (((0,), (0,)), ((), ())), preferred_element_type=F32)


def layer_norm(resid):
    center = resid - jnp.mean(resid, axis=1, keepdims=True)
    inv_std = lax.rsqrt(jnp.mean(center * center, axis=1, keepdims=True) + eps_norm)
    return center * inv_std, inv_std


def norm_back(grad, normed, inv_std, gain):
    scaled = grad * gain
    return inv_std * (
        scaled
        - jnp.mean(scaled, axis=1, keepdims=True)
        - normed * jnp.mean(scaled * normed, axis=1, keepdims=True)
    )


def half_row(parity):
    lane = lax.broadcasted_iota(jnp.int32, (1, LANES), 1)
    inside = (lane // 64) == parity
    return jnp.where(inside, 1.0, 0.0).astype(BF)


def lane_row(first, count):
    lane = lax.broadcasted_iota(jnp.int32, (1, LANES), 1)
    inside = (lane >= first) & (lane < first + count)
    return jnp.where(inside, 1.0, 0.0).astype(BF)


def causal_bias(transposed):
    row = lax.broadcasted_iota(jnp.int32, (ROWS, ROWS), 0)
    col = lax.broadcasted_iota(jnp.int32, (ROWS, ROWS), 1)
    ok = (row <= col) if transposed else (col <= row)
    return jnp.where(ok, 0.0, masked_value)


def attend_forward(q_ref, k_ref, v_ref, qa_ref, ka_ref, o_ref, qal_ref, kt_ref, kat_ref, causal):
    size, depth = (ROWS, 2) if causal else (2 * ROWS, 1)
    lane = lax.broadcasted_iota(jnp.int32, (size, LANES), 1)
    low = lane < 64
    bias = causal_bias(False) if causal else None
    kt_ref[...] = k_ref[...].T
    kat_ref[...] = ka_ref[...].T

    def score(block, head):
        rows = pl.ds(block * size, size)
        lanes = pl.ds(head // 2 * LANES, LANES)
        keys = (block + 1) * size if causal else LEN
        q_cat = jnp.concatenate([q_ref[rows, lanes] * half_row(head % 2), qa_ref[rows, :]], axis=1)
        k_cat = jnp.concatenate([kt_ref[lanes, :keys], kat_ref[:, :keys]], axis=0)
        scores = nn(q_cat, k_cat)
        if causal:
            diag = scores[:, keys - size :] + bias
            scores = jnp.concatenate([scores[:, : keys - size], diag], axis=1) if block else diag
        return scores

    def finish(head, scores, lse_parts):
        half = half_row(head % 2)
        top = jnp.max(scores, axis=1, keepdims=True)
        probs = jnp.exp2(scores - top).astype(BF)
        values = v_ref[: scores.shape[1], pl.ds(head // 2 * LANES, LANES)]
        mixed = nn(probs, values * half + (1.0 - half).astype(BF))
        turned = pltpu.roll(mixed, 64, 1)
        lse = -(top + jnp.log2(turned if head % 2 == 0 else mixed))
        first = lse.astype(BF).astype(F32)
        rest = lse - first
        second = rest.astype(BF).astype(F32)
        for place, part in enumerate((first, second, rest - second)):
            lse_parts = jnp.where(lane == head * 3 + place, part, lse_parts)
        return mixed / turned, lse_parts

    for block in range(LEN // size):
        rows = pl.ds(block * size, size)
        waiting, outs = [], []
        lse_parts = jnp.zeros((size, LANES), F32)
        for step in range(HEADS + depth):
            if step < HEADS:
                waiting.append(score(block, step))
            if step >= depth:
                head = step - depth
                out, lse_parts = finish(head, waiting.pop(0), lse_parts)
                outs.append(out)
                if head % 2:
                    lanes = pl.ds(head // 2 * LANES, LANES)
                    o_ref[rows, lanes] = jnp.where(low, outs[-2], outs[-1]).astype(BF)
        qal_ref[rows, :] = (qa_ref[rows, :].astype(F32) + lse_parts).astype(BF)


def attend_backward(
    q_ref, k_ref, v_ref, do_ref, qal_ref, del_ref, ka_ref, dq_ref, dk_ref, dv_ref, p_ref, s_ref, kt_ref, dqt_ref,
    causal, span=(0, PAIRS),
):
    bias = causal_bias(True) if causal else None
    kt_ref[...] = k_ref[...].T

    def score(head, block):
        lanes = pl.ds(head // 2 * LANES, LANES)
        half = half_row(head % 2)
        rows = pl.ds(block * ROWS, ROWS)
        keys = (block + 1) * ROWS if causal else LEN
        marks = ka_ref[:keys, :] + lane_row(head * 3, 3)
        k_cat = jnp.concatenate([k_ref[:keys, lanes] * half, marks], axis=1)
        ones = jnp.broadcast_to(lane_row(head * 2, 2), (keys, LANES))
        v_cat = jnp.concatenate([v_ref[:keys, lanes] * half, ones], axis=1)
        q_cat = jnp.concatenate([q_ref[rows, lanes], qal_ref[rows, :]], axis=1)
        do_cat = jnp.concatenate([do_ref[rows, lanes], del_ref[rows, :]], axis=1)
        return nt(k_cat, q_cat), nt(v_cat, do_cat)

    def finish(head, block, scores, grads):
        rows = pl.ds(block * ROWS, ROWS)
        keys = scores.shape[0]
        if causal:
            diag = scores[keys - ROWS :] + bias
            scores = jnp.concatenate([scores[: keys - ROWS], diag], axis=0) if block else diag
        probs = jnp.exp2(scores)
        p_ref[head % 2, :keys, rows] = probs.astype(BF)
        inner = (probs * grads).astype(BF)
        s_ref[head % 2, :keys, rows] = inner
        own = pl.ds(head * 64, 64)
        dqt_ref[own, rows] = nn(kt_ref[own, :keys], inner)

    def pair_end(pair):
        lanes = pl.ds(pair * LANES, LANES)
        for kb in range(BLOCKS):
            rows = pl.ds(kb * ROWS, ROWS)
            first = kb * ROWS if causal else 0
            tail = pl.ds(first, LEN - first)
            do_pair = do_ref[tail, lanes]
            q_pair = q_ref[tail, lanes]
            dv = nn(p_ref[0, rows, tail], do_pair * half_row(0))
            dv = dv + nn(p_ref[1, rows, tail], do_pair * half_row(1))
            dv_ref[rows, lanes] = dv.astype(BF)
            dk = nn(s_ref[0, rows, tail], q_pair * half_row(0))
            dk = dk + nn(s_ref[1, rows, tail], q_pair * half_row(1))
            dk_ref[rows, lanes] = (dk * key_scale).astype(BF)

    steps = [(h, b) for h in range(2 * span[0], 2 * span[1]) for b in range(BLOCKS)]
    waiting = score(*steps[0])
    for place, (head, block) in enumerate(steps):
        current = waiting
        if place + 1 < len(steps):
            waiting = score(*steps[place + 1])
        finish(head, block, *current)
        if head % 2 and block == BLOCKS - 1:
            pair_end(head // 2)
    cols = pl.ds(span[0] * LANES, (span[1] - span[0]) * LANES)
    for block in range(BLOCKS):
        rows = pl.ds(block * ROWS, ROWS)
        dq_ref[rows, cols] = (dqt_ref[cols, rows] * 0.125).T.astype(BF)


def mix_gradient(g_ref, w_out, o_ref, do_ref, del_ref):
    lane = lax.broadcasted_iota(jnp.int32, (ROWS, LANES), 1)
    even = lane % 2 == 0
    col = lax.broadcasted_iota(jnp.int32, (D, LANES), 0) // 64
    pick = jnp.where(lax.broadcasted_iota(jnp.int32, (D, LANES), 1) // 2 == col, -1.0, 0.0).astype(BF)
    for qb in range(BLOCKS):
        rows = pl.ds(qb * ROWS, ROWS)
        do = nt(g_ref[rows, :], w_out).astype(BF)
        do_ref[rows, :] = do
        prod = do.astype(F32) * o_ref[rows, :].astype(F32)
        high = prod.astype(BF)
        inner = nn(high, pick) + nn((prod - high.astype(F32)).astype(BF), pick)
        first = inner.astype(BF).astype(F32)
        del_ref[rows, :] = jnp.where(even, first, inner - first).astype(BF)


def vec_row(vec_ref, index):
    return vec_ref[index : index + 1, :]


def fetch(core_ref, parts, w_ref, sems, rows=ROWS, first=0):
    core, chip = core_ref[0], core_ref[1]
    near, far = chip ^ (1 + core), chip ^ (2 - core)
    own, other = core, 1 - core
    moves = (
        (0, 0, chip, own),
        (1, 0, chip, other),
        (2, 0, near, own),
        (2, rows, near, other),
        (3, 0, far, other),
        (3, rows, far, own),
        (4, 0, chip ^ 3, own),
        (5, 0, chip ^ 3, other),
    )
    copies = []
    for i, (part, start, place, half) in enumerate(moves):
        source = parts[part].at[pl.ds(start + first, ROWS)]
        copies.append(pltpu.make_async_copy(source, w_ref.at[2 * place + half], sems.at[i]))
    for copy in copies:
        copy.start()
    return copies


def wait_all(copies):
    for copy in copies:
        copy.wait()


def square(w_ref, matrix):
    return w_ref[2 * matrix : 2 * matrix + 2].reshape(D, D)


def put_square(mine_ref, other_ref, core, matrix, turned_ref, grad, place=0):
    for ref, half in ((mine_ref, core), (other_ref, 1 - core)):
        rows = turned_ref[pl.ds(pl.multiple_of(half * ROWS, ROWS), ROWS), :]
        ref[matrix ^ place, :ROWS, :] = nn(rows, grad).astype(BF)


def put_square_tn(mine_ref, other_ref, core, matrix, left_ref, grad, place=0):
    for ref, half in ((mine_ref, core), (other_ref, 1 - core)):
        cols = left_ref[:, pl.ds(pl.multiple_of(half * ROWS, ROWS), ROWS)]
        ref[matrix ^ place, :ROWS, :] = tn(cols, grad).astype(BF)


def self_forward_kernel(
    core_ref, parts, x_ref, vec_ref, qa_ref, ka_ref,
    q_ref, k_ref, v_ref, o_ref, qal_ref, n_ref, r_ref,
    w_ref, kt_ref, kat_ref, sems,
):
    copies = fetch(core_ref, parts, w_ref, sems, FIRST_ROWS)
    wait_all(copies)
    for qb in range(BLOCKS):
        rows = pl.ds(qb * ROWS, ROWS)
        x = x_ref[rows, :]
        q_ref[rows, :] = ((nn(x, square(w_ref, 0)) + vec_row(vec_ref, 6)) * query_scale).astype(BF)
        k_ref[rows, :] = nn(x, square(w_ref, 1)).astype(BF)
        v_ref[rows, :] = (nn(x, square(w_ref, 2)) + vec_row(vec_ref, 7)).astype(BF)
    attend_forward(q_ref, k_ref, v_ref, qa_ref, ka_ref, o_ref, qal_ref, kt_ref, kat_ref, True)
    for qb in range(BLOCKS):
        rows = pl.ds(qb * ROWS, ROWS)
        resid = x_ref[rows, :].astype(F32) + nn(o_ref[rows, :], square(w_ref, 3)) + vec_row(vec_ref, 8)
        normed, inv_std = layer_norm(resid)
        n_ref[rows, :] = normed
        r_ref[rows, :] = jnp.broadcast_to(inv_std, (ROWS, LANES))


def cross_forward_kernel(
    core_ref, parts, n1_ref, m_ref, vec_ref, qa_ref, ka_ref,
    q_ref, k_ref, v_ref, o_ref, qal_ref, n_ref, r_ref,
    w_ref, kt_ref, kat_ref, sems,
):
    wait_all(fetch(core_ref, parts, w_ref, sems))
    for qb in range(BLOCKS):
        rows = pl.ds(qb * ROWS, ROWS)
        h = (n1_ref[rows, :] * vec_row(vec_ref, 0) + vec_row(vec_ref, 1)).astype(BF)
        m = m_ref[rows, :]
        q_ref[rows, :] = ((nn(h, square(w_ref, 0)) + vec_row(vec_ref, 9)) * query_scale).astype(BF)
        k_ref[rows, :] = nn(m, square(w_ref, 1)).astype(BF)
        v_ref[rows, :] = (nn(m, square(w_ref, 2)) + vec_row(vec_ref, 10)).astype(BF)
    attend_forward(q_ref, k_ref, v_ref, qa_ref, ka_ref, o_ref, qal_ref, kt_ref, kat_ref, False)
    for qb in range(BLOCKS):
        rows = pl.ds(qb * ROWS, ROWS)
        h = n1_ref[rows, :] * vec_row(vec_ref, 0) + vec_row(vec_ref, 1)
        resid = h + nn(o_ref[rows, :], square(w_ref, 3)) + vec_row(vec_ref, 11)
        normed, inv_std = layer_norm(resid)
        n_ref[rows, :] = normed
        r_ref[rows, :] = jnp.broadcast_to(inv_std, (ROWS, LANES))


def col_sum(x):
    return jnp.sum(x.astype(F32), axis=0, keepdims=True)


def ffn_kernel(
    core_ref, parts, n2_ref, r2_ref, cot_ref, vec_ref,
    out_ref, mine_ref, other_ref, dr_ref, vg_ref,
    w1_ref, w2_ref, u_ref, da_ref, h_ref, dz_ref, f_ref, ht_ref, sems1, sems2,
):
    copies = fetch(core_ref, parts, w1_ref, sems1, 2 * ROWS)
    copies += fetch(core_ref, parts, w2_ref, sems2, 2 * ROWS, ROWS)
    wait_all(copies)

    def w1_block(j):
        return w1_ref[:, 64 * j : 64 * j + 64].reshape(D, D)

    def w2_block(j):
        return square(w2_ref, j)

    vg_ref[...] = jnp.zeros_like(vg_ref)

    def one_tile(tile, carry):
        rows = pl.ds(pl.multiple_of(tile * ROWS, ROWS), ROWS)
        n2 = n2_ref[rows, :]
        h2 = n2 * vec_row(vec_ref, 2) + vec_row(vec_ref, 3)
        h2_low = h2.astype(BF)
        h_ref[rows, :] = h2_low
        resid = h2 + vec_row(vec_ref, 16)
        for j in range(4):
            a = nn(h2_low, w1_block(j)) + vec_row(vec_ref, 12 + j)
            s = 0.5 * jnp.tanh(0.5 * a) + 0.5
            u = (a * s).astype(BF)
            u_ref[rows, j * D : (j + 1) * D] = u
            f_ref[:, j * D : (j + 1) * D] = s * (1.0 + a * (1.0 - s))
            resid = resid + nn(u, w2_block(j))
        n3, inv3 = layer_norm(resid)
        gain3 = vec_row(vec_ref, 4)
        out_ref[rows, :] = (n3 * gain3 + vec_row(vec_ref, 5)).astype(BF)
        cot = cot_ref[rows, :].astype(F32)
        dr3 = norm_back(cot, n3, inv3, gain3)
        dz = dr3.astype(BF)
        dz_ref[rows, :] = dz
        vg_ref[4:5, :] += col_sum(cot * n3)
        vg_ref[5:6, :] += col_sum(cot)
        vg_ref[16:17, :] += col_sum(dz)
        dh = dr3
        for j in range(4):
            da = (nt(dz, w2_block(j)) * f_ref[:, j * D : (j + 1) * D]).astype(BF)
            da_ref[rows, j * D : (j + 1) * D] = da
            vg_ref[12 + j : 13 + j, :] += col_sum(da)
            dh = dh + nt(da, w1_block(j))
        vg_ref[2:3, :] += col_sum(dh * n2)
        vg_ref[3:4, :] += col_sum(dh)
        dr2 = norm_back(dh, n2, r2_ref[rows, 0:1], vec_row(vec_ref, 2))
        dr_ref[rows, :] = dr2
        vg_ref[11:12, :] += col_sum(dr2.astype(BF))
        return carry

    lax.fori_loop(0, BLOCKS, one_tile, 0)
    core = core_ref[0]
    ht_ref[...] = jnp.swapaxes(h_ref[...].T.reshape(4, 2, 64, LEN), 0, 1).reshape(2, ROWS, LEN)
    for j in range(4):
        da = da_ref[:, j * D : (j + 1) * D]
        dz = dz_ref[...]
        for ref, half in ((mine_ref, core), (other_ref, 1 - core)):
            dw1 = nn(ht_ref[half], da).astype(BF)
            ref[:, 64 * j : 64 * j + 64, :] = dw1.reshape(4, 64, D)
            cols = pl.ds(pl.multiple_of(j * D + half * ROWS, ROWS), ROWS)
            ref[j, ROWS:, :] = tn(u_ref[:, cols], dz).astype(BF)


def cross_backward_kernel(
    core_ref, parts, dr2_ref, vec_ref, q_ref, k_ref, v_ref, o_ref, qal_ref, ka_ref, n1_ref, r1_ref, mt_ref, vf_ref,
    mine_ref, other_ref, dr1_ref, dk_ref, dv_ref,
    g_ref, do_ref, del_ref, dq_ref, p_ref, s_ref, h_ref, w_ref, vg_ref, kt_ref, dqt_ref, sems,
):
    core = core_ref[0]
    copies = fetch(core_ref, parts, w_ref, sems)
    for qb in range(BLOCKS):
        rows = pl.ds(qb * ROWS, ROWS)
        g_ref[rows, :] = dr2_ref[rows, :].astype(BF)
        h_ref[rows, :] = (n1_ref[rows, :] * vec_row(vec_ref, 0) + vec_row(vec_ref, 1)).astype(BF)
    wait_all(copies)
    mix_gradient(g_ref, square(w_ref, 3), o_ref, do_ref, del_ref)
    put_square_tn(mine_ref, other_ref, core, 3, o_ref, g_ref[...])
    attend_backward(
        q_ref, k_ref, v_ref, do_ref, qal_ref, del_ref, ka_ref, dq_ref, dk_ref, dv_ref, p_ref, s_ref, kt_ref, dqt_ref, False
    )
    put_square_tn(mine_ref, other_ref, core, 0, h_ref, dq_ref[...])
    put_square(mine_ref, other_ref, core, 1, mt_ref, dk_ref[...])
    put_square(mine_ref, other_ref, core, 2, mt_ref, dv_ref[...])
    vg_ref[...] = vf_ref[...]
    for qb in range(BLOCKS):
        rows = pl.ds(qb * ROWS, ROWS)
        dq = dq_ref[rows, :]
        dv = dv_ref[rows, :]
        vg_ref[9:10, :] += col_sum(dq)
        vg_ref[10:11, :] += col_sum(dv)
        dh = dr2_ref[rows, :] + nt(dq, square(w_ref, 0))
        n1 = n1_ref[rows, :]
        vg_ref[0:1, :] += col_sum(dh * n1)
        vg_ref[1:2, :] += col_sum(dh)
        dr1 = norm_back(dh, n1, r1_ref[rows, 0:1], vec_row(vec_ref, 0))
        dr1_ref[rows, :] = dr1
        vg_ref[8:9, :] += col_sum(dr1.astype(BF))
    blank = jnp.zeros((12, D), F32)
    for ref, half in ((mine_ref, core), (other_ref, 1 - core)):
        for xy in range(4):
            low, high = vg_ref[8 * xy : 8 * xy + 4, :], vg_ref[8 * xy + 4 : 8 * xy + 8, :]
            rows = jnp.where(half == 0, low, high)
            ref[xy, ROWS:, :] = jnp.concatenate([rows, blank], axis=0).astype(BF)


def self_backward_start_kernel(
    core_ref, parts, dr1_ref, q_ref, k_ref, v_ref, o_ref, qal_ref, ka_ref,
    do_ref, del_ref, dq_ref, dk_ref, dv_ref,
    g_ref, p_ref, s_ref, w_ref, kt_ref, dqt_ref, sems,
):
    copies = fetch(core_ref, parts, w_ref, sems, FIRST_ROWS)
    for qb in range(BLOCKS):
        rows = pl.ds(qb * ROWS, ROWS)
        g_ref[rows, :] = dr1_ref[rows, :].astype(BF)
    wait_all(copies)
    mix_gradient(g_ref, square(w_ref, 3), o_ref, do_ref, del_ref)
    attend_backward(
        q_ref, k_ref, v_ref, do_ref, qal_ref, del_ref, ka_ref, dq_ref, dk_ref, dv_ref, p_ref, s_ref, kt_ref, dqt_ref, True,
        (0, EARLY_PAIRS),
    )


def self_backward_end_kernel(
    core_ref, dr1_ref, q_ref, k_ref, v_ref, o_ref, qal_ref, ka_ref, xt_ref,
    do_ref, del_ref, dqe_ref, dke_ref, dve_ref,
    mine_ref, other_ref, dq_ref, dk_ref, dv_ref,
    g_ref, p_ref, s_ref, late_ref, kt_ref, dqt_ref,
):
    core, chip = core_ref[0], core_ref[1]
    for qb in range(BLOCKS):
        rows = pl.ds(qb * ROWS, ROWS)
        g_ref[rows, :] = dr1_ref[rows, :].astype(BF)
    early = EARLY_PAIRS * LANES
    for ref, source in ((dq_ref, dqe_ref), (dk_ref, dke_ref), (dv_ref, dve_ref)):
        ref[:, :early] = source[:, :early]
    attend_backward(
        q_ref, k_ref, v_ref, do_ref, qal_ref, del_ref, ka_ref, dq_ref, dk_ref, dv_ref, p_ref, s_ref, kt_ref, dqt_ref, True,
        (EARLY_PAIRS, PAIRS),
    )
    put_square_tn(mine_ref, other_ref, core, 3, o_ref, g_ref[...], chip)
    put_square(mine_ref, other_ref, core, 0, xt_ref, dq_ref[...], chip)
    put_square(mine_ref, other_ref, core, 1, xt_ref, dk_ref[...], chip)
    put_square(mine_ref, other_ref, core, 2, xt_ref, dv_ref[...], chip)
    late_ref[...] = jnp.zeros_like(late_ref)
    for qb in range(BLOCKS):
        rows = pl.ds(qb * ROWS, ROWS)
        dq = dq_ref[rows, :]
        dv = dv_ref[rows, :]
        late_ref[0:1, :] += col_sum(dq)
        late_ref[1:2, :] += col_sum(dv)
    for ref, half in ((mine_ref, core), (other_ref, 1 - core)):
        for xy in range(4):
            place = pl.multiple_of((2 * (xy % 2) + half) * LANES, LANES)
            piece = late_ref[xy // 2 : xy // 2 + 1, pl.ds(place, LANES)]
            after = lax.broadcasted_iota(jnp.int32, (16, LANES), 0) >= 4
            ref[xy ^ chip, ROWS:, :] = jnp.zeros((16, D), BF)
            ref[xy ^ chip, ROWS:, :LANES] = jnp.where(after, piece, 0.0).astype(BF)


def input_grads_kernel(
    core_ref, parts, parts2, dr1_ref, dqs_ref, dks_ref, dvs_ref, dkc_ref, dvc_ref,
    ig_ref, mg_ref,
    w_ref, wc_ref, sems1, sems2,
):
    copies = fetch(core_ref, parts, w_ref, sems1, FIRST_ROWS)
    copies += fetch(core_ref, parts2, wc_ref, sems2)
    wait_all(copies)
    for qb in range(BLOCKS):
        rows = pl.ds(qb * ROWS, ROWS)
        total = dr1_ref[rows, :] + nt(dqs_ref[rows, :], square(w_ref, 0))
        total = total + nt(dks_ref[rows, :], square(w_ref, 1))
        ig_ref[rows, :] = (total + nt(dvs_ref[rows, :], square(w_ref, 2))).astype(BF)
        total = nt(dkc_ref[rows, :], square(wc_ref, 1))
        mg_ref[rows, :] = (total + nt(dvc_ref[rows, :], square(wc_ref, 2))).astype(BF)


def call(kernel, outs, scratch, flops, core, parts, args, sems=1):
    sds = [jax.ShapeDtypeStruct(shape, dtype) for shape, dtype in outs]
    arrays = [block for group in parts for block in group]
    moved = sum(a.size * a.dtype.itemsize for a in arrays + list(args))
    spaces = [pltpu.SMEM] + [pl.ANY] * len(arrays) + [pltpu.VMEM] * len(args)
    memory = [pltpu.VMEM(shape, dtype) for shape, dtype in scratch]
    memory += [pltpu.SemaphoreType.DMA((8,))] * sems

    def body(core_ref, *refs):
        groups = [refs[6 * i : 6 * i + 6] for i in range(len(parts))]
        kernel(core_ref, *groups, *refs[6 * len(parts) :])

    return pl.pallas_call(
        body,
        out_shape=sds,
        in_specs=[pl.BlockSpec(memory_space=space) for space in spaces],
        scratch_shapes=memory,
        compiler_params=pltpu.CompilerParams(vmem_limit_bytes=VMEM_BYTES),
        cost_estimate=pl.CostEstimate(flops=flops, bytes_accessed=moved, transcendentals=0),
    )(core, *arrays, *args)


TOK = (LEN, D)
STAT = (LEN, LANES)
OCT = (8, ROWS, D)
unit = 2 * LEN * D * D
FORWARD_OUTS = [(TOK, BF)] * 4 + [(STAT, BF), (TOK, F32), (STAT, F32)]
HALVES = ((4, ROWS + 16, D), BF)
TOKB = (TOK, BF)
PROBS = ((2, LEN, LEN), BF)
TURN = ((D, LEN), BF)
TURN32 = ((D, LEN), F32)
FORWARD_SCRATCH = [(OCT, BF), TURN, ((LANES, LEN), BF)]


def self_forward(core, w, *args):
    return call(self_forward_kernel, FORWARD_OUTS, FORWARD_SCRATCH, 20 * unit, core, [w], args)


def cross_forward(core, w, *args):
    return call(cross_forward_kernel, FORWARD_OUTS, FORWARD_SCRATCH, 25 * unit, core, [w], args)


def ffn(core, w, *args):
    outs = [TOKB, ((4, 2 * ROWS, D), BF), ((4, 2 * ROWS, D), BF), (TOK, F32), ((32, D), F32)]
    scratch = [(OCT, BF), (OCT, BF), ((LEN, FF), BF), ((LEN, FF), BF), TOKB, TOKB]
    scratch += [((ROWS, FF), F32), ((2, ROWS, LEN), BF)]
    return call(ffn_kernel, outs, scratch, 26 * unit, core, [w], args, 2)


def cross_backward(core, w, *args):
    outs = [HALVES, HALVES, (TOK, F32), TOKB, TOKB]
    scratch = [TOKB, TOKB, (STAT, BF), TOKB, PROBS, PROBS, TOKB, (OCT, BF), ((32, D), F32), TURN, TURN32]
    return call(cross_backward_kernel, outs, scratch, 50 * unit, core, [w], args)


def self_backward_start(core, w, *args):
    outs = [TOKB, (STAT, BF), TOKB, TOKB, TOKB]
    scratch = [TOKB, PROBS, PROBS, (OCT, BF), TURN, TURN32]
    return call(self_backward_start_kernel, outs, scratch, 25 * unit, core, [w], args)


def self_backward_end(core, *args):
    outs = [HALVES, HALVES, TOKB, TOKB, TOKB]
    scratch = [TOKB, PROBS, PROBS, ((8, D), F32), TURN, TURN32]
    return call(self_backward_end_kernel, outs, scratch, 12 * unit, core, [], args, 0)


def input_grads(core, ws, wc, *args):
    scratch = [(OCT, BF), (OCT, BF)]
    return call(input_grads_kernel, [TOKB, TOKB], scratch, 6 * unit, core, [ws, wc], args, 2)


SQUARES = 8 * D * D
VEC_ROWS = 17
VEC_LEN = VEC_ROWS * D


def groups_xy():
    return [[z * 8 + c * 2 + core for c in range(4)] for z in range(4) for core in range(2)]


def groups_z():
    return [[z * 8 + p for z in range(4)] for p in range(8)]


def swap(x, bit):
    return lax.ppermute(x, "dp", [(i, i ^ bit) for i in range(32)])


def turn_w1(chunk, here, out_first):
    if out_first:
        alt = chunk.reshape(64, 4, D).transpose(1, 0, 2).reshape(ROWS, D)
    else:
        alt = chunk.reshape(4, 64, D).transpose(1, 0, 2).reshape(ROWS, D)
    return jnp.where(here, alt, chunk)


def along_z(x, moves):
    return lax.ppermute(x, "dp", [(8 * a + p, 8 * b + p) for a, b in moves for p in range(8)])


def gather_blocks(params, index, others):
    low = params.astype(BF)
    share = low.shape[0]
    shift = share - ROWS * D
    z = index // 8
    prev = lax.ppermute(low[share - VEC_LEN :], "dp", [(i, (i + 1) % 32) for i in range(32)])
    flat = lax.dynamic_slice(jnp.concatenate([prev, low]), (VEC_LEN - shift * index,), (ROWS * D,))
    chunk = turn_w1(flat.reshape(ROWS, D), z == 2, True)
    vec = jnp.pad(prev.reshape(VEC_ROWS, D), ((0, 15), (0, 0)))
    mine = jnp.concatenate([chunk, vec])
    first = along_z(mine, ((0, 2), (1, 0), (2, 3), (3, 1)))
    first, others = lax.optimization_barrier((first, others))
    second = along_z(jnp.where(z == 2, first, mine), ((0, 1), (1, 2), (2, 3)))
    third = along_z(jnp.where(z == 1, first, mine)[:ROWS], ((3, 2), (2, 1), (1, 0)))
    second, third = lax.optimization_barrier((second, third))
    block0 = jnp.where(z == 0, mine, jnp.where(z == 2, first, second))
    fourth = along_z(jnp.where(z == 1, third, second[:ROWS]), ((1, 0), (2, 3)))
    pair0, near0 = to_sides(block0)
    near0, fourth = lax.optimization_barrier((near0, fourth))
    first, second = first[:ROWS], second[:ROWS]

    def pick(*blocks):
        return jnp.where(z < 2, jnp.where(z == 0, *blocks[:2]), jnp.where(z == 2, *blocks[2:]))

    block1 = pick(first, chunk, second, fourth)
    block2 = pick(fourth, third, chunk, first)
    block3 = pick(third, first, third, chunk)
    across0 = to_corners(near0)
    pair1, near1 = to_sides(block1)
    across0, near1 = lax.optimization_barrier((across0, near1))
    part0 = finish_block(pair0, near0, across0)
    across1 = to_corners(near1)
    pair2, near2 = to_sides(jnp.concatenate([block2, block3]))
    core, chip = index % 2, index % 8 // 2
    rows = [part0[0], part0[1], part0[2], part0[2], part0[3], part0[3], part0[4], part0[5]]
    starts = [ROWS, ROWS, ROWS, 2 * ROWS + 32, ROWS, 2 * ROWS + 32, ROWS, ROWS]
    rows = jnp.stack([lax.slice_in_dim(a, s, s + 32) for a, s in zip(rows, starts)])
    place = jnp.where(chip == 0, core, jnp.where(chip == 3, 6 + core, jnp.where(chip == 1 + core, 2 + core, 5 - core)))
    source = lax.dynamic_index_in_dim(rows, place, 0, keepdims=False)
    return part0, (pair1, near1, across1), (pair2, near2), source.astype(F32), others


def sides(first, second):
    return [(i, i ^ (first if i % 2 == 0 else second)) for i in range(32)]


def to_sides(block):
    pair = (block, swap(block, 1))
    return pair, lax.ppermute(jnp.concatenate(pair), "dp", sides(2, 4))


def to_corners(near):
    return lax.ppermute(near[: near.shape[0] // 2], "dp", sides(4, 2))


def finish_block(pair, near, across):
    return [*pair, near, swap(near, 1), across, swap(across, 1)]


def gather_plain(params, index, others):
    flat = lax.all_gather(params.astype(BF), "dp", axis=0, tiled=True)
    end = SQUARES + D * FF
    w1 = flat[SQUARES:end].reshape(8, 64, 4, D).transpose(0, 2, 1, 3).reshape(8, ROWS, D)
    w2 = flat[end : end + D * FF].reshape(8, ROWS, D)
    vec = flat[end + D * FF :].reshape(VEC_ROWS, D).astype(F32)
    mats = flat[:SQUARES].reshape(2, 4, 2, ROWS, D)

    core = index % 2

    def parts(pairs, rows):
        pairs = jnp.pad(pairs, ((0, 0), (0, 0), (0, rows - pairs.shape[2]), (0, 0)))
        own = lax.dynamic_index_in_dim(pairs, core, 1, keepdims=False)
        other = lax.dynamic_index_in_dim(pairs, 1 - core, 1, keepdims=False)
        one, two = jnp.concatenate([own, other], axis=1), jnp.concatenate([other, own], axis=1)
        near = lax.dynamic_index_in_dim(one, 1 + core, 0, keepdims=False)
        far = lax.dynamic_index_in_dim(two, 2 - core, 0, keepdims=False)
        return [own[0], other[0], near, far, own[3], other[3]]

    vec = jnp.pad(vec, ((0, 15), (0, 0)))
    wide = jnp.concatenate([w1.reshape(4, 2, ROWS, D), w2.reshape(4, 2, ROWS, D)], axis=2)
    return parts(mats[0], FIRST_ROWS), parts(mats[1], ROWS), parts(wide, 2 * ROWS), vec, others


def plane_sum(mine, other):
    pair = (mine.astype(F32) + swap(other, 1).astype(F32)).astype(BF)
    parts = lax.all_to_all(pair, "dp", 0, 0, tiled=True, axis_index_groups=groups_xy())
    return jnp.sum(parts.astype(F32), axis=0).astype(BF)


def add(a, b):
    return (a.astype(F32) + b.astype(F32)).astype(BF)


def first_round(part_c, part_f, z):
    extra = part_c[ROWS:]
    part_1 = jnp.concatenate([part_f[:ROWS], extra])
    part_2 = jnp.concatenate([part_f[ROWS:], extra])
    return part_c, part_1, part_2, along_z(jnp.where(z == 0, part_1, part_c), ((0, 1), (3, 2)))


def finish_blocks(mine, other, blocks, index):
    z = index // 8
    got = swap(other, 1)
    pairs = [(mine[j].astype(F32) + got[j].astype(F32)).astype(BF) for j in range(4)]
    part_c, part_1, part_2, early = blocks
    part = pairs[0].astype(F32) + swap(pairs[1], 2).astype(F32) + swap(pairs[2], 4).astype(F32)
    part = part + swap(pairs[3], 6).astype(F32)
    part = (part + jnp.pad(part_c[ROWS:].astype(F32), ((ROWS, 0), (0, 0)))).astype(BF)
    left = jnp.where(z == 2, add(part_c, early), part)
    right = jnp.where(z == 1, add(part_1, early), part_2)
    got_left = along_z(left, ((1, 0), (2, 1), (3, 2)))
    got_right = along_z(right, ((0, 1), (1, 2), (2, 3)))
    last = jnp.where(z < 2, jnp.where(z == 0, part_c, add(part_2, got_right)), jnp.where(z == 2, add(part, got_left), part_1))
    got = along_z(last, ((2, 0), (0, 1), (3, 2), (1, 3)))
    own = jnp.where(z < 2, jnp.where(z == 0, part, part_c), jnp.where(z == 2, part_1, part_2)).astype(F32)
    own = own + jnp.where(z < 2, got_left, got_right).astype(F32) + got.astype(F32)
    chunk = own[:ROWS]
    flat = turn_w1(chunk, z == 2, False).reshape(ROWS * D)
    after = lax.ppermute(flat[:VEC_LEN], "dp", [(i + 1, i) for i in range(31)])
    pieces = jnp.concatenate(
        [
            lax.dynamic_index_in_dim(own[ROWS : ROWS + 4], z, 0, keepdims=False).reshape(4, LANES),
            own[ROWS + 4 : ROWS + 5, :LANES],
            jnp.full((3, LANES), jnp.sum(chunk * chunk)),
        ]
    )
    pieces = jnp.broadcast_to(pieces[None], (32, 8, LANES))
    pieces = lax.all_to_all(pieces, "dp", 0, 0, tiled=True)
    vec = pieces[:, :4].reshape(4, 8, D).transpose(1, 0, 2).reshape(32, D)
    late = jnp.pad(pieces[:8, 4].reshape(2, D), ((6, 9), (0, 0)))
    vec = (vec[:VEC_ROWS] + late).reshape(VEC_LEN)
    square = jnp.sum(pieces[:, 5, 0]) + jnp.sum(vec * vec)
    after = jnp.where(index == 31, vec, after)
    share = lax.dynamic_slice(jnp.concatenate([flat, after]), (272 * index,), (ROWS * D + 272,))
    return share, vec, square


def share_plain(pairs, index, share_len):
    def joined(mine, other):
        low = jnp.where(index % 2 == 0, mine, other).astype(F32)
        return jnp.stack([low, jnp.where(index % 2 == 0, other, mine).astype(F32)], axis=1)

    self_g, cross_g, ffn_g = (joined(*pair) for pair in pairs)
    dw1 = ffn_g[:, :, :ROWS].reshape(8, 4, 64, D).transpose(0, 2, 1, 3)
    vec = cross_g[:, :, ROWS : ROWS + 4].reshape(32, D)
    late = jnp.pad(self_g[:, :, ROWS + 4, :LANES].reshape(2, D), ((6, 9), (0, 0)))
    vec = vec[:VEC_ROWS] + late
    parts = (self_g[:, :, :ROWS], cross_g[:, :, :ROWS], dw1, ffn_g[:, :, ROWS:], vec)
    flat = lax.psum(jnp.concatenate([g.reshape(-1) for g in parts]), "dp")
    share = lax.dynamic_slice(flat, (index * share_len,), (share_len,))
    return share, flat[-VEC_LEN:], jnp.sum(flat * flat)


def shards(count, targets, memory, target_ids, memory_ids, cotangent, params, first_moment, second_moment):
    index = lax.axis_index("dp")
    blocked = count == 32
    place = jnp.where(blocked, index % 8 // 2, 0)
    core = jnp.stack([index % 2, place]).astype(jnp.int32)
    lane = jnp.arange(LANES)[None, :] - MASK_LANE
    live = (lane >= 0) & (lane < 8)
    same_t = lane == target_ids[:, None]
    same_m = lane == memory_ids[:, None]
    others = (
        jnp.where(live & ~same_t, masked_value, 0.0).astype(BF),
        jnp.where(same_t, 1.0, 0.0).astype(BF),
        jnp.where(same_m, 1.0, 0.0).astype(BF),
        memory.T,
        targets.T,
        core,
    )
    gather = gather_blocks if blocked else gather_plain
    ws, wc, wide, vec, others = gather(params, index, others)
    qa, ka_self, ka_cross, memory_turn, targets_turn, core = others
    qs, ks, vs, os, qal_s, n1, r1 = self_forward(core, ws, targets, vec, qa, ka_self)
    if blocked:
        wc, wide, n1 = lax.optimization_barrier((wc, wide, n1))
        wc = finish_block(*wc)
        across = to_corners(wide[1])
    qc, kc, vc, oc, qal_c, n2, r2 = cross_forward(core, wc, n1, memory, vec, qa, ka_cross)
    if blocked:
        across, n2 = lax.optimization_barrier((across, n2))
        wide = finish_block(*wide, across)
    out, mine_f, other_f, dr2, vg_f = ffn(core, wide, n2, r2, cotangent, vec)
    mine_c, other_c, dr1, dkc, dvc = cross_backward(
        core, wc, dr2, vec, qc, kc, vc, oc, qal_c, ka_cross, n1, r1, memory_turn, vg_f
    )
    if blocked:
        part_f = plane_sum(mine_f, other_f)
        part_f, mine_c, other_c, dr1 = lax.optimization_barrier((part_f, mine_c, other_c, dr1))
        part_c = plane_sum(mine_c, other_c)
    early = self_backward_start(core, ws, dr1, qs, ks, vs, os, qal_s, ka_self)
    if blocked:
        part_c, early = lax.optimization_barrier((part_c, early))
        blocks = first_round(part_c, part_f, index // 8)
    mine_s, other_s, dqs, dks, dvs = self_backward_end(
        core, dr1, qs, ks, vs, os, qal_s, ka_self, targets_turn, *early
    )
    input_grad, memory_grad = input_grads(core, ws, wc, dr1, dqs, dks, dvs, dkc, dvc)
    if blocked:
        blocks, mine_s, other_s = lax.optimization_barrier((blocks, mine_s, other_s))
        grad, vec_total, square = finish_blocks(mine_s, other_s, blocks, index)
    else:
        pairs = ((mine_s, other_s), (mine_c, other_c), (mine_f, other_f))
        grad, vec_total, square = share_plain(pairs, index, params.shape[0])
    norm_value = jnp.sqrt(square)
    factor = jnp.minimum(1.0, clip_limit / (norm_value + 1e-06))
    clipped = grad * factor
    new_first = beta_one * first_moment + (1.0 - beta_one) * clipped
    new_second = beta_two * second_moment + (1.0 - beta_two) * clipped * clipped
    first_hat = new_first / (1.0 - beta_one**STEP)
    second_hat = new_second / (1.0 - beta_two**STEP)
    new_params = params - step_rate * (
        first_hat / (jnp.sqrt(second_hat) + adam_eps) + weight_decay * params
    )
    return (
        out,
        input_grad,
        memory_grad,
        norm_value,
        grad,
        vec_total,
        new_params,
        new_first,
        new_second,
        new_params.astype(BF),
    )


def solution(mesh):
    rows, flat = P("dp", None), P("dp")
    return jax.shard_map(
        functools.partial(shards, mesh.shape["dp"]),
        mesh=mesh,
        in_specs=(rows, rows, flat, flat, rows, flat, flat, flat),
        out_specs=(rows, rows, rows, P(), flat, P(), flat, flat, flat, flat),
        check_vma=False,
    )
```

time: 327 us -> 288 us (0.88)
  blocking collectives: 19.3 us -> 0 us
  starting transfers between devices: 26.9 us -> 44.5 us
  Pallas kernels: 153 us -> 136 us
  between operations: 17.4 us -> 4.13 us
  waiting for transfers between devices: 80.7 us -> 69.1 us
    all_to_all x1 -> x0, blocking collectives: 19.3 us -> none  [plane_sum(): lax.all_to_all(pair, 'dp', 0, 0, tiled=True, axis_index_groups=groups_xy())]
    pallas_call x6 -> x7, Pallas kernels: 153 us -> 136 us  [call(): pl.pallas_call(body, out_shape=sds, in_specs=[pl.BlockSpec(memory_space=s...]
    ppermute x5 -> x14, starting transfers between devices: 8.31 us -> 23.7 us  [the longest x8 17.8 us: along_z(): lax.ppermute(x, 'dp', [(8 * a + p, 8 * b + p) for a, b in moves for p in...]
    all_gather x1 -> x0, waiting for transfers between devices: 13.9 us -> none  [gather_blocks(): everything = lax.all_gather(chunk, 'dp', axis=0)]
    ppermute x8 -> x15, waiting for transfers between devices: 20.6 us -> 26.9 us  [swap(): return lax.ppermute(x, 'dp', [(i, i ^ bit) for i in range(32)])]
    all_to_all x1, waiting for transfers between devices: 5.96 us -> 0.01 us  [finish_blocks(): pieces = lax.all_to_all(pieces, 'dp', 0, 0, tiled=True)]
    ppermute x5 -> x14, waiting for transfers between devices: 29.3 us -> 34.8 us  [the longest x8 26.1 us: along_z(): lax.ppermute(x, 'dp', [(8 * a + p, 8 * b + p) for a, b in moves for p in...]
    reduce_scatter x1 -> x0, waiting for transfers between devices: 3.46 us -> none  [column_sum(): lax.psum_scatter(stack, 'dp', scatter_dimension=0, tiled=True, axis_index...]
  transfers between devices with their start and end apart: 20 -> 34, of which waited for: 16 -> 18; matrix products, arithmetic and copies ran while one was open for 4% -> 3% of each run, Pallas kernels for 26% -> 39%
where the time goes in v1:
time: 288 us; the launch traced here: 283 us
  Pallas kernels  136 us (47%)
  waiting for transfers between devices  69.1 us (24%)
  starting transfers between devices  44.5 us (15%)
  other arithmetic  19 us (7%)
  local copies, waits for them, and re-layouts  9.93 us (3%)
  between operations  4.13 us (1%)
    pallas_call x7, Pallas kernels, call(): pl.pallas_call(body, out_shape=sds, in_specs=[pl.BlockSpec(memory_space=s...  136 us
    ppermute x15, waiting for transfers between devices, swap(): return lax.ppermute(x, 'dp', [(i, i ^ bit) for i in range(32)])  26.9 us
    ppermute x8, waiting for transfers between devices, along_z(): lax.ppermute(x, 'dp', [(8 * a + p, 8 * b + p) for a, b in moves for p in...  26.1 us
    ppermute x8, starting transfers between devices, along_z(): lax.ppermute(x, 'dp', [(8 * a + p, 8 * b + p) for a, b in moves for p in...  17.8 us
    all_to_all x2, starting transfers between devices, plane_sum(): lax.all_to_all(pair, 'dp', 0, 0, tiled=True, axis_index_groups=groups_xy())  7.92 us
    ppermute x15, starting transfers between devices, swap(): return lax.ppermute(x, 'dp', [(i, i ^ bit) for i in range(32)])  7.8 us
    ppermute x1, waiting for transfers between devices, gather_blocks(): lax.ppermute(low[share - VEC_LEN:], 'dp', [(i, (i + 1) % 32) for i in ran...  7.35 us
    unnamed x62, local copies, waits for them, and re-layouts  6.24 us
  transfers between devices with their start and end apart: 34, of which 18 were waited for; matrix products, arithmetic and copies ran while one was open for 3% of the time, Pallas kernels for 39%

profile of v1, /device:TPU:0, one launch (start us, length us, event | category | flops | bytes accessed | tf_op | source)
XLA Modules:
  0.0 282.8 jit_solution(16500587257071085400)
XLA Ops:
  2.4 7.4 %collective-permute-done = bf16[8704]{0:T(1024)(128)(2,1)S(1)} collective-permute-done((bf16[8704]{0:T(1024)(128)(2,1)S(1)}, bf16[8704]{0:T(1024)(128)(2,1)S(1)}, u32[]{:S(2)}, u32[]{:S(2)}) %collective-permute-start) | collective-permute-done | bytes 17440 | tf_op jit(solution)/shard_map/ppermute | solution.py:600
  17.3 3.0 %collective-permute-start.2 = (bf16[288,512]{1,0:T(8,128)(2,1)S(1)}, bf16[288,512]{1,0:T(8,128)(2,1)S(1)}, u32[]{:S(2)}, u32[]{:S(2)}) collective-permute-start(bf16[288,512]{1,0:T(8,128)(2,1)S(1)} %broadcast_select_fusion), channel_id=1, source_target_pairs={{0,8},{1,9},{2,10},{3,11},{4,12},{5,13},{6,14},{7,15},{8,16},{9,17... | collective-permute-start | bytes 884744 | tf_op jit(solution)/shard_map/ppermute | solution.py:592
  21.7 7.0 %collective-permute-done.3 = bf16[256,512]{1,0:T(8,128)(2,1)S(1)} collective-permute-done((bf16[256,512]{1,0:T(8,128)(2,1)S(1)}, bf16[256,512]{1,0:T(8,128)(2,1)S(1)}, u32[]{:S(2)}, u32[]{:S(2)}) %collective-permute-start.3) | collective-permute-done | bytes 262176 | tf_op jit(solution)/shard_map/ppermute | solution.py:592
  28.9 1.5 collective-permute-done.4.refs_1_
  33.3 8.5 %collective-permute-done.6 = bf16[256,512]{1,0:T(8,128)(2,1)S(1)} collective-permute-done((bf16[256,512]{1,0:T(8,128)(2,1)S(1)}, bf16[256,512]{1,0:T(8,128)(2,1)S(1)}, u32[]{:S(2)}, u32[]{:S(2)}) %collective-permute-start.6) | collective-permute-done | bytes 262176 | tf_op jit(solution)/shard_map/ppermute | solution.py:592
  45.9 6.0 %collective-permute-done.8.refs_4_ = bf16[288,512]{1,0:T(8,128)(2,1)S(1)} collective-permute-done((bf16[288,512]{1,0:T(8,128)(2,1)S(1)}, bf16[288,512]{1,0:T(8,128)(2,1)S(1)}, u32[]{:S(2)}, u32[]{:S(2)}) %collective-permute-start.8) | collective-permute-done | bytes 294944 | tf_op jit(solution)/shard_map/ppermute | solution.py:647
  51.9 2.7 collective-permute-done.9.refs_2_.refs_8_
  57.9 15.7 %shard_map.159 = (bf16[1024,512]{1,0:T(8,128)(2,1)}, bf16[1024,512]{1,0:T(8,128)(2,1)}, bf16[1024,512]{1,0:T(8,128)(2,1)}, bf16[1024,512]{1,0:T(8,128)(2,1)}, bf...) custom-call(s32[2]{0:T(128)} %pad_add_fusion.core_ref, bf16[288,512]{1,0:T(8,128)(2,1)} %copy-done.1, ...), custom_call_target="tpu_custom_call" | custom-call | flops 10737418240 | bytes 3997696 | tf_op jit(solution)/shard_map/pallas_call | solution.py:505
  78.1 19.6 %shard_map.160 = (bf16[1024,512]{1,0:T(8,128)(2,1)}, bf16[1024,512]{1,0:T(8,128)(2,1)}, bf16[1024,512]{1,0:T(8,128)(2,1)}, bf16[1024,512]{1,0:T(8,128)(2,1)}, bf...) custom-call(s32[2]{0:T(128)} %pad_add_fusion.core_ref, bf16[256,512]{1,0:T(8,128)(2,1)} %copy-done.4, ...), custom_call_target="tpu_custom_call" | custom-call | flops 13421772800 | bytes 5832704 | tf_op jit(solution)/shard_map/pallas_call | solution.py:505
  101.0 26.0 %shard_map.161 = (bf16[1024,512]{1,0:T(8,128)(2,1)}, bf16[4,512,512]{2,1,0:T(8,128)(2,1)}, bf16[4,512,512]{2,1,0:T(8,128)(2,1)}, f32[1024,512]{1,0:T(8,128)}, f32[32,512]{1,0:T(8,128)}) custom-call(s32[2]{0:T(128)} %pad_add_fusion.core_ref, bf16[512,512]{1,0:T(8,128)(2,1)} %copy-done.7, bf16[512,512]{1,0:T(8,128)(2,1)} %copy-done.8, ...), custom_call_target="tpu_custom_call" | custom-call | flops 13958643712 | bytes 7929856 | tf_op jit(solution)/shard_map/pallas_call | solution.py:505
  127.5 4.0 %collective-permute-done.20 = bf16[4,512,512]{2,1,0:T(8,128)(2,1)S(1)} collective-permute-done((bf16[4,512,512]{2,1,0:T(8,128)(2,1)}, bf16[4,512,512]{2,1,0:T(8,128)(2,1)S(1)}, u32[]{:S(2)}, u32[]{:S(2)}) %collective-permute-start.20) | collective-permute-done | bytes 2097184 | tf_op jit(solution)/shard_map/ppermute | solution.py:580
  131.5 3.6 %add_convert_fusion = bf16[4,512,512]{2,1,0:T(8,128)(2,1)} fusion(bf16[4,512,512]{2,1,0:T(8,128)(2,1)S(1)} %collective-permute-done.20, bf16[4,512,512]{2,1,0:T(8,128)(2,1)} %get-tuple-element.110), kind=kLoop, calls=%fused_computation | loop fusion | flops 4194304 | bytes 6291456 | tf_op jit(solution)/shard_map/convert_element_type | solution.py:679
  135.0 3.8 %all-to-all-start = ((bf16[4,512,512]{2,1,0:T(8,128)(2,1)}), bf16[4,512,512]{2,1,0:T(8,128)(2,1)S(1)}, u32[]{:S(2)}, u32[]{:S(2)}) async-start(bf16[4,512,512]{2,1,0:T(8,128)(2,1)} %add_convert_fusion), calls=%async_computation | async-start | bytes 4194304 | tf_op jit(solution)/shard_map/all_to_all | solution.py:680
  138.8 34.4 %shard_map.162 = (bf16[4,272,512]{2,1,0:T(8,128)(2,1)}, bf16[4,272,512]{2,1,0:T(8,128)(2,1)}, f32[1024,512]{1,0:T(8,128)}, bf16[1024,512]{1,0:T(8,128)(2,1)}, bf16[1024,512]{1,0:T(8,128)(2,1)}) custom-call(s32[2]{0:T(128)} %pad_add_fusion.core_ref, bf16[256,512]{1,0:T(8,128)(2,1)} %copy-done.4, bf16[256,512]{1,0:T(8,128)(2,1)} %copy-done.10, ...), custom_call_target="tpu_custom_call" | custom-call | flops 26843545600 | bytes 12713984 | tf_op jit(solution)/shard_map/pallas_call | solution.py:505
  174.4 2.6 collective-permute-done.21
  177.0 2.6 add_convert_fusion.1
  179.5 4.1 %all-to-all-start.1 = ((bf16[4,272,512]{2,1,0:T(8,128)(2,1)}), bf16[4,272,512]{2,1,0:T(8,128)(2,1)S(1)}, u32[]{:S(2)}, u32[]{:S(2)}) async-start(bf16[4,272,512]{2,1,0:T(8,128)(2,1)} %add_convert_fusion.1), calls=%async_computation.1 | async-start | bytes 2228224 | tf_op jit(solution)/shard_map/all_to_all | solution.py:680
  183.7 18.6 %shard_map.163 = (bf16[1024,512]{1,0:T(8,128)(2,1)}, bf16[1024,128]{1,0:T(8,128)(2,1)}, bf16[1024,512]{1,0:T(8,128)(2,1)}, bf16[1024,512]{1,0:T(8,128)(2,1)}, bf16[1024,512]{1,0:T(8,128)(2,1)}) custom-call(s32[2]{0:T(128)} %pad_add_fusion.core_ref, bf16[288,512]{1,0:T(8,128)(2,1)} %copy-done.1, bf16[288,512]{1,0:T(8,128)(2,1)} %copy-done.9, ...), custom_call_target="tpu_custom_call" | custom-call | flops 13421772800 | bytes 9175040 | tf_op jit(solution)/shard_map/pallas_call | solution.py:505
  202.7 2.3 collective-permute-start.22
  205.0 12.5 %shard_map.164 = (bf16[4,272,512]{2,1,0:T(8,128)(2,1)}, bf16[4,272,512]{2,1,0:T(8,128)(2,1)}, bf16[1024,512]{1,0:T(8,128)(2,1)}, bf16[1024,512]{1,0:T(8,128)(2,1)}, bf16[1024,512]{1,0:T(8,128)(2,1)}) custom-call(s32[2]{0:T(128)} %pad_add_fusion.core_ref, f32[1024,512]{1,0:T(8,128)} %get-tuple-element.124.refs_6_.refs_0_.refs_12_, ...), custom_call_target="tpu_custom_call" | custom-call | flops 6442450944 | bytes 12320768 | tf_op jit(solution)/shard_map/pallas_call | solution.py:505
  217.6 3.0 %collective-permute-done.23 = bf16[4,272,512]{2,1,0:T(8,128)(2,1)S(1)} collective-permute-done((bf16[4,272,512]{2,1,0:T(8,128)(2,1)}, bf16[4,272,512]{2,1,0:T(8,128)(2,1)S(1)}, u32[]{:S(2)}, u32[]{:S(2)}) %collective-permute-start.23) | collective-permute-done | bytes 1114144 | tf_op jit(solution)/shard_map/ppermute | solution.py:580
  222.0 2.1 collective-permute-start.24
  225.6 5.9 %collective-permute-done.24 = bf16[272,512]{1,0:T(8,128)(2,1)S(1)} collective-permute-done((bf16[272,512]{1,0:T(8,128)(2,1)S(1)}, bf16[272,512]{1,0:T(8,128)(2,1)S(1)}, u32[]{:S(2)}, u32[]{:S(2)}) %collective-permute-start.24) | collective-permute-done | bytes 278560 | tf_op jit(solution)/shard_map/ppermute | solution.py:580
  231.5 6.8 %collective-permute-done.26 = bf16[272,512]{1,0:T(8,128)(2,1)S(1)} collective-permute-done((bf16[272,512]{1,0:T(8,128)(2,1)S(1)}, bf16[272,512]{1,0:T(8,128)(2,1)S(1)}, u32[]{:S(2)}, u32[]{:S(2)}) %collective-permute-start.26) | collective-permute-done | bytes 278560 | tf_op jit(solution)/shard_map/ppermute | solution.py:580
  242.2 4.6 %collective-permute-start.28 = (bf16[272,512]{1,0:T(8,128)(2,1)S(1)}, bf16[272,512]{1,0:T(8,128)(2,1)S(1)}, u32[]{:S(2)}, u32[]{:S(2)}) collective-permute-start(bf16[272,512]{1,0:T(8,128)(2,1)S(1)} %get-tuple-element.179), channel_id=1, source_target_pairs={{0,8},{1,9},{2,10},{3,11},{4,12},{5,13},{6,14},{7,15},{8,16},{9,17... | collective-permute-start | bytes 835592 | tf_op jit(solution)/shard_map/ppermute | solution.py:592
  246.8 2.6 collective-permute-done.27
  249.4 2.1 collective-permute-done.28
  251.7 2.5 collective-permute-start.29
  254.2 5.0 %collective-permute-done.29 = bf16[272,512]{1,0:T(8,128)(2,1)S(1)} collective-permute-done((bf16[272,512]{1,0:T(8,128)(2,1)S(1)}, bf16[272,512]{1,0:T(8,128)(2,1)S(1)}, u32[]{:S(2)}, u32[]{:S(2)}) %collective-permute-start.29) | collective-permute-done | bytes 278560 | tf_op jit(solution)/shard_map/ppermute | solution.py:592
  262.3 3.2 %all-to-all-start.2 = ((f32[32,8,128]{2,1,0:T(8,128)}), f32[32,8,128]{2,1,0:T(8,128)S(1)}, u32[]{:S(2)}, u32[]{:S(2)}) async-start(f32[32,8,128]{2,1,0:T(8,128)} %broadcast_in_dim.30), calls=%async_computation.2 | async-start | bytes 262144 | tf_op jit(solution)/shard_map/all_to_all | solution.py:722
  265.5 9.4 %shard_map.165 = (bf16[1024,512]{1,0:T(8,128)(2,1)}, bf16[1024,512]{1,0:T(8,128)(2,1)}) custom-call(s32[2]{0:T(128)} %pad_add_fusion.core_ref, bf16[288,512]{1,0:T(8,128)(2,1)} %copy-done.1, bf16[288,512]{1,0:T(8,128)(2,1)} %copy-done.9, bf16[576,512]{1,0:T(8,128)(2,1)} %copy-done.11, bf16[576,512]{1,0:T(8,128)(2,1)} %copy-done.15, ...), custom_call_target="tpu_custom_call" | custom-call | flops 3221225472 | bytes 11796480 | tf_op jit(solution)/shard_map/pallas_call | solution.py:505
  279.4 2.1 fusion.27
  (168 shorter events, 43.8 us)
Async XLA Ops:
  1.9 7.8 %collective-permute-start = (bf16[8704]{0:T(1024)(128)(2,1)S(1)}, bf16[8704]{0:T(1024)(128)(2,1)S(1)}, u32[]{:S(2)}, u32[]{:S(2)}) collective-permute-start(bf16[8704]{0:T(1024)(128)(2,1)S(1)} %slice.145), channel_id=1, source_target_pairs={{0,1},{1,2},{2,3},{3,4},{4,5},{5,6},{6,7},{7,8},{8,9},{9,10},{10,1... | collective-permute-start | bytes 52232 | tf_op jit(solution)/shard_map/ppermute | solution.py:600
  10.5 6.8 %collective-permute-start.1 = (bf16[288,512]{1,0:T(8,128)(2,1)S(1)}, bf16[288,512]{1,0:T(8,128)(2,1)S(1)}, u32[]{:S(2)}, u32[]{:S(2)}) collective-permute-start(bf16[288,512]{1,0:T(8,128)(2,1)S(1)} %fusion.11), channel_id=1, source_target_pairs={{0,16},{1,17},{2,18},{3,19},{4,20},{5,21},{6,22},{7,23},{8,0},{9,1... | collective-permute-start | bytes 884744 | tf_op jit(solution)/shard_map/ppermute | solution.py:592
  17.3 11.3 %collective-permute-start.2 = (bf16[288,512]{1,0:T(8,128)(2,1)S(1)}, bf16[288,512]{1,0:T(8,128)(2,1)S(1)}, u32[]{:S(2)}, u32[]{:S(2)}) collective-permute-start(bf16[288,512]{1,0:T(8,128)(2,1)S(1)} %broadcast_select_fusion), channel_id=1, source_target_pairs={{0,8},{1,9},{2,10},{3,11},{4,12},{5,13},{6,14},{7,15},{8,16},{9,17... | collective-permute-start | bytes 884744 | tf_op jit(solution)/shard_map/ppermute | solution.py:592
  20.4 8.3 %collective-permute-start.3 = (bf16[256,512]{1,0:T(8,128)(2,1)S(1)}, bf16[256,512]{1,0:T(8,128)(2,1)S(1)}, u32[]{:S(2)}, u32[]{:S(2)}) collective-permute-start(bf16[256,512]{1,0:T(8,128)(2,1)S(1)} %slice_select_fusion), channel_id=1, source_target_pairs={{24,16},{25,17},{26,18},{27,19},{28,20},{29,21},{30,22},{31,23},{1... | collective-permute-start | bytes 786440 | tf_op jit(solution)/shard_map/ppermute | solution.py:592
  30.5 11.3 %collective-permute-start.5 = (bf16[576,512]{1,0:T(8,128)(2,1)S(1)}, bf16[576,512]{1,0:T(8,128)(2,1)S(1)}, u32[]{:S(2)}, u32[]{:S(2)}) collective-permute-start(bf16[576,512]{1,0:T(8,128)(2,1)S(1)} %pad_maximum_fusion.1), channel_id=1, source_target_pairs={{0,2},{1,5},{2,0},{3,7},{4,6},{5,1},{6,4},{7,3},{8,10},{9,13},{10,... | collective-permute-start | bytes 1769480 | tf_op jit(solution)/shard_map/ppermute | solution.py:643
  31.8 10.0 %collective-permute-start.6 = (bf16[256,512]{1,0:T(8,128)(2,1)S(1)}, bf16[256,512]{1,0:T(8,128)(2,1)S(1)}, u32[]{:S(2)}, u32[]{:S(2)}) collective-permute-start(bf16[256,512]{1,0:T(8,128)(2,1)S(1)} %broadcast_select_fusion.2), channel_id=1, source_target_pairs={{8,0},{9,1},{10,2},{11,3},{12,4},{13,5},{14,6},{15,7},{16,24},{17,... | collective-permute-start | bytes 786440 | tf_op jit(solution)/shard_map/ppermute | solution.py:592
  42.0 3.1 %collective-permute-start.11 = (bf16[512,512]{1,0:T(8,128)(2,1)S(1)}, bf16[512,512]{1,0:T(8,128)(2,1)S(1)}, u32[]{:S(2)}, u32[]{:S(2)}) collective-permute-start(bf16[512,512]{1,0:T(8,128)(2,1)S(1)} %pad_maximum_fusion.3.refs_0_), channel_id=1, source_target_pairs={{0,1},{1,0},{2,3},{3,2},{4,5},{5,4},{6,7},{7,6},{8,9},{9,8},{10,11... | collective-permute-start | bytes 1572872 | tf_op jit(solution)/shard_map/ppermute | solution.py:580
  42.6 3.3 %collective-permute-start.13 = (bf16[576,512]{1,0:T(8,128)(2,1)S(1)}, bf16[576,512]{1,0:T(8,128)(2,1)S(1)}, u32[]{:S(2)}, u32[]{:S(2)}) collective-permute-start(bf16[576,512]{1,0:T(8,128)(2,1)S(1)} %collective-permute-done.5.refs_2_), channel_id=1, source_target_pairs={{0,1},{1,0},{2,3},{3,2},{4,5},{5,4},{6,7},{7,6},{8,9},{9,8},{10,11... | collective-permute-start | bytes 1769480 | tf_op jit(solution)/shard_map/ppermute | solution.py:580
  42.7 9.2 %collective-permute-start.8 = (bf16[288,512]{1,0:T(8,128)(2,1)S(1)}, bf16[288,512]{1,0:T(8,128)(2,1)S(1)}, u32[]{:S(2)}, u32[]{:S(2)}) collective-permute-start(bf16[288,512]{1,0:T(8,128)(2,1)S(1)} %slice.113), channel_id=1, source_target_pairs={{0,4},{1,3},{2,6},{3,1},{4,0},{5,7},{6,2},{7,5},{8,12},{9,11},{10,... | collective-permute-start | bytes 884744 | tf_op jit(solution)/shard_map/ppermute | solution.py:647
  43.6 11.0 %collective-permute-start.9 = (bf16[512,512]{1,0:T(8,128)(2,1)S(1)}, bf16[512,512]{1,0:T(8,128)(2,1)S(1)}, u32[]{:S(2)}, u32[]{:S(2)}) collective-permute-start(bf16[512,512]{1,0:T(8,128)(2,1)S(1)} %pad_maximum_fusion.2), channel_id=1, source_target_pairs={{0,2},{1,5},{2,0},{3,7},{4,6},{5,1},{6,4},{7,3},{8,10},{9,13},{10,... | collective-permute-start | bytes 1572872 | tf_op jit(solution)/shard_map/ppermute | solution.py:643
  45.2 28.4 %collective-permute-start.12 = (bf16[1024,512]{1,0:T(8,128)(2,1)S(1)}, bf16[1024,512]{1,0:T(8,128)(2,1)}, u32[]{:S(2)}, u32[]{:S(2)}) collective-permute-start(bf16[1024,512]{1,0:T(8,128)(2,1)S(1)} %pad_maximum_fusion), channel_id=1, source_target_pairs={{0,2},{1,5},{2,0},{3,7},{4,6},{5,1},{6,4},{7,3},{8,10},{9,13},{10,... | collective-permute-start | bytes 3145736 | tf_op jit(solution)/shard_map/ppermute | solution.py:643
  54.6 2.0 collective-permute-start.14
  55.4 18.2 %collective-permute-start.10 = (bf16[256,512]{1,0:T(8,128)(2,1)S(1)}, bf16[256,512]{1,0:T(8,128)(2,1)S(1)}, u32[]{:S(2)}, u32[]{:S(2)}) collective-permute-start(bf16[256,512]{1,0:T(8,128)(2,1)S(1)} %slice.114), channel_id=1, source_target_pairs={{0,4},{1,3},{2,6},{3,1},{4,0},{5,7},{6,2},{7,5},{8,12},{9,11},{10,... | collective-permute-start | bytes 786440 | tf_op jit(solution)/shard_map/ppermute | solution.py:647
  73.6 2.9 %collective-permute-start.17 = (bf16[512,512]{1,0:T(8,128)(2,1)S(1)}, bf16[512,512]{1,0:T(8,128)(2,1)S(1)}, u32[]{:S(2)}, u32[]{:S(2)}) collective-permute-start(bf16[512,512]{1,0:T(8,128)(2,1)S(1)} %copy-done.14), channel_id=1, source_target_pairs={{0,1},{1,0},{2,3},{3,2},{4,5},{5,4},{6,7},{7,6},{8,9},{9,8},{10,11... | collective-permute-start | bytes 1572872 | tf_op jit(solution)/shard_map/ppermute | solution.py:580
  74.1 2.5 collective-permute-start.18
  75.3 24.6 %collective-permute-start.15 = (bf16[1024,512]{1,0:T(8,128)(2,1)}, bf16[1024,512]{1,0:T(8,128)(2,1)S(1)}, u32[]{:S(2)}, u32[]{:S(2)}) collective-permute-start(bf16[1024,512]{1,0:T(8,128)(2,1)} %collective-permute-done.12.refs_2_), channel_id=1, source_target_pairs={{0,1},{1,0},{2,3},{3,2},{4,5},{5,4},{6,7},{7,6},{8,9},{9,8},{10,11... | collective-permute-start | bytes 3145736 | tf_op jit(solution)/shard_map/ppermute | solution.py:580
  75.7 21.9 %collective-permute-start.16 = (bf16[512,512]{1,0:T(8,128)(2,1)S(1)}, bf16[512,512]{1,0:T(8,128)(2,1)S(1)}, u32[]{:S(2)}, u32[]{:S(2)}) collective-permute-start(bf16[512,512]{1,0:T(8,128)(2,1)S(1)} %slice.123), channel_id=1, source_target_pairs={{0,4},{1,3},{2,6},{3,1},{4,0},{5,7},{6,2},{7,5},{8,12},{9,11},{10,... | collective-permute-start | bytes 1572872 | tf_op jit(solution)/shard_map/ppermute | solution.py:647
  97.7 2.2 collective-permute-start.19
  127.0 4.5 %collective-permute-start.20 = (bf16[4,512,512]{2,1,0:T(8,128)(2,1)}, bf16[4,512,512]{2,1,0:T(8,128)(2,1)S(1)}, u32[]{:S(2)}, u32[]{:S(2)}) collective-permute-start(bf16[4,512,512]{2,1,0:T(8,128)(2,1)} %get-tuple-element.111), channel_id=1, source_target_pairs={{0,1},{1,0},{2,3},{3,2},{4,5},{5,4},{6,7},{7,6},{8,9},{9,8},{10,11... | collective-permute-start | bytes 6291464 | tf_op jit(solution)/shard_map/ppermute | solution.py:580
  135.0 38.2 %all-to-all-start = ((bf16[4,512,512]{2,1,0:T(8,128)(2,1)}), bf16[4,512,512]{2,1,0:T(8,128)(2,1)S(1)}, u32[]{:S(2)}, u32[]{:S(2)}) async-start(bf16[4,512,512]{2,1,0:T(8,128)(2,1)} %add_convert_fusion), calls=%async_computation | async-start | bytes 4194304 | tf_op jit(solution)/shard_map/all_to_all | solution.py:680
  173.9 3.0 %collective-permute-start.21 = (bf16[4,272,512]{2,1,0:T(8,128)(2,1)}, bf16[4,272,512]{2,1,0:T(8,128)(2,1)S(1)}, u32[]{:S(2)}, u32[]{:S(2)}) collective-permute-start(bf16[4,272,512]{2,1,0:T(8,128)(2,1)} %get-tuple-element.132), channel_id=1, source_target_pairs={{0,1},{1,0},{2,3},{3,2},{4,5},{5,4},{6,7},{7,6},{8,9},{9,8},{10,11... | collective-permute-start | bytes 3342344 | tf_op jit(solution)/shard_map/ppermute | solution.py:580
  179.5 22.8 %all-to-all-start.1 = ((bf16[4,272,512]{2,1,0:T(8,128)(2,1)}), bf16[4,272,512]{2,1,0:T(8,128)(2,1)S(1)}, u32[]{:S(2)}, u32[]{:S(2)}) async-start(bf16[4,272,512]{2,1,0:T(8,128)(2,1)} %add_convert_fusion.1), calls=%async_computation.1 | async-start | bytes 2228224 | tf_op jit(solution)/shard_map/all_to_all | solution.py:680
  202.7 14.9 %collective-permute-start.22 = (bf16[272,512]{1,0:T(8,128)(2,1)S(1)}, bf16[272,512]{1,0:T(8,128)(2,1)S(1)}, u32[]{:S(2)}, u32[]{:S(2)}) collective-permute-start(bf16[272,512]{1,0:T(8,128)(2,1)S(1)} %get-tuple-element.180), channel_id=1, source_target_pairs={{0,8},{1,9},{2,10},{3,11},{4,12},{5,13},{6,14},{7,15},{24,16},{25,... | collective-permute-start | bytes 835592 | tf_op jit(solution)/shard_map/ppermute | solution.py:592
  217.6 3.0 %collective-permute-start.23 = (bf16[4,272,512]{2,1,0:T(8,128)(2,1)}, bf16[4,272,512]{2,1,0:T(8,128)(2,1)S(1)}, u32[]{:S(2)}, u32[]{:S(2)}) collective-permute-start(bf16[4,272,512]{2,1,0:T(8,128)(2,1)} %get-tuple-element.155), channel_id=1, source_target_pairs={{0,1},{1,0},{2,3},{3,2},{4,5},{5,4},{6,7},{7,6},{8,9},{9,8},{10,11... | collective-permute-start | bytes 3342344 | tf_op jit(solution)/shard_map/ppermute | solution.py:580
  222.0 9.5 %collective-permute-start.24 = (bf16[272,512]{1,0:T(8,128)(2,1)S(1)}, bf16[272,512]{1,0:T(8,128)(2,1)S(1)}, u32[]{:S(2)}, u32[]{:S(2)}) collective-permute-start(bf16[272,512]{1,0:T(8,128)(2,1)S(1)} %get-tuple-element.169), channel_id=1, source_target_pairs={{0,2},{1,3},{2,0},{3,1},{4,6},{5,7},{6,4},{7,5},{8,10},{9,11},{10,... | collective-permute-start | bytes 835592 | tf_op jit(solution)/shard_map/ppermute | solution.py:580
  224.1 14.2 %collective-permute-start.26 = (bf16[272,512]{1,0:T(8,128)(2,1)S(1)}, bf16[272,512]{1,0:T(8,128)(2,1)S(1)}, u32[]{:S(2)}, u32[]{:S(2)}) collective-permute-start(bf16[272,512]{1,0:T(8,128)(2,1)S(1)} %get-tuple-element.170), channel_id=1, source_target_pairs={{0,6},{1,7},{2,4},{3,5},{4,2},{5,3},{6,0},{7,1},{8,14},{9,15},{10,... | collective-permute-start | bytes 835592 | tf_op jit(solution)/shard_map/ppermute | solution.py:580
  225.5 14.1 %collective-permute-start.25 = (bf16[272,512]{1,0:T(8,128)(2,1)S(1)}, bf16[272,512]{1,0:T(8,128)(2,1)S(1)}, u32[]{:S(2)}, u32[]{:S(2)}) collective-permute-start(bf16[272,512]{1,0:T(8,128)(2,1)S(1)} %get-tuple-element.171), channel_id=1, source_target_pairs={{0,4},{1,5},{2,6},{3,7},{4,0},{5,1},{6,2},{7,3},{8,12},{9,13},{10,... | collective-permute-start | bytes 835592 | tf_op jit(solution)/shard_map/ppermute | solution.py:580
  240.9 8.4 %collective-permute-start.27 = (bf16[272,512]{1,0:T(8,128)(2,1)S(1)}, bf16[272,512]{1,0:T(8,128)(2,1)S(1)}, u32[]{:S(2)}, u32[]{:S(2)}) collective-permute-start(bf16[272,512]{1,0:T(8,128)(2,1)S(1)} %get-tuple-element.167), channel_id=1, source_target_pairs={{8,0},{9,1},{10,2},{11,3},{12,4},{13,5},{14,6},{15,7},{16,8},{17,9... | collective-permute-start | bytes 835592 | tf_op jit(solution)/shard_map/ppermute | solution.py:592
  242.2 9.2 %collective-permute-start.28 = (bf16[272,512]{1,0:T(8,128)(2,1)S(1)}, bf16[272,512]{1,0:T(8,128)(2,1)S(1)}, u32[]{:S(2)}, u32[]{:S(2)}) collective-permute-start(bf16[272,512]{1,0:T(8,128)(2,1)S(1)} %get-tuple-element.179), channel_id=1, source_target_pairs={{0,8},{1,9},{2,10},{3,11},{4,12},{5,13},{6,14},{7,15},{8,16},{9,17... | collective-permute-start | bytes 835592 | tf_op jit(solution)/shard_map/ppermute | solution.py:592
  251.7 7.5 %collective-permute-start.29 = (bf16[272,512]{1,0:T(8,128)(2,1)S(1)}, bf16[272,512]{1,0:T(8,128)(2,1)S(1)}, u32[]{:S(2)}, u32[]{:S(2)}) collective-permute-start(bf16[272,512]{1,0:T(8,128)(2,1)S(1)} %fusion.17), channel_id=1, source_target_pairs={{16,0},{17,1},{18,2},{19,3},{20,4},{21,5},{22,6},{23,7},{0,8},{1,9... | collective-permute-start | bytes 835592 | tf_op jit(solution)/shard_map/ppermute | solution.py:592
  262.3 14.2 %all-to-all-start.2 = ((f32[32,8,128]{2,1,0:T(8,128)}), f32[32,8,128]{2,1,0:T(8,128)S(1)}, u32[]{:S(2)}, u32[]{:S(2)}) async-start(f32[32,8,128]{2,1,0:T(8,128)} %broadcast_in_dim.30), calls=%async_computation.2 | async-start | bytes 262144 | tf_op jit(solution)/shard_map/all_to_all | solution.py:722
  274.9 4.4 %collective-permute-start.30 = (f32[8704]{0:T(1024)S(1)}, f32[8704]{0:T(1024)S(1)}, u32[]{:S(2)}, u32[]{:S(2)}) collective-permute-start(f32[8704]{0:T(1024)S(1)} %slice.144), channel_id=1, source_target_pairs={{1,0},{2,1},{3,2},{4,3},{5,4},{6,5},{7,6},{8,7},{9,8},{10,9},{11,1... | collective-permute-start | bytes 104456 | tf_op jit(solution)/shard_map/ppermute | solution.py:713
  (28 other events, 185.7 us)

commit v2 on v1

--- a/solution.py
+++ b/solution.py
@@ -13,6 +13,8 @@
 STEP = 10
 ROWS = 256
 BLOCKS = LEN // ROWS
+TALL = 512
+TALLS = LEN // TALL
 LANES = 128
 PAIRS = D // LANES
 MASK_LANE = 32
@@ -82,7 +84,7 @@
     return jnp.where(ok, 0.0, masked_value)
 
 
-def attend_forward(q_ref, k_ref, v_ref, qa_ref, ka_ref, o_ref, qal_ref, kt_ref, kat_ref, causal):
+def attend_forward(moves, q_ref, k_ref, v_ref, qa_ref, ka_ref, o_ref, qal_ref, kt_ref, kat_ref, causal):
     size, depth = (ROWS, 2) if causal else (2 * ROWS, 1)
     lane = lax.broadcasted_iota(jnp.int32, (size, LANES), 1)
     low = lane < 64
@@ -132,6 +134,8 @@
                     lanes = pl.ds(head // 2 * LANES, LANES)
                     o_ref[rows, lanes] = jnp.where(low, outs[-2], outs[-1]).astype(BF)
         qal_ref[rows, :] = (qa_ref[rows, :].astype(F32) + lse_parts).astype(BF)
+        moves.done(o_ref, rows)
+        moves.done(qal_ref, rows)
 
 
 def attend_backward(
@@ -139,7 +143,8 @@
     causal, span=(0, PAIRS),
 ):
     bias = causal_bias(True) if causal else None
-    kt_ref[...] = k_ref[...].T
+    cols = pl.ds(span[0] * LANES, (span[1] - span[0]) * LANES)
+    kt_ref[cols, :] = k_ref[:, cols].T
 
     def score(head, block):
         lanes = pl.ds(head // 2 * LANES, LANES)
@@ -191,19 +196,18 @@
         finish(head, block, *current)
         if head % 2 and block == BLOCKS - 1:
             pair_end(head // 2)
-    cols = pl.ds(span[0] * LANES, (span[1] - span[0]) * LANES)
     for block in range(BLOCKS):
         rows = pl.ds(block * ROWS, ROWS)
         dq_ref[rows, cols] = (dqt_ref[cols, rows] * 0.125).T.astype(BF)
 
 
 def mix_gradient(g_ref, w_out, o_ref, do_ref, del_ref):
-    lane = lax.broadcasted_iota(jnp.int32, (ROWS, LANES), 1)
+    lane = lax.broadcasted_iota(jnp.int32, (TALL, LANES), 1)
     even = lane % 2 == 0
     col = lax.broadcasted_iota(jnp.int32, (D, LANES), 0) // 64
     pick = jnp.where(lax.broadcasted_iota(jnp.int32, (D, LANES), 1) // 2 == col, -1.0, 0.0).astype(BF)
-    for qb in range(BLOCKS):
-        rows = pl.ds(qb * ROWS, ROWS)
+    for qb in range(TALLS):
+        rows = pl.ds(qb * TALL, TALL)
         do = nt(g_ref[rows, :], w_out).astype(BF)
         do_ref[rows, :] = do
         prod = do.astype(F32) * o_ref[rows, :].astype(F32)
@@ -217,11 +221,48 @@
     return vec_ref[index : index + 1, :]
 
 
-def fetch(core_ref, parts, w_ref, sems, rows=ROWS, first=0):
+class Moves:
+    def __init__(self, sems):
+        self.sems, self.used = sems, 0
+        self.inward, self.outward = {}, []
+
+    def copy(self, source, target):
+        move = pltpu.make_async_copy(source, target, self.sems.at[self.used])
+        self.used += 1
+        move.start()
+        return move
+
+    def bring(self, source, target, key):
+        self.inward.setdefault(id(key), []).append(self.copy(source, target))
+
+    def need(self, *refs):
+        for ref in refs:
+            for move in self.inward.pop(id(ref), []):
+                move.wait()
+
+    def pair(self, scratch, out):
+        self.outs = getattr(self, "outs", {})
+        self.outs[id(scratch)] = out
+
+    def done(self, ref, *where):
+        out = self.outs[id(ref)]
+        if where:
+            ref, out = ref.at[where], out.at[where]
+        self.outward.append(self.copy(ref, out))
+
+    def finish(self):
+        for moves in self.inward.values():
+            for move in moves:
+                move.wait()
+        for move in self.outward:
+            move.wait()
+
+
+def fetch(moves, core_ref, parts, w_ref, rows=ROWS, first=0):
     core, chip = core_ref[0], core_ref[1]
     near, far = chip ^ (1 + core), chip ^ (2 - core)
     own, other = core, 1 - core
-    moves = (
+    places = (
         (0, 0, chip, own),
         (1, 0, chip, other),
         (2, 0, near, own),
@@ -231,18 +272,9 @@
         (4, 0, chip ^ 3, own),
         (5, 0, chip ^ 3, other),
     )
-    copies = []
-    for i, (part, start, place, half) in enumerate(moves):
+    for part, start, place, half in places:
         source = parts[part].at[pl.ds(start + first, ROWS)]
-        copies.append(pltpu.make_async_copy(source, w_ref.at[2 * place + half], sems.at[i]))
-    for copy in copies:
-        copy.start()
-    return copies
-
-
-def wait_all(copies):
-    for copy in copies:
-        copy.wait()
+        moves.bring(source, w_ref.at[2 * place + half], w_ref)
 
 
 def square(w_ref, matrix):
@@ -250,60 +282,76 @@
 
 
 def put_square(mine_ref, other_ref, core, matrix, turned_ref, grad, place=0):
-    for ref, half in ((mine_ref, core), (other_ref, 1 - core)):
-        rows = turned_ref[pl.ds(pl.multiple_of(half * ROWS, ROWS), ROWS), :]
-        ref[matrix ^ place, :ROWS, :] = nn(rows, grad).astype(BF)
+    halves = [turned_ref[pl.ds(pl.multiple_of(h * ROWS, ROWS), ROWS), :] for h in (core, 1 - core)]
+    both = nn(jnp.concatenate(halves, axis=0), grad).astype(BF)
+    mine_ref[matrix ^ place, :ROWS, :] = both[:ROWS]
+    other_ref[matrix ^ place, :ROWS, :] = both[ROWS:]
 
 
 def put_square_tn(mine_ref, other_ref, core, matrix, left_ref, grad, place=0):
-    for ref, half in ((mine_ref, core), (other_ref, 1 - core)):
-        cols = left_ref[:, pl.ds(pl.multiple_of(half * ROWS, ROWS), ROWS)]
-        ref[matrix ^ place, :ROWS, :] = tn(cols, grad).astype(BF)
+    halves = [left_ref[:, pl.ds(pl.multiple_of(h * ROWS, ROWS), ROWS)] for h in (core, 1 - core)]
+    both = tn(jnp.concatenate(halves, axis=1), grad).astype(BF)
+    mine_ref[matrix ^ place, :ROWS, :] = both[:ROWS]
+    other_ref[matrix ^ place, :ROWS, :] = both[ROWS:]
 
 
 def self_forward_kernel(
-    core_ref, parts, x_ref, vec_ref, qa_ref, ka_ref,
+    moves, core_ref, parts, x_ref, vec_ref, qa_ref, ka_ref,
     q_ref, k_ref, v_ref, o_ref, qal_ref, n_ref, r_ref,
-    w_ref, kt_ref, kat_ref, sems,
+    w_ref, kt_ref, kat_ref,
 ):
-    copies = fetch(core_ref, parts, w_ref, sems, FIRST_ROWS)
-    wait_all(copies)
-    for qb in range(BLOCKS):
-        rows = pl.ds(qb * ROWS, ROWS)
+    fetch(moves, core_ref, parts, w_ref, FIRST_ROWS)
+    moves.need(x_ref, vec_ref, w_ref)
+    for qb in range(TALLS):
+        rows = pl.ds(qb * TALL, TALL)
         x = x_ref[rows, :]
         q_ref[rows, :] = ((nn(x, square(w_ref, 0)) + vec_row(vec_ref, 6)) * query_scale).astype(BF)
         k_ref[rows, :] = nn(x, square(w_ref, 1)).astype(BF)
         v_ref[rows, :] = (nn(x, square(w_ref, 2)) + vec_row(vec_ref, 7)).astype(BF)
-    attend_forward(q_ref, k_ref, v_ref, qa_ref, ka_ref, o_ref, qal_ref, kt_ref, kat_ref, True)
-    for qb in range(BLOCKS):
-        rows = pl.ds(qb * ROWS, ROWS)
+    moves.need(qa_ref, ka_ref)
+    for ref in (q_ref, k_ref, v_ref):
+        moves.done(ref)
+    attend_forward(moves, q_ref, k_ref, v_ref, qa_ref, ka_ref, o_ref, qal_ref, kt_ref, kat_ref, True)
+    for qb in range(TALLS):
+        rows = pl.ds(qb * TALL, TALL)
         resid = x_ref[rows, :].astype(F32) + nn(o_ref[rows, :], square(w_ref, 3)) + vec_row(vec_ref, 8)
         normed, inv_std = layer_norm(resid)
         n_ref[rows, :] = normed
-        r_ref[rows, :] = jnp.broadcast_to(inv_std, (ROWS, LANES))
+        r_ref[rows, :] = jnp.broadcast_to(inv_std, (TALL, LANES))
+        moves.done(n_ref, rows)
+    moves.done(r_ref)
 
 
 def cross_forward_kernel(
-    core_ref, parts, n1_ref, m_ref, vec_ref, qa_ref, ka_ref,
+    moves, core_ref, parts, n1_ref, vec_ref, m_ref, qa_ref, ka_ref,
     q_ref, k_ref, v_ref, o_ref, qal_ref, n_ref, r_ref,
-    w_ref, kt_ref, kat_ref, sems,
+    w_ref, kt_ref, kat_ref,
 ):
-    wait_all(fetch(core_ref, parts, w_ref, sems))
-    for qb in range(BLOCKS):
-        rows = pl.ds(qb * ROWS, ROWS)
-        h = (n1_ref[rows, :] * vec_row(vec_ref, 0) + vec_row(vec_ref, 1)).astype(BF)
+    fetch(moves, core_ref, parts, w_ref)
+    moves.need(m_ref, vec_ref, w_ref)
+    for qb in range(TALLS):
+        rows = pl.ds(qb * TALL, TALL)
         m = m_ref[rows, :]
-        q_ref[rows, :] = ((nn(h, square(w_ref, 0)) + vec_row(vec_ref, 9)) * query_scale).astype(BF)
         k_ref[rows, :] = nn(m, square(w_ref, 1)).astype(BF)
         v_ref[rows, :] = (nn(m, square(w_ref, 2)) + vec_row(vec_ref, 10)).astype(BF)
-    attend_forward(q_ref, k_ref, v_ref, qa_ref, ka_ref, o_ref, qal_ref, kt_ref, kat_ref, False)
-    for qb in range(BLOCKS):
-        rows = pl.ds(qb * ROWS, ROWS)
+    moves.need(n1_ref)
+    for qb in range(TALLS):
+        rows = pl.ds(qb * TALL, TALL)
+        h = (n1_ref[rows, :] * vec_row(vec_ref, 0) + vec_row(vec_ref, 1)).astype(BF)
+        q_ref[rows, :] = ((nn(h, square(w_ref, 0)) + vec_row(vec_ref, 9)) * query_scale).astype(BF)
+    moves.need(qa_ref, ka_ref)
+    for ref in (q_ref, k_ref, v_ref):
+        moves.done(ref)
+    attend_forward(moves, q_ref, k_ref, v_ref, qa_ref, ka_ref, o_ref, qal_ref, kt_ref, kat_ref, False)
+    for qb in range(TALLS):
+        rows = pl.ds(qb * TALL, TALL)
         h = n1_ref[rows, :] * vec_row(vec_ref, 0) + vec_row(vec_ref, 1)
         resid = h + nn(o_ref[rows, :], square(w_ref, 3)) + vec_row(vec_ref, 11)
         normed, inv_std = layer_norm(resid)
         n_ref[rows, :] = normed
-        r_ref[rows, :] = jnp.broadcast_to(inv_std, (ROWS, LANES))
+        r_ref[rows, :] = jnp.broadcast_to(inv_std, (TALL, LANES))
+        moves.done(n_ref, rows)
+    moves.done(r_ref)
 
 
 def col_sum(x):
@@ -311,13 +359,12 @@
 
 
 def ffn_kernel(
-    core_ref, parts, n2_ref, r2_ref, cot_ref, vec_ref,
+    moves, core_ref, parts, n2_ref, vec_ref, cot_ref, r2_ref,
     out_ref, mine_ref, other_ref, dr_ref, vg_ref,
-    w1_ref, w2_ref, u_ref, da_ref, h_ref, dz_ref, f_ref, ht_ref, sems1, sems2,
+    w1_ref, w2_ref, u_ref, da_ref, h_ref, dz_ref, f_ref, ht_ref,
 ):
-    copies = fetch(core_ref, parts, w1_ref, sems1, 2 * ROWS)
-    copies += fetch(core_ref, parts, w2_ref, sems2, 2 * ROWS, ROWS)
-    wait_all(copies)
+    fetch(moves, core_ref, parts, w1_ref, 2 * ROWS)
+    fetch(moves, core_ref, parts, w2_ref, 2 * ROWS, ROWS)
 
     def w1_block(j):
         return w1_ref[:, 64 * j : 64 * j + 64].reshape(D, D)
@@ -326,9 +373,9 @@
         return square(w2_ref, j)
 
     vg_ref[...] = jnp.zeros_like(vg_ref)
-
-    def one_tile(tile, carry):
-        rows = pl.ds(pl.multiple_of(tile * ROWS, ROWS), ROWS)
+    moves.need(n2_ref, vec_ref, w1_ref)
+    for tile in range(TALLS):
+        rows = pl.ds(tile * TALL, TALL)
         n2 = n2_ref[rows, :]
         h2 = n2 * vec_row(vec_ref, 2) + vec_row(vec_ref, 3)
         h2_low = h2.astype(BF)
@@ -340,10 +387,13 @@
             u = (a * s).astype(BF)
             u_ref[rows, j * D : (j + 1) * D] = u
             f_ref[:, j * D : (j + 1) * D] = s * (1.0 + a * (1.0 - s))
+            moves.need(w2_ref)
             resid = resid + nn(u, w2_block(j))
         n3, inv3 = layer_norm(resid)
         gain3 = vec_row(vec_ref, 4)
         out_ref[rows, :] = (n3 * gain3 + vec_row(vec_ref, 5)).astype(BF)
+        moves.done(out_ref, rows)
+        moves.need(cot_ref)
         cot = cot_ref[rows, :].astype(F32)
         dr3 = norm_back(cot, n3, inv3, gain3)
         dz = dr3.astype(BF)
@@ -359,111 +409,136 @@
             dh = dh + nt(da, w1_block(j))
         vg_ref[2:3, :] += col_sum(dh * n2)
         vg_ref[3:4, :] += col_sum(dh)
+        moves.need(r2_ref)
         dr2 = norm_back(dh, n2, r2_ref[rows, 0:1], vec_row(vec_ref, 2))
         dr_ref[rows, :] = dr2
+        moves.done(dr_ref, rows)
         vg_ref[11:12, :] += col_sum(dr2.astype(BF))
-        return carry
-
-    lax.fori_loop(0, BLOCKS, one_tile, 0)
+    moves.done(vg_ref)
     core = core_ref[0]
     ht_ref[...] = jnp.swapaxes(h_ref[...].T.reshape(4, 2, 64, LEN), 0, 1).reshape(2, ROWS, LEN)
+    dz = dz_ref[...]
+    turned = jnp.concatenate([ht_ref[1 - core], ht_ref[core]], axis=0)
     for j in range(4):
-        da = da_ref[:, j * D : (j + 1) * D]
-        dz = dz_ref[...]
-        for ref, half in ((mine_ref, core), (other_ref, 1 - core)):
-            dw1 = nn(ht_ref[half], da).astype(BF)
-            ref[:, 64 * j : 64 * j + 64, :] = dw1.reshape(4, 64, D)
-            cols = pl.ds(pl.multiple_of(j * D + half * ROWS, ROWS), ROWS)
-            ref[j, ROWS:, :] = tn(u_ref[:, cols], dz).astype(BF)
+        starts = [pl.multiple_of(j * D + h * ROWS, ROWS) for h in (1 - core, core)]
+        cols = jnp.concatenate([u_ref[:, pl.ds(start, ROWS)] for start in starts], axis=1)
+        dw1 = nn(turned, da_ref[:, j * D : (j + 1) * D]).astype(BF)
+        dw2 = tn(cols, dz).astype(BF)
+        for place, ref in enumerate((other_ref, mine_ref)):
+            half = slice(place * ROWS, place * ROWS + ROWS)
+            ref[:, 64 * j : 64 * j + 64, :] = dw1[half].reshape(4, 64, D)
+            ref[j, ROWS:, :] = dw2[half]
+            moves.done(ref, j, pl.ds(ROWS, ROWS))
+    for j in range(4):
+        for ref in (other_ref, mine_ref):
+            moves.done(ref, j, pl.ds(0, ROWS))
 
 
 def cross_backward_kernel(
-    core_ref, parts, dr2_ref, vec_ref, q_ref, k_ref, v_ref, o_ref, qal_ref, ka_ref, n1_ref, r1_ref, mt_ref, vf_ref,
+    moves, core_ref, parts, dr2_ref, o_ref, q_ref, k_ref, v_ref, qal_ref, ka_ref, mt_ref, n1_ref, vec_ref, vf_ref, r1_ref,
     mine_ref, other_ref, dr1_ref, dk_ref, dv_ref,
-    g_ref, do_ref, del_ref, dq_ref, p_ref, s_ref, h_ref, w_ref, vg_ref, kt_ref, dqt_ref, sems,
+    g_ref, do_ref, del_ref, dq_ref, p_ref, s_ref, h_ref, w_ref, vg_ref, kt_ref, dqt_ref,
 ):
     core = core_ref[0]
-    copies = fetch(core_ref, parts, w_ref, sems)
-    for qb in range(BLOCKS):
-        rows = pl.ds(qb * ROWS, ROWS)
+    fetch(moves, core_ref, parts, w_ref)
+    moves.need(dr2_ref)
+    for qb in range(TALLS):
+        rows = pl.ds(qb * TALL, TALL)
         g_ref[rows, :] = dr2_ref[rows, :].astype(BF)
-        h_ref[rows, :] = (n1_ref[rows, :] * vec_row(vec_ref, 0) + vec_row(vec_ref, 1)).astype(BF)
-    wait_all(copies)
+    moves.need(w_ref, o_ref)
     mix_gradient(g_ref, square(w_ref, 3), o_ref, do_ref, del_ref)
     put_square_tn(mine_ref, other_ref, core, 3, o_ref, g_ref[...])
+    moves.need(q_ref, k_ref, v_ref, qal_ref, ka_ref)
     attend_backward(
         q_ref, k_ref, v_ref, do_ref, qal_ref, del_ref, ka_ref, dq_ref, dk_ref, dv_ref, p_ref, s_ref, kt_ref, dqt_ref, False
     )
-    put_square_tn(mine_ref, other_ref, core, 0, h_ref, dq_ref[...])
-    put_square(mine_ref, other_ref, core, 1, mt_ref, dk_ref[...])
-    put_square(mine_ref, other_ref, core, 2, mt_ref, dv_ref[...])
+    moves.done(dk_ref)
+    moves.done(dv_ref)
+    moves.need(n1_ref, vec_ref, vf_ref, r1_ref, mt_ref)
     vg_ref[...] = vf_ref[...]
-    for qb in range(BLOCKS):
-        rows = pl.ds(qb * ROWS, ROWS)
+    for qb in range(TALLS):
+        rows = pl.ds(qb * TALL, TALL)
         dq = dq_ref[rows, :]
-        dv = dv_ref[rows, :]
         vg_ref[9:10, :] += col_sum(dq)
-        vg_ref[10:11, :] += col_sum(dv)
+        vg_ref[10:11, :] += col_sum(dv_ref[rows, :])
         dh = dr2_ref[rows, :] + nt(dq, square(w_ref, 0))
         n1 = n1_ref[rows, :]
         vg_ref[0:1, :] += col_sum(dh * n1)
         vg_ref[1:2, :] += col_sum(dh)
         dr1 = norm_back(dh, n1, r1_ref[rows, 0:1], vec_row(vec_ref, 0))
         dr1_ref[rows, :] = dr1
+        moves.done(dr1_ref, rows)
         vg_ref[8:9, :] += col_sum(dr1.astype(BF))
+        h_ref[rows, :] = (n1 * vec_row(vec_ref, 0) + vec_row(vec_ref, 1)).astype(BF)
     blank = jnp.zeros((12, D), F32)
     for ref, half in ((mine_ref, core), (other_ref, 1 - core)):
         for xy in range(4):
             low, high = vg_ref[8 * xy : 8 * xy + 4, :], vg_ref[8 * xy + 4 : 8 * xy + 8, :]
             rows = jnp.where(half == 0, low, high)
             ref[xy, ROWS:, :] = jnp.concatenate([rows, blank], axis=0).astype(BF)
+        moves.done(ref, 3)
+    put_square(mine_ref, other_ref, core, 1, mt_ref, dk_ref[...])
+    put_square(mine_ref, other_ref, core, 2, mt_ref, dv_ref[...])
+    for ref in (mine_ref, other_ref):
+        moves.done(ref, 1)
+        moves.done(ref, 2)
+    put_square_tn(mine_ref, other_ref, core, 0, h_ref, dq_ref[...])
+    for ref in (mine_ref, other_ref):
+        moves.done(ref, 0)
+
+
+EARLY = pl.ds(0, EARLY_PAIRS * LANES)
+LATE = pl.ds(EARLY_PAIRS * LANES, (PAIRS - EARLY_PAIRS) * LANES)
+EVERY = slice(None)
 
 
 def self_backward_start_kernel(
-    core_ref, parts, dr1_ref, q_ref, k_ref, v_ref, o_ref, qal_ref, ka_ref,
-    do_ref, del_ref, dq_ref, dk_ref, dv_ref,
-    g_ref, p_ref, s_ref, w_ref, kt_ref, dqt_ref, sems,
+    moves, core_ref, parts, dr1_ref, o_ref, q_ref, k_ref, v_ref, qal_ref, ka_ref,
+    do_ref, del_ref, dq_ref, dk_ref, dv_ref, so_ref,
+    g_ref, p_ref, s_ref, w_ref, kt_ref, dqt_ref,
 ):
-    copies = fetch(core_ref, parts, w_ref, sems, FIRST_ROWS)
-    for qb in range(BLOCKS):
-        rows = pl.ds(qb * ROWS, ROWS)
+    core = core_ref[0]
+    fetch(moves, core_ref, parts, w_ref, FIRST_ROWS)
+    moves.need(dr1_ref)
+    for qb in range(TALLS):
+        rows = pl.ds(qb * TALL, TALL)
         g_ref[rows, :] = dr1_ref[rows, :].astype(BF)
-    wait_all(copies)
+    moves.need(w_ref, o_ref)
     mix_gradient(g_ref, square(w_ref, 3), o_ref, do_ref, del_ref)
+    moves.done(do_ref, EVERY, LATE)
+    moves.done(del_ref)
+    halves = [o_ref[:, pl.ds(pl.multiple_of(h * ROWS, ROWS), ROWS)] for h in (core, 1 - core)]
+    so_ref[...] = tn(jnp.concatenate(halves, axis=1), g_ref[...]).astype(BF).reshape(2, ROWS, D)
+    moves.done(so_ref)
+    moves.need(q_ref, k_ref, v_ref, qal_ref, ka_ref)
     attend_backward(
         q_ref, k_ref, v_ref, do_ref, qal_ref, del_ref, ka_ref, dq_ref, dk_ref, dv_ref, p_ref, s_ref, kt_ref, dqt_ref, True,
         (0, EARLY_PAIRS),
     )
+    for ref in (dq_ref, dk_ref, dv_ref):
+        moves.done(ref, EVERY, EARLY)
 
 
 def self_backward_end_kernel(
-    core_ref, dr1_ref, q_ref, k_ref, v_ref, o_ref, qal_ref, ka_ref, xt_ref,
-    do_ref, del_ref, dqe_ref, dke_ref, dve_ref,
+    moves, core_ref, q_ref, k_ref, v_ref, do_ref, qal_ref, del_ref, ka_ref, dqe_ref, dke_ref, dve_ref, xt_ref, so_ref,
     mine_ref, other_ref, dq_ref, dk_ref, dv_ref,
-    g_ref, p_ref, s_ref, late_ref, kt_ref, dqt_ref,
+    p_ref, s_ref, late_ref, kt_ref, dqt_ref,
 ):
     core, chip = core_ref[0], core_ref[1]
-    for qb in range(BLOCKS):
-        rows = pl.ds(qb * ROWS, ROWS)
-        g_ref[rows, :] = dr1_ref[rows, :].astype(BF)
-    early = EARLY_PAIRS * LANES
-    for ref, source in ((dq_ref, dqe_ref), (dk_ref, dke_ref), (dv_ref, dve_ref)):
-        ref[:, :early] = source[:, :early]
+    moves.need(q_ref, k_ref, v_ref, do_ref, qal_ref, del_ref, ka_ref)
     attend_backward(
         q_ref, k_ref, v_ref, do_ref, qal_ref, del_ref, ka_ref, dq_ref, dk_ref, dv_ref, p_ref, s_ref, kt_ref, dqt_ref, True,
         (EARLY_PAIRS, PAIRS),
     )
-    put_square_tn(mine_ref, other_ref, core, 3, o_ref, g_ref[...], chip)
-    put_square(mine_ref, other_ref, core, 0, xt_ref, dq_ref[...], chip)
-    put_square(mine_ref, other_ref, core, 1, xt_ref, dk_ref[...], chip)
-    put_square(mine_ref, other_ref, core, 2, xt_ref, dv_ref[...], chip)
-    late_ref[...] = jnp.zeros_like(late_ref)
-    for qb in range(BLOCKS):
-        rows = pl.ds(qb * ROWS, ROWS)
-        dq = dq_ref[rows, :]
-        dv = dv_ref[rows, :]
-        late_ref[0:1, :] += col_sum(dq)
-        late_ref[1:2, :] += col_sum(dv)
+    for ref, source in ((dq_ref, dqe_ref), (dk_ref, dke_ref), (dv_ref, dve_ref)):
+        moves.need(source)
+        ref[:, EARLY] = source[:, EARLY]
+        moves.done(ref)
+    moves.need(xt_ref, so_ref)
+    mine_ref[3 ^ chip, :ROWS, :] = so_ref[0]
+    other_ref[3 ^ chip, :ROWS, :] = so_ref[1]
+    late_ref[0:1, :] = col_sum(dq_ref[...])
+    late_ref[1:2, :] = col_sum(dv_ref[...])
     for ref, half in ((mine_ref, core), (other_ref, 1 - core)):
         for xy in range(4):
             place = pl.multiple_of((2 * (xy % 2) + half) * LANES, LANES)
@@ -471,41 +546,67 @@
             after = lax.broadcasted_iota(jnp.int32, (16, LANES), 0) >= 4
             ref[xy ^ chip, ROWS:, :] = jnp.zeros((16, D), BF)
             ref[xy ^ chip, ROWS:, :LANES] = jnp.where(after, piece, 0.0).astype(BF)
+        moves.done(ref, 3 ^ chip)
+    for matrix, source in ((0, dq_ref), (1, dk_ref), (2, dv_ref)):
+        put_square(mine_ref, other_ref, core, matrix, xt_ref, source[...], chip)
+        moves.done(mine_ref, matrix ^ chip)
+        moves.done(other_ref, matrix ^ chip)
 
 
 def input_grads_kernel(
-    core_ref, parts, parts2, dr1_ref, dqs_ref, dks_ref, dvs_ref, dkc_ref, dvc_ref,
+    moves, core_ref, parts, parts2, dr1_ref, dqs_ref, dks_ref, dvs_ref, dkc_ref, dvc_ref,
     ig_ref, mg_ref,
-    w_ref, wc_ref, sems1, sems2,
+    w_ref, wc_ref,
 ):
-    copies = fetch(core_ref, parts, w_ref, sems1, FIRST_ROWS)
-    copies += fetch(core_ref, parts2, wc_ref, sems2)
-    wait_all(copies)
-    for qb in range(BLOCKS):
-        rows = pl.ds(qb * ROWS, ROWS)
+    fetch(moves, core_ref, parts, w_ref, FIRST_ROWS)
+    fetch(moves, core_ref, parts2, wc_ref)
+    moves.need(w_ref, dr1_ref, dqs_ref, dks_ref, dvs_ref)
+    for qb in range(TALLS):
+        rows = pl.ds(qb * TALL, TALL)
         total = dr1_ref[rows, :] + nt(dqs_ref[rows, :], square(w_ref, 0))
         total = total + nt(dks_ref[rows, :], square(w_ref, 1))
         ig_ref[rows, :] = (total + nt(dvs_ref[rows, :], square(w_ref, 2))).astype(BF)
+        moves.done(ig_ref, rows)
+    moves.need(wc_ref, dkc_ref, dvc_ref)
+    for qb in range(TALLS):
+        rows = pl.ds(qb * TALL, TALL)
         total = nt(dkc_ref[rows, :], square(wc_ref, 1))
         mg_ref[rows, :] = (total + nt(dvc_ref[rows, :], square(wc_ref, 2))).astype(BF)
-
-
-def call(kernel, outs, scratch, flops, core, parts, args, sems=1):
+        moves.done(mg_ref, rows)
+
+
+def call(kernel, outs, scratch, flops, core, parts, args, views=None):
+    views = views or {}
     sds = [jax.ShapeDtypeStruct(shape, dtype) for shape, dtype in outs]
     arrays = [block for group in parts for block in group]
     moved = sum(a.size * a.dtype.itemsize for a in arrays + list(args))
-    spaces = [pltpu.SMEM] + [pl.ANY] * len(arrays) + [pltpu.VMEM] * len(args)
-    memory = [pltpu.VMEM(shape, dtype) for shape, dtype in scratch]
-    memory += [pltpu.SemaphoreType.DMA((8,))] * sems
+    spaces = [pltpu.SMEM] + [pl.ANY] * (len(arrays) + len(args))
+    memory = [pltpu.VMEM(a.shape, a.dtype) for a in args]
+    memory += [pltpu.VMEM(shape, dtype) for shape, dtype in list(outs) + scratch]
+    memory += [pltpu.SemaphoreType.DMA((64,))]
 
     def body(core_ref, *refs):
         groups = [refs[6 * i : 6 * i + 6] for i in range(len(parts))]
-        kernel(core_ref, *groups, *refs[6 * len(parts) :])
+        refs = refs[6 * len(parts) :]
+        given, refs = refs[: len(args)], refs[len(args) :]
+        results, refs = refs[: len(outs)], refs[len(outs) :]
+        held, refs = refs[: len(args)], refs[len(args) :]
+        moves = Moves(refs[-1])
+        for i, (source, target) in enumerate(zip(given, held)):
+            if i in views:
+                moves.bring(source.at[views[i]], target.at[views[i]], target)
+            else:
+                moves.bring(source, target, target)
+        for place, result in zip(refs, results):
+            moves.pair(place, result)
+        kernel(moves, core_ref, *groups, *held, *refs[:-1])
+        moves.finish()
 
     return pl.pallas_call(
         body,
         out_shape=sds,
         in_specs=[pl.BlockSpec(memory_space=space) for space in spaces],
+        out_specs=[pl.BlockSpec(memory_space=pl.ANY)] * len(outs),
         scratch_shapes=memory,
         compiler_params=pltpu.CompilerParams(vmem_limit_bytes=VMEM_BYTES),
         cost_estimate=pl.CostEstimate(flops=flops, bytes_accessed=moved, transcendentals=0),
@@ -536,8 +637,8 @@
 def ffn(core, w, *args):
     outs = [TOKB, ((4, 2 * ROWS, D), BF), ((4, 2 * ROWS, D), BF), (TOK, F32), ((32, D), F32)]
     scratch = [(OCT, BF), (OCT, BF), ((LEN, FF), BF), ((LEN, FF), BF), TOKB, TOKB]
-    scratch += [((ROWS, FF), F32), ((2, ROWS, LEN), BF)]
-    return call(ffn_kernel, outs, scratch, 26 * unit, core, [w], args, 2)
+    scratch += [((TALL, FF), F32), ((2, ROWS, LEN), BF)]
+    return call(ffn_kernel, outs, scratch, 26 * unit, core, [w], args)
 
 
 def cross_backward(core, w, *args):
@@ -547,20 +648,21 @@
 
 
 def self_backward_start(core, w, *args):
-    outs = [TOKB, (STAT, BF), TOKB, TOKB, TOKB]
+    outs = [TOKB, (STAT, BF), TOKB, TOKB, TOKB, ((2, ROWS, D), BF)]
     scratch = [TOKB, PROBS, PROBS, (OCT, BF), TURN, TURN32]
     return call(self_backward_start_kernel, outs, scratch, 25 * unit, core, [w], args)
 
 
 def self_backward_end(core, *args):
     outs = [HALVES, HALVES, TOKB, TOKB, TOKB]
-    scratch = [TOKB, PROBS, PROBS, ((8, D), F32), TURN, TURN32]
-    return call(self_backward_end_kernel, outs, scratch, 12 * unit, core, [], args, 0)
+    scratch = [PROBS, PROBS, ((8, D), F32), TURN, TURN32]
+    views = {i: (EVERY, LATE) for i in (0, 1, 2, 3)} | {i: (EVERY, EARLY) for i in (7, 8, 9)}
+    return call(self_backward_end_kernel, outs, scratch, 12 * unit, core, [], args, views)
 
 
 def input_grads(core, ws, wc, *args):
     scratch = [(OCT, BF), (OCT, BF)]
-    return call(input_grads_kernel, [TOKB, TOKB], scratch, 6 * unit, core, [ws, wc], args, 2)
+    return call(input_grads_kernel, [TOKB, TOKB], scratch, 6 * unit, core, [ws, wc], args)
 
 
 SQUARES = 8 * D * D
@@ -692,13 +794,14 @@
     return part_c, part_1, part_2, along_z(jnp.where(z == 0, part_1, part_c), ((0, 1), (3, 2)))
 
 
-def finish_blocks(mine, other, blocks, index):
+def finish_blocks(mine, other, blocks, grads, index):
     z = index // 8
     got = swap(other, 1)
     pairs = [(mine[j].astype(F32) + got[j].astype(F32)).astype(BF) for j in range(4)]
     part_c, part_1, part_2, early = blocks
     part = pairs[0].astype(F32) + swap(pairs[1], 2).astype(F32) + swap(pairs[2], 4).astype(F32)
     part = part + swap(pairs[3], 6).astype(F32)
+    part, grads = lax.optimization_barrier((part, grads))
     part = (part + jnp.pad(part_c[ROWS:].astype(F32), ((ROWS, 0), (0, 0)))).astype(BF)
     left = jnp.where(z == 2, add(part_c, early), part)
     right = jnp.where(z == 1, add(part_1, early), part_2)
@@ -726,7 +829,7 @@
     square = jnp.sum(pieces[:, 5, 0]) + jnp.sum(vec * vec)
     after = jnp.where(index == 31, vec, after)
     share = lax.dynamic_slice(jnp.concatenate([flat, after]), (272 * index,), (ROWS * D + 272,))
-    return share, vec, square
+    return share, vec, square, grads
 
 
 def share_plain(pairs, index, share_len):
@@ -770,29 +873,31 @@
         wc, wide, n1 = lax.optimization_barrier((wc, wide, n1))
         wc = finish_block(*wc)
         across = to_corners(wide[1])
-    qc, kc, vc, oc, qal_c, n2, r2 = cross_forward(core, wc, n1, memory, vec, qa, ka_cross)
+    qc, kc, vc, oc, qal_c, n2, r2 = cross_forward(core, wc, n1, vec, memory, qa, ka_cross)
     if blocked:
         across, n2 = lax.optimization_barrier((across, n2))
         wide = finish_block(*wide, across)
-    out, mine_f, other_f, dr2, vg_f = ffn(core, wide, n2, r2, cotangent, vec)
+    out, mine_f, other_f, dr2, vg_f = ffn(core, wide, n2, vec, cotangent, r2)
     mine_c, other_c, dr1, dkc, dvc = cross_backward(
-        core, wc, dr2, vec, qc, kc, vc, oc, qal_c, ka_cross, n1, r1, memory_turn, vg_f
+        core, wc, dr2, oc, qc, kc, vc, qal_c, ka_cross, memory_turn, n1, vec, vg_f, r1
     )
     if blocked:
         part_f = plane_sum(mine_f, other_f)
         part_f, mine_c, other_c, dr1 = lax.optimization_barrier((part_f, mine_c, other_c, dr1))
         part_c = plane_sum(mine_c, other_c)
-    early = self_backward_start(core, ws, dr1, qs, ks, vs, os, qal_s, ka_self)
+    early = self_backward_start(core, ws, dr1, os, qs, ks, vs, qal_s, ka_self)
     if blocked:
         part_c, early = lax.optimization_barrier((part_c, early))
         blocks = first_round(part_c, part_f, index // 8)
     mine_s, other_s, dqs, dks, dvs = self_backward_end(
-        core, dr1, qs, ks, vs, os, qal_s, ka_self, targets_turn, *early
+        core, qs, ks, vs, early[0], qal_s, early[1], ka_self, *early[2:5], targets_turn, early[5]
     )
     input_grad, memory_grad = input_grads(core, ws, wc, dr1, dqs, dks, dvs, dkc, dvc)
     if blocked:
         blocks, mine_s, other_s = lax.optimization_barrier((blocks, mine_s, other_s))
-        grad, vec_total, square = finish_blocks(mine_s, other_s, blocks, index)
+        grads = (input_grad, memory_grad)
+        grad, vec_total, square, grads = finish_blocks(mine_s, other_s, blocks, grads, index)
+        input_grad, memory_grad = grads
     else:
         pairs = ((mine_s, other_s), (mine_c, other_c), (mine_f, other_f))
         grad, vec_total, square = share_plain(pairs, index, params.shape[0])

time: 288 us -> 278 us (0.965)
  Pallas kernels: 136 us -> 131 us
    ppermute x15, waiting for transfers between devices: 26.9 us -> 18.1 us  [swap(): return lax.ppermute(x, 'dp', [(i, i ^ bit) for i in range(32)])]
    all_to_all x1, waiting for transfers between devices: 0.01 us -> 6.75 us  [finish_blocks(): pieces = lax.all_to_all(pieces, 'dp', 0, 0, tiled=True)]
    pallas_call x7, Pallas kernels: 136 us -> 131 us  [call(): pl.pallas_call(body, out_shape=sds, in_specs=[pl.BlockSpec(memory_space=s...]
    unnamed x62 -> x60, local copies, waits for them, and re-layouts: 6.24 us -> 5.57 us
where the time goes in v2:
time: 278 us; the launch traced here: 275 us
  Pallas kernels  131 us (47%)
  waiting for transfers between devices  67 us (24%)
  starting transfers between devices  44.4 us (16%)
  other arithmetic  19.1 us (7%)
  local copies, waits for them, and re-layouts  9.26 us (3%)
  between operations  4.16 us (1%)
    pallas_call x7, Pallas kernels, call(): pl.pallas_call(body, out_shape=sds, in_specs=[pl.BlockSpec(memory_space=s...  131 us
    ppermute x8, waiting for transfers between devices, along_z(): lax.ppermute(x, 'dp', [(8 * a + p, 8 * b + p) for a, b in moves for p in...  26.1 us
    ppermute x15, waiting for transfers between devices, swap(): return lax.ppermute(x, 'dp', [(i, i ^ bit) for i in range(32)])  18.1 us
    ppermute x8, starting transfers between devices, along_z(): lax.ppermute(x, 'dp', [(8 * a + p, 8 * b + p) for a, b in moves for p in...  17.8 us
    ppermute x15, starting transfers between devices, swap(): return lax.ppermute(x, 'dp', [(i, i ^ bit) for i in range(32)])  8 us
    all_to_all x2, starting transfers between devices, plane_sum(): lax.all_to_all(pair, 'dp', 0, 0, tiled=True, axis_index_groups=groups_xy())  7.75 us
    ppermute x1, waiting for transfers between devices, gather_blocks(): lax.ppermute(low[share - VEC_LEN:], 'dp', [(i, (i + 1) % 32) for i in ran...  7.35 us
    all_to_all x1, waiting for transfers between devices, finish_blocks(): pieces = lax.all_to_all(pieces, 'dp', 0, 0, tiled=True)  6.75 us
  transfers between devices with their start and end apart: 34, of which 18 were waited for; matrix products, arithmetic and copies ran while one was open for 3% of the time, Pallas kernels for 39%

profile of v2, /device:TPU:0, one launch (start us, length us, event | category | flops | bytes accessed | tf_op | source)
XLA Modules:
  0.0 275.1 jit_solution(4103834874108486544)
XLA Ops:
  2.4 7.4 %collective-permute-done = bf16[8704]{0:T(1024)(128)(2,1)S(1)} collective-permute-done((bf16[8704]{0:T(1024)(128)(2,1)S(1)}, bf16[8704]{0:T(1024)(128)(2,1)S(1)}, u32[]{:S(2)}, u32[]{:S(2)}) %collective-permute-start) | collective-permute-done | bytes 17440 | tf_op jit(solution)/shard_map/ppermute | solution.py:702
  17.3 3.0 %collective-permute-start.2 = (bf16[288,512]{1,0:T(8,128)(2,1)S(1)}, bf16[288,512]{1,0:T(8,128)(2,1)S(1)}, u32[]{:S(2)}, u32[]{:S(2)}) collective-permute-start(bf16[288,512]{1,0:T(8,128)(2,1)S(1)} %broadcast_select_fusion), channel_id=1, source_target_pairs={{0,8},{1,9},{2,10},{3,11},{4,12},{5,13},{6,14},{7,15},{8,16},{9,17... | collective-permute-start | bytes 884744 | tf_op jit(solution)/shard_map/ppermute | solution.py:694
  21.7 7.0 %collective-permute-done.3 = bf16[256,512]{1,0:T(8,128)(2,1)S(1)} collective-permute-done((bf16[256,512]{1,0:T(8,128)(2,1)S(1)}, bf16[256,512]{1,0:T(8,128)(2,1)S(1)}, u32[]{:S(2)}, u32[]{:S(2)}) %collective-permute-start.3) | collective-permute-done | bytes 262176 | tf_op jit(solution)/shard_map/ppermute | solution.py:694
  28.9 1.5 collective-permute-done.4.refs_1_
  33.3 8.5 %collective-permute-done.6 = bf16[256,512]{1,0:T(8,128)(2,1)S(1)} collective-permute-done((bf16[256,512]{1,0:T(8,128)(2,1)S(1)}, bf16[256,512]{1,0:T(8,128)(2,1)S(1)}, u32[]{:S(2)}, u32[]{:S(2)}) %collective-permute-start.6) | collective-permute-done | bytes 262176 | tf_op jit(solution)/shard_map/ppermute | solution.py:694
  45.9 6.0 %collective-permute-done.8.refs_4_ = bf16[288,512]{1,0:T(8,128)(2,1)S(1)} collective-permute-done((bf16[288,512]{1,0:T(8,128)(2,1)S(1)}, bf16[288,512]{1,0:T(8,128)(2,1)S(1)}, u32[]{:S(2)}, u32[]{:S(2)}) %collective-permute-start.8) | collective-permute-done | bytes 294944 | tf_op jit(solution)/shard_map/ppermute | solution.py:749
  51.9 2.7 collective-permute-done.9.refs_2_.refs_8_
  57.3 15.6 %shard_map.159 = (bf16[1024,512]{1,0:T(8,128)(2,1)}, bf16[1024,512]{1,0:T(8,128)(2,1)}, bf16[1024,512]{1,0:T(8,128)(2,1)}, bf16[1024,512]{1,0:T(8,128)(2,1)}, bf...) custom-call(s32[2]{0:T(128)} %pad_add_fusion.core_ref, bf16[288,512]{1,0:T(8,128)(2,1)} %copy-done.1, ...), custom_call_target="tpu_custom_call" | custom-call | flops 10737418240 | bytes 3997696 | tf_op jit(solution)/shard_map/pallas_call | solution.py:605
  77.6 20.1 %shard_map.160 = (bf16[1024,512]{1,0:T(8,128)(2,1)}, bf16[1024,512]{1,0:T(8,128)(2,1)}, bf16[1024,512]{1,0:T(8,128)(2,1)}, bf16[1024,512]{1,0:T(8,128)(2,1)}, bf...) custom-call(s32[2]{0:T(128)} %pad_add_fusion.core_ref, bf16[256,512]{1,0:T(8,128)(2,1)} %copy-done.4, ...), custom_call_target="tpu_custom_call" | custom-call | flops 13421772800 | bytes 5832704 | tf_op jit(solution)/shard_map/pallas_call | solution.py:605
  101.0 23.3 %shard_map.161 = (bf16[1024,512]{1,0:T(8,128)(2,1)}, bf16[4,512,512]{2,1,0:T(8,128)(2,1)}, bf16[4,512,512]{2,1,0:T(8,128)(2,1)}, f32[1024,512]{1,0:T(8,128)}, f32[32,512]{1,0:T(8,128)}) custom-call(s32[2]{0:T(128)} %pad_add_fusion.core_ref, bf16[512,512]{1,0:T(8,128)(2,1)} %copy-done.7, bf16[512,512]{1,0:T(8,128)(2,1)} %copy-done.8, ...), custom_call_target="tpu_custom_call" | custom-call | flops 13958643712 | bytes 7929856 | tf_op jit(solution)/shard_map/pallas_call | solution.py:605
  124.8 4.0 %collective-permute-done.20 = bf16[4,512,512]{2,1,0:T(8,128)(2,1)S(1)} collective-permute-done((bf16[4,512,512]{2,1,0:T(8,128)(2,1)}, bf16[4,512,512]{2,1,0:T(8,128)(2,1)S(1)}, u32[]{:S(2)}, u32[]{:S(2)}) %collective-permute-start.20) | collective-permute-done | bytes 2097184 | tf_op jit(solution)/shard_map/ppermute | solution.py:682
  128.8 3.5 %add_convert_fusion = bf16[4,512,512]{2,1,0:T(8,128)(2,1)} fusion(bf16[4,512,512]{2,1,0:T(8,128)(2,1)S(1)} %collective-permute-done.20, bf16[4,512,512]{2,1,0:T(8,128)(2,1)} %get-tuple-element.115), kind=kLoop, calls=%fused_computation | loop fusion | flops 4194304 | bytes 6291456 | tf_op jit(solution)/shard_map/convert_element_type | solution.py:781
  132.3 3.6 %all-to-all-start = ((bf16[4,512,512]{2,1,0:T(8,128)(2,1)}), bf16[4,512,512]{2,1,0:T(8,128)(2,1)S(1)}, u32[]{:S(2)}, u32[]{:S(2)}) async-start(bf16[4,512,512]{2,1,0:T(8,128)(2,1)} %add_convert_fusion), calls=%async_computation | async-start | bytes 4194304 | tf_op jit(solution)/shard_map/all_to_all | solution.py:782
  135.9 34.6 %shard_map.162 = (bf16[4,272,512]{2,1,0:T(8,128)(2,1)}, bf16[4,272,512]{2,1,0:T(8,128)(2,1)}, f32[1024,512]{1,0:T(8,128)}, bf16[1024,512]{1,0:T(8,128)(2,1)}, bf16[1024,512]{1,0:T(8,128)(2,1)}) custom-call(s32[2]{0:T(128)} %pad_add_fusion.core_ref, bf16[256,512]{1,0:T(8,128)(2,1)} %copy-done.4, bf16[256,512]{1,0:T(8,128)(2,1)} %copy-done.10, ...), custom_call_target="tpu_custom_call" | custom-call | flops 26843545600 | bytes 12713984 | tf_op jit(solution)/shard_map/pallas_call | solution.py:605
  171.6 2.6 collective-permute-done.21
  174.2 2.6 add_convert_fusion.1
  176.8 4.1 %all-to-all-start.1 = ((bf16[4,272,512]{2,1,0:T(8,128)(2,1)}), bf16[4,272,512]{2,1,0:T(8,128)(2,1)S(1)}, u32[]{:S(2)}, u32[]{:S(2)}) async-start(bf16[4,272,512]{2,1,0:T(8,128)(2,1)} %add_convert_fusion.1), calls=%async_computation.1 | async-start | bytes 2228224 | tf_op jit(solution)/shard_map/all_to_all | solution.py:782
  180.9 19.5 %shard_map.163 = (bf16[1024,512]{1,0:T(8,128)(2,1)}, bf16[1024,128]{1,0:T(8,128)(2,1)}, bf16[1024,512]{1,0:T(8,128)(2,1)}, bf16[1024,512]{1,0:T(8,128)(2,1)}, bf...) custom-call(s32[2]{0:T(128)} %pad_add_fusion.core_ref, bf16[288,512]{1,0:T(8,128)(2,1)} %copy-done.1, ...), custom_call_target="tpu_custom_call" | custom-call | flops 13421772800 | bytes 9175040 | tf_op jit(solution)/shard_map/pallas_call | solution.py:605
  200.8 2.4 collective-permute-start.22
  203.2 9.3 %shard_map.164 = (bf16[4,272,512]{2,1,0:T(8,128)(2,1)}, bf16[4,272,512]{2,1,0:T(8,128)(2,1)}, bf16[1024,512]{1,0:T(8,128)(2,1)}, bf16[1024,512]{1,0:T(8,128)(2,1)}, bf16[1024,512]{1,0:T(8,128)(2,1)}) custom-call(s32[2]{0:T(128)} %pad_add_fusion.core_ref, bf16[1024,512]{1,0:T(8,128)(2,1)} %get-tuple-element.133.refs_8_.refs_0_, ...), custom_call_target="tpu_custom_call" | custom-call | flops 6442450944 | bytes 9699328 | tf_op jit(solution)/shard_map/pallas_call | solution.py:605
  212.6 3.0 %collective-permute-done.23 = bf16[4,272,512]{2,1,0:T(8,128)(2,1)S(1)} collective-permute-done((bf16[4,272,512]{2,1,0:T(8,128)(2,1)}, bf16[4,272,512]{2,1,0:T(8,128)(2,1)S(1)}, u32[]{:S(2)}, u32[]{:S(2)}) %collective-permute-start.23) | collective-permute-done | bytes 1114144 | tf_op jit(solution)/shard_map/ppermute | solution.py:682
  216.9 2.1 collective-permute-start.24
  220.6 8.8 %shard_map.165 = (bf16[1024,512]{1,0:T(8,128)(2,1)}, bf16[1024,512]{1,0:T(8,128)(2,1)}) custom-call(s32[2]{0:T(128)} %pad_add_fusion.core_ref, bf16[288,512]{1,0:T(8,128)(2,1)} %copy-done.1, bf16[288,512]{1,0:T(8,128)(2,1)} %copy-done.9, bf16[576,512]{1,0:T(8,128)(2,1)} %copy-done.11, bf16[576,512]{1,0:T(8,128)(2,1)} %copy-done.14, ...), custom_call_target="tpu_custom_call" | custom-call | flops 3221225472 | bytes 11796480 | tf_op jit(solution)/shard_map/pallas_call | solution.py:605
  229.4 3.9 %collective-permute-done.26 = bf16[272,512]{1,0:T(8,128)(2,1)S(1)} collective-permute-done((bf16[272,512]{1,0:T(8,128)(2,1)S(1)}, bf16[272,512]{1,0:T(8,128)(2,1)S(1)}, u32[]{:S(2)}, u32[]{:S(2)}) %collective-permute-start.26) | collective-permute-done | bytes 278560 | tf_op jit(solution)/shard_map/ppermute | solution.py:682
  237.2 4.6 %collective-permute-start.28 = (bf16[272,512]{1,0:T(8,128)(2,1)S(1)}, bf16[272,512]{1,0:T(8,128)(2,1)S(1)}, u32[]{:S(2)}, u32[]{:S(2)}) collective-permute-start(bf16[272,512]{1,0:T(8,128)(2,1)S(1)} %get-tuple-element.189), channel_id=1, source_target_pairs={{0,8},{1,9},{2,10},{3,11},{4,12},{5,13},{6,14},{7,15},{8,16},{9,17... | collective-permute-start | bytes 835592 | tf_op jit(solution)/shard_map/ppermute | solution.py:694
  241.8 2.6 collective-permute-done.27
  244.4 2.1 collective-permute-done.28
  246.7 2.5 collective-permute-start.29
  249.2 5.0 %collective-permute-done.29 = bf16[272,512]{1,0:T(8,128)(2,1)S(1)} collective-permute-done((bf16[272,512]{1,0:T(8,128)(2,1)S(1)}, bf16[272,512]{1,0:T(8,128)(2,1)S(1)}, u32[]{:S(2)}, u32[]{:S(2)}) %collective-permute-start.29) | collective-permute-done | bytes 278560 | tf_op jit(solution)/shard_map/ppermute | solution.py:694
  257.3 3.2 %all-to-all-start.2 = ((f32[32,8,128]{2,1,0:T(8,128)}), f32[32,8,128]{2,1,0:T(8,128)S(1)}, u32[]{:S(2)}, u32[]{:S(2)}) async-start(f32[32,8,128]{2,1,0:T(8,128)} %broadcast_in_dim.30), calls=%async_computation.2 | async-start | bytes 262144 | tf_op jit(solution)/shard_map/all_to_all | solution.py:825
  262.0 6.8 %all-to-all-done.2 = f32[32,8,128]{2,1,0:T(8,128)S(1)} async-done(((f32[32,8,128]{2,1,0:T(8,128)}), f32[32,8,128]{2,1,0:T(8,128)S(1)}, u32[]{:S(2)}, u32[]{:S(2)}) %all-to-all-start.2) | async-done | bytes 131104 | tf_op jit(solution)/shard_map/all_to_all | solution.py:825
  271.6 2.1 fusion.25
  (167 shorter events, 43.3 us)
Async XLA Ops:
  1.9 7.8 %collective-permute-start = (bf16[8704]{0:T(1024)(128)(2,1)S(1)}, bf16[8704]{0:T(1024)(128)(2,1)S(1)}, u32[]{:S(2)}, u32[]{:S(2)}) collective-permute-start(bf16[8704]{0:T(1024)(128)(2,1)S(1)} %slice.145), channel_id=1, source_target_pairs={{0,1},{1,2},{2,3},{3,4},{4,5},{5,6},{6,7},{7,8},{8,9},{9,10},{10,1... | collective-permute-start | bytes 52232 | tf_op jit(solution)/shard_map/ppermute | solution.py:702
  10.5 6.8 %collective-permute-start.1 = (bf16[288,512]{1,0:T(8,128)(2,1)S(1)}, bf16[288,512]{1,0:T(8,128)(2,1)S(1)}, u32[]{:S(2)}, u32[]{:S(2)}) collective-permute-start(bf16[288,512]{1,0:T(8,128)(2,1)S(1)} %fusion.9), channel_id=1, source_target_pairs={{0,16},{1,17},{2,18},{3,19},{4,20},{5,21},{6,22},{7,23},{8,0},{9,1... | collective-permute-start | bytes 884744 | tf_op jit(solution)/shard_map/ppermute | solution.py:694
  17.3 11.3 %collective-permute-start.2 = (bf16[288,512]{1,0:T(8,128)(2,1)S(1)}, bf16[288,512]{1,0:T(8,128)(2,1)S(1)}, u32[]{:S(2)}, u32[]{:S(2)}) collective-permute-start(bf16[288,512]{1,0:T(8,128)(2,1)S(1)} %broadcast_select_fusion), channel_id=1, source_target_pairs={{0,8},{1,9},{2,10},{3,11},{4,12},{5,13},{6,14},{7,15},{8,16},{9,17... | collective-permute-start | bytes 884744 | tf_op jit(solution)/shard_map/ppermute | solution.py:694
  20.4 8.3 %collective-permute-start.3 = (bf16[256,512]{1,0:T(8,128)(2,1)S(1)}, bf16[256,512]{1,0:T(8,128)(2,1)S(1)}, u32[]{:S(2)}, u32[]{:S(2)}) collective-permute-start(bf16[256,512]{1,0:T(8,128)(2,1)S(1)} %slice_select_fusion), channel_id=1, source_target_pairs={{24,16},{25,17},{26,18},{27,19},{28,20},{29,21},{30,22},{31,23},{1... | collective-permute-start | bytes 786440 | tf_op jit(solution)/shard_map/ppermute | solution.py:694
  30.5 11.3 %collective-permute-start.5 = (bf16[576,512]{1,0:T(8,128)(2,1)S(1)}, bf16[576,512]{1,0:T(8,128)(2,1)S(1)}, u32[]{:S(2)}, u32[]{:S(2)}) collective-permute-start(bf16[576,512]{1,0:T(8,128)(2,1)S(1)} %pad_maximum_fusion.1), channel_id=1, source_target_pairs={{0,2},{1,5},{2,0},{3,7},{4,6},{5,1},{6,4},{7,3},{8,10},{9,13},{10,... | collective-permute-start | bytes 1769480 | tf_op jit(solution)/shard_map/ppermute | solution.py:745
  31.8 10.0 %collective-permute-start.6 = (bf16[256,512]{1,0:T(8,128)(2,1)S(1)}, bf16[256,512]{1,0:T(8,128)(2,1)S(1)}, u32[]{:S(2)}, u32[]{:S(2)}) collective-permute-start(bf16[256,512]{1,0:T(8,128)(2,1)S(1)} %broadcast_select_fusion.2), channel_id=1, source_target_pairs={{8,0},{9,1},{10,2},{11,3},{12,4},{13,5},{14,6},{15,7},{16,24},{17,... | collective-permute-start | bytes 786440 | tf_op jit(solution)/shard_map/ppermute | solution.py:694
  42.0 3.1 %collective-permute-start.11 = (bf16[512,512]{1,0:T(8,128)(2,1)S(1)}, bf16[512,512]{1,0:T(8,128)(2,1)S(1)}, u32[]{:S(2)}, u32[]{:S(2)}) collective-permute-start(bf16[512,512]{1,0:T(8,128)(2,1)S(1)} %pad_maximum_fusion.3.refs_0_), channel_id=1, source_target_pairs={{0,1},{1,0},{2,3},{3,2},{4,5},{5,4},{6,7},{7,6},{8,9},{9,8},{10,11... | collective-permute-start | bytes 1572872 | tf_op jit(solution)/shard_map/ppermute | solution.py:682
  42.6 3.3 %collective-permute-start.13 = (bf16[576,512]{1,0:T(8,128)(2,1)S(1)}, bf16[576,512]{1,0:T(8,128)(2,1)S(1)}, u32[]{:S(2)}, u32[]{:S(2)}) collective-permute-start(bf16[576,512]{1,0:T(8,128)(2,1)S(1)} %collective-permute-done.5.refs_2_), channel_id=1, source_target_pairs={{0,1},{1,0},{2,3},{3,2},{4,5},{5,4},{6,7},{7,6},{8,9},{9,8},{10,11... | collective-permute-start | bytes 1769480 | tf_op jit(solution)/shard_map/ppermute | solution.py:682
  42.7 9.2 %collective-permute-start.8 = (bf16[288,512]{1,0:T(8,128)(2,1)S(1)}, bf16[288,512]{1,0:T(8,128)(2,1)S(1)}, u32[]{:S(2)}, u32[]{:S(2)}) collective-permute-start(bf16[288,512]{1,0:T(8,128)(2,1)S(1)} %slice.113), channel_id=1, source_target_pairs={{0,4},{1,3},{2,6},{3,1},{4,0},{5,7},{6,2},{7,5},{8,12},{9,11},{10,... | collective-permute-start | bytes 884744 | tf_op jit(solution)/shard_map/ppermute | solution.py:749
  43.6 11.0 %collective-permute-start.9 = (bf16[512,512]{1,0:T(8,128)(2,1)S(1)}, bf16[512,512]{1,0:T(8,128)(2,1)S(1)}, u32[]{:S(2)}, u32[]{:S(2)}) collective-permute-start(bf16[512,512]{1,0:T(8,128)(2,1)S(1)} %pad_maximum_fusion.2), channel_id=1, source_target_pairs={{0,2},{1,5},{2,0},{3,7},{4,6},{5,1},{6,4},{7,3},{8,10},{9,13},{10,... | collective-permute-start | bytes 1572872 | tf_op jit(solution)/shard_map/ppermute | solution.py:745
  45.2 27.7 %collective-permute-start.12 = (bf16[1024,512]{1,0:T(8,128)(2,1)S(1)}, bf16[1024,512]{1,0:T(8,128)(2,1)}, u32[]{:S(2)}, u32[]{:S(2)}) collective-permute-start(bf16[1024,512]{1,0:T(8,128)(2,1)S(1)} %pad_maximum_fusion), channel_id=1, source_target_pairs={{0,2},{1,5},{2,0},{3,7},{4,6},{5,1},{6,4},{7,3},{8,10},{9,13},{10,... | collective-permute-start | bytes 3145736 | tf_op jit(solution)/shard_map/ppermute | solution.py:745
  54.6 2.0 collective-permute-start.14
  55.4 17.5 %collective-permute-start.10 = (bf16[256,512]{1,0:T(8,128)(2,1)S(1)}, bf16[256,512]{1,0:T(8,128)(2,1)S(1)}, u32[]{:S(2)}, u32[]{:S(2)}) collective-permute-start(bf16[256,512]{1,0:T(8,128)(2,1)S(1)} %slice.114), channel_id=1, source_target_pairs={{0,4},{1,3},{2,6},{3,1},{4,0},{5,7},{6,2},{7,5},{8,12},{9,11},{10,... | collective-permute-start | bytes 786440 | tf_op jit(solution)/shard_map/ppermute | solution.py:749
  72.9 3.1 %collective-permute-start.17 = (bf16[512,512]{1,0:T(8,128)(2,1)S(1)}, bf16[512,512]{1,0:T(8,128)(2,1)S(1)}, u32[]{:S(2)}, u32[]{:S(2)}) collective-permute-start(bf16[512,512]{1,0:T(8,128)(2,1)S(1)} %collective-permute-done.9.refs_2_.refs_8_), channel_id=1, source_target_pairs={{0,1},{1,0},{2,3},{3,2},{4,5},{5,4},{6,7},{7,6},{8,9},{9,8},{10,11... | collective-permute-start | bytes 1572872 | tf_op jit(solution)/shard_map/ppermute | solution.py:682
  73.6 2.5 collective-permute-start.18
  74.8 25.0 %collective-permute-start.15 = (bf16[1024,512]{1,0:T(8,128)(2,1)}, bf16[1024,512]{1,0:T(8,128)(2,1)S(1)}, u32[]{:S(2)}, u32[]{:S(2)}) collective-permute-start(bf16[1024,512]{1,0:T(8,128)(2,1)} %collective-permute-done.12.refs_2_), channel_id=1, source_target_pairs={{0,1},{1,0},{2,3},{3,2},{4,5},{5,4},{6,7},{7,6},{8,9},{9,8},{10,11... | collective-permute-start | bytes 3145736 | tf_op jit(solution)/shard_map/ppermute | solution.py:682
  75.2 22.4 %collective-permute-start.16 = (bf16[512,512]{1,0:T(8,128)(2,1)S(1)}, bf16[512,512]{1,0:T(8,128)(2,1)S(1)}, u32[]{:S(2)}, u32[]{:S(2)}) collective-permute-start(bf16[512,512]{1,0:T(8,128)(2,1)S(1)} %slice.123), channel_id=1, source_target_pairs={{0,4},{1,3},{2,6},{3,1},{4,0},{5,7},{6,2},{7,5},{8,12},{9,11},{10,... | collective-permute-start | bytes 1572872 | tf_op jit(solution)/shard_map/ppermute | solution.py:749
  97.7 2.1 collective-permute-start.19
  124.3 4.5 %collective-permute-start.20 = (bf16[4,512,512]{2,1,0:T(8,128)(2,1)}, bf16[4,512,512]{2,1,0:T(8,128)(2,1)S(1)}, u32[]{:S(2)}, u32[]{:S(2)}) collective-permute-start(bf16[4,512,512]{2,1,0:T(8,128)(2,1)} %get-tuple-element.116), channel_id=1, source_target_pairs={{0,1},{1,0},{2,3},{3,2},{4,5},{5,4},{6,7},{7,6},{8,9},{9,8},{10,11... | collective-permute-start | bytes 6291464 | tf_op jit(solution)/shard_map/ppermute | solution.py:682
  132.3 38.2 %all-to-all-start = ((bf16[4,512,512]{2,1,0:T(8,128)(2,1)}), bf16[4,512,512]{2,1,0:T(8,128)(2,1)S(1)}, u32[]{:S(2)}, u32[]{:S(2)}) async-start(bf16[4,512,512]{2,1,0:T(8,128)(2,1)} %add_convert_fusion), calls=%async_computation | async-start | bytes 4194304 | tf_op jit(solution)/shard_map/all_to_all | solution.py:782
  171.1 3.0 %collective-permute-start.21 = (bf16[4,272,512]{2,1,0:T(8,128)(2,1)}, bf16[4,272,512]{2,1,0:T(8,128)(2,1)S(1)}, u32[]{:S(2)}, u32[]{:S(2)}) collective-permute-start(bf16[4,272,512]{2,1,0:T(8,128)(2,1)} %get-tuple-element.130), channel_id=1, source_target_pairs={{0,1},{1,0},{2,3},{3,2},{4,5},{5,4},{6,7},{7,6},{8,9},{9,8},{10,11... | collective-permute-start | bytes 3342344 | tf_op jit(solution)/shard_map/ppermute | solution.py:682
  176.8 23.6 %all-to-all-start.1 = ((bf16[4,272,512]{2,1,0:T(8,128)(2,1)}), bf16[4,272,512]{2,1,0:T(8,128)(2,1)S(1)}, u32[]{:S(2)}, u32[]{:S(2)}) async-start(bf16[4,272,512]{2,1,0:T(8,128)(2,1)} %add_convert_fusion.1), calls=%async_computation.1 | async-start | bytes 2228224 | tf_op jit(solution)/shard_map/all_to_all | solution.py:782
  200.8 11.7 %collective-permute-start.22 = (bf16[272,512]{1,0:T(8,128)(2,1)S(1)}, bf16[272,512]{1,0:T(8,128)(2,1)S(1)}, u32[]{:S(2)}, u32[]{:S(2)}) collective-permute-start(bf16[272,512]{1,0:T(8,128)(2,1)S(1)} %get-tuple-element.190), channel_id=1, source_target_pairs={{0,8},{1,9},{2,10},{3,11},{4,12},{5,13},{6,14},{7,15},{24,16},{25,... | collective-permute-start | bytes 835592 | tf_op jit(solution)/shard_map/ppermute | solution.py:694
  212.5 3.0 %collective-permute-start.23 = (bf16[4,272,512]{2,1,0:T(8,128)(2,1)}, bf16[4,272,512]{2,1,0:T(8,128)(2,1)S(1)}, u32[]{:S(2)}, u32[]{:S(2)}) collective-permute-start(bf16[4,272,512]{2,1,0:T(8,128)(2,1)} %get-tuple-element.155), channel_id=1, source_target_pairs={{0,1},{1,0},{2,3},{3,2},{4,5},{5,4},{6,7},{7,6},{8,9},{9,8},{10,11... | collective-permute-start | bytes 3342344 | tf_op jit(solution)/shard_map/ppermute | solution.py:682
  216.9 12.5 %collective-permute-start.24 = (bf16[272,512]{1,0:T(8,128)(2,1)S(1)}, bf16[272,512]{1,0:T(8,128)(2,1)S(1)}, u32[]{:S(2)}, u32[]{:S(2)}) collective-permute-start(bf16[272,512]{1,0:T(8,128)(2,1)S(1)} %get-tuple-element.179), channel_id=1, source_target_pairs={{0,2},{1,3},{2,0},{3,1},{4,6},{5,7},{6,4},{7,5},{8,10},{9,11},{10,... | collective-permute-start | bytes 835592 | tf_op jit(solution)/shard_map/ppermute | solution.py:682
  219.0 14.2 %collective-permute-start.26 = (bf16[272,512]{1,0:T(8,128)(2,1)S(1)}, bf16[272,512]{1,0:T(8,128)(2,1)S(1)}, u32[]{:S(2)}, u32[]{:S(2)}) collective-permute-start(bf16[272,512]{1,0:T(8,128)(2,1)S(1)} %get-tuple-element.180), channel_id=1, source_target_pairs={{0,6},{1,7},{2,4},{3,5},{4,2},{5,3},{6,0},{7,1},{8,14},{9,15},{10,... | collective-permute-start | bytes 835592 | tf_op jit(solution)/shard_map/ppermute | solution.py:682
  220.5 14.1 %collective-permute-start.25 = (bf16[272,512]{1,0:T(8,128)(2,1)S(1)}, bf16[272,512]{1,0:T(8,128)(2,1)S(1)}, u32[]{:S(2)}, u32[]{:S(2)}) collective-permute-start(bf16[272,512]{1,0:T(8,128)(2,1)S(1)} %get-tuple-element.181), channel_id=1, source_target_pairs={{0,4},{1,5},{2,6},{3,7},{4,0},{5,1},{6,2},{7,3},{8,12},{9,13},{10,... | collective-permute-start | bytes 835592 | tf_op jit(solution)/shard_map/ppermute | solution.py:682
  235.9 8.4 %collective-permute-start.27 = (bf16[272,512]{1,0:T(8,128)(2,1)S(1)}, bf16[272,512]{1,0:T(8,128)(2,1)S(1)}, u32[]{:S(2)}, u32[]{:S(2)}) collective-permute-start(bf16[272,512]{1,0:T(8,128)(2,1)S(1)} %get-tuple-element.177), channel_id=1, source_target_pairs={{8,0},{9,1},{10,2},{11,3},{12,4},{13,5},{14,6},{15,7},{16,8},{17,9... | collective-permute-start | bytes 835592 | tf_op jit(solution)/shard_map/ppermute | solution.py:694
  237.2 9.2 %collective-permute-start.28 = (bf16[272,512]{1,0:T(8,128)(2,1)S(1)}, bf16[272,512]{1,0:T(8,128)(2,1)S(1)}, u32[]{:S(2)}, u32[]{:S(2)}) collective-permute-start(bf16[272,512]{1,0:T(8,128)(2,1)S(1)} %get-tuple-element.189), channel_id=1, source_target_pairs={{0,8},{1,9},{2,10},{3,11},{4,12},{5,13},{6,14},{7,15},{8,16},{9,17... | collective-permute-start | bytes 835592 | tf_op jit(solution)/shard_map/ppermute | solution.py:694
  246.7 7.5 %collective-permute-start.29 = (bf16[272,512]{1,0:T(8,128)(2,1)S(1)}, bf16[272,512]{1,0:T(8,128)(2,1)S(1)}, u32[]{:S(2)}, u32[]{:S(2)}) collective-permute-start(bf16[272,512]{1,0:T(8,128)(2,1)S(1)} %fusion.15), channel_id=1, source_target_pairs={{16,0},{17,1},{18,2},{19,3},{20,4},{21,5},{22,6},{23,7},{0,8},{1,9... | collective-permute-start | bytes 835592 | tf_op jit(solution)/shard_map/ppermute | solution.py:694
  257.3 11.4 %all-to-all-start.2 = ((f32[32,8,128]{2,1,0:T(8,128)}), f32[32,8,128]{2,1,0:T(8,128)S(1)}, u32[]{:S(2)}, u32[]{:S(2)}) async-start(f32[32,8,128]{2,1,0:T(8,128)} %broadcast_in_dim.30), calls=%async_computation.2 | async-start | bytes 262144 | tf_op jit(solution)/shard_map/all_to_all | solution.py:825
  260.5 11.0 %collective-permute-start.30 = (f32[8704]{0:T(1024)S(1)}, f32[8704]{0:T(1024)S(1)}, u32[]{:S(2)}, u32[]{:S(2)}) collective-permute-start(f32[8704]{0:T(1024)S(1)} %slice.144), channel_id=1, source_target_pairs={{1,0},{2,1},{3,2},{4,3},{5,4},{6,5},{7,6},{8,7},{9,8},{10,9},{11,1... | collective-permute-start | bytes 104456 | tf_op jit(solution)/shard_map/ppermute | solution.py:816
  (27 other events, 220.4 us)

commit v3 on v2

--- a/solution.py
+++ b/solution.py
@@ -32,6 +32,7 @@
 log2_e = 1.4426950408889634
 query_scale = 0.125 * log2_e
 key_scale = 1.0 / log2_e
+safe_least, safe_most = 2.0**-40, 2.0**40
 
 BF = jnp.bfloat16
 F32 = jnp.float32
@@ -86,8 +87,7 @@
 
 def attend_forward(moves, q_ref, k_ref, v_ref, qa_ref, ka_ref, o_ref, qal_ref, kt_ref, kat_ref, causal):
     size, depth = (ROWS, 2) if causal else (2 * ROWS, 1)
-    lane = lax.broadcasted_iota(jnp.int32, (size, LANES), 1)
-    low = lane < 64
+    low = lax.broadcasted_iota(jnp.int32, (size, LANES), 1) < 64
     bias = causal_bias(False) if causal else None
     kt_ref[...] = k_ref[...].T
     kat_ref[...] = ka_ref[...].T
@@ -104,21 +104,27 @@
             scores = jnp.concatenate([scores[:, : keys - size], diag], axis=1) if block else diag
         return scores
 
-    def finish(head, scores, lse_parts):
+    def parts_of(lse, head, lse_parts):
+        place = lax.broadcasted_iota(jnp.int32, lse.shape, 1)
+        first = lse.astype(BF).astype(F32)
+        rest = lse - first
+        second = rest.astype(BF).astype(F32)
+        for i, part in enumerate((first, second, rest - second)):
+            lse_parts = jnp.where(place == head * 3 + i, part, lse_parts)
+        return lse_parts
+
+    def finish(head, scores, lse_parts, least, most):
         half = half_row(head % 2)
-        top = jnp.max(scores, axis=1, keepdims=True)
-        probs = jnp.exp2(scores - top).astype(BF)
+        probs = jnp.exp2(scores).astype(BF)
         values = v_ref[: scores.shape[1], pl.ds(head // 2 * LANES, LANES)]
         mixed = nn(probs, values * half + (1.0 - half).astype(BF))
         turned = pltpu.roll(mixed, 64, 1)
-        lse = -(top + jnp.log2(turned if head % 2 == 0 else mixed))
-        first = lse.astype(BF).astype(F32)
-        rest = lse - first
-        second = rest.astype(BF).astype(F32)
-        for place, part in enumerate((first, second, rest - second)):
-            lse_parts = jnp.where(lane == head * 3 + place, part, lse_parts)
-        return mixed / turned, lse_parts
-
+        total = jnp.where(low, turned, mixed) if head % 2 == 0 else jnp.where(low, mixed, turned)
+        lse_parts = parts_of(-jnp.log2(total), head, lse_parts)
+        return mixed / turned, lse_parts, jnp.minimum(least, total), jnp.maximum(most, total)
+
+    least = jnp.full((size, LANES), 1.0, F32)
+    most = least
     for block in range(LEN // size):
         rows = pl.ds(block * size, size)
         waiting, outs = [], []
@@ -128,14 +134,49 @@
                 waiting.append(score(block, step))
             if step >= depth:
                 head = step - depth
-                out, lse_parts = finish(head, waiting.pop(0), lse_parts)
+                out, lse_parts, least, most = finish(head, waiting.pop(0), lse_parts, least, most)
                 outs.append(out)
                 if head % 2:
                     lanes = pl.ds(head // 2 * LANES, LANES)
                     o_ref[rows, lanes] = jnp.where(low, outs[-2], outs[-1]).astype(BF)
         qal_ref[rows, :] = (qa_ref[rows, :].astype(F32) + lse_parts).astype(BF)
-        moves.done(o_ref, rows)
-        moves.done(qal_ref, rows)
+    safe = (jnp.min(least) > safe_least) & (jnp.max(most) < safe_most)
+
+    @pl.when(jnp.logical_not(safe))
+    def _():
+        for block in range(BLOCKS):
+            rows = pl.ds(block * ROWS, ROWS)
+            keys = (block + 1) * ROWS if causal else LEN
+            qa = qa_ref[rows, :]
+
+            def one_pair(pair, lse_parts):
+                lanes = pl.ds(pl.multiple_of(pair * LANES, LANES), LANES)
+                k_cat = jnp.concatenate([kt_ref[lanes, :keys], kat_ref[:, :keys]], axis=0)
+                outs = []
+                for parity in range(2):
+                    half = half_row(parity)
+                    scores = nn(jnp.concatenate([q_ref[rows, lanes] * half, qa], axis=1), k_cat)
+                    if causal:
+                        diag = scores[:, keys - ROWS :] + bias
+                        scores = (
+                            jnp.concatenate([scores[:, : keys - ROWS], diag], axis=1) if block else diag
+                        )
+                    top = jnp.max(scores, axis=1, keepdims=True)
+                    probs = jnp.exp2(scores - top).astype(BF)
+                    mixed = nn(probs, v_ref[:keys, lanes] * half + (1.0 - half).astype(BF))
+                    turned = pltpu.roll(mixed, 64, 1)
+                    outs.append(mixed / turned)
+                    lse = -(top + jnp.log2(turned if parity == 0 else mixed))
+                    lse_parts = parts_of(lse, pair * 2 + parity, lse_parts)
+                lower = lax.broadcasted_iota(jnp.int32, (ROWS, LANES), 1) < 64
+                o_ref[rows, lanes] = jnp.where(lower, outs[0], outs[1]).astype(BF)
+                return lse_parts
+
+            lse_parts = lax.fori_loop(0, PAIRS, one_pair, jnp.zeros((ROWS, LANES), F32))
+            qal_ref[rows, :] = (qa.astype(F32) + lse_parts).astype(BF)
+
+    moves.done(o_ref)
+    moves.done(qal_ref)
 
 
 def attend_backward(
@@ -224,7 +265,7 @@
 class Moves:
     def __init__(self, sems):
         self.sems, self.used = sems, 0
-        self.inward, self.outward = {}, []
+        self.asked, self.inward, self.outward = {}, {}, []
 
     def copy(self, source, target):
         move = pltpu.make_async_copy(source, target, self.sems.at[self.used])
@@ -233,7 +274,17 @@
         return move
 
     def bring(self, source, target, key):
-        self.inward.setdefault(id(key), []).append(self.copy(source, target))
+        self.asked.setdefault(id(key), []).append((source, target))
+
+    def start(self, keys):
+        for key in keys:
+            for source, target in self.asked.pop(key, []):
+                self.inward.setdefault(key, []).append(self.copy(source, target))
+
+    def first(self, *refs):
+        self.start([id(ref) for ref in refs])
+        self.need(*refs)
+        self.start(list(self.asked))
 
     def need(self, *refs):
         for ref in refs:
@@ -301,7 +352,7 @@
     w_ref, kt_ref, kat_ref,
 ):
     fetch(moves, core_ref, parts, w_ref, FIRST_ROWS)
-    moves.need(x_ref, vec_ref, w_ref)
+    moves.first(x_ref, vec_ref, w_ref)
     for qb in range(TALLS):
         rows = pl.ds(qb * TALL, TALL)
         x = x_ref[rows, :]
@@ -328,7 +379,7 @@
     w_ref, kt_ref, kat_ref,
 ):
     fetch(moves, core_ref, parts, w_ref)
-    moves.need(m_ref, vec_ref, w_ref)
+    moves.first(m_ref, vec_ref, w_ref)
     for qb in range(TALLS):
         rows = pl.ds(qb * TALL, TALL)
         m = m_ref[rows, :]
@@ -373,7 +424,7 @@
         return square(w2_ref, j)
 
     vg_ref[...] = jnp.zeros_like(vg_ref)
-    moves.need(n2_ref, vec_ref, w1_ref)
+    moves.first(n2_ref, vec_ref, w1_ref, w2_ref)
     for tile in range(TALLS):
         rows = pl.ds(tile * TALL, TALL)
         n2 = n2_ref[rows, :]
@@ -441,11 +492,10 @@
 ):
     core = core_ref[0]
     fetch(moves, core_ref, parts, w_ref)
-    moves.need(dr2_ref)
+    moves.first(dr2_ref, w_ref, o_ref)
     for qb in range(TALLS):
         rows = pl.ds(qb * TALL, TALL)
         g_ref[rows, :] = dr2_ref[rows, :].astype(BF)
-    moves.need(w_ref, o_ref)
     mix_gradient(g_ref, square(w_ref, 3), o_ref, do_ref, del_ref)
     put_square_tn(mine_ref, other_ref, core, 3, o_ref, g_ref[...])
     moves.need(q_ref, k_ref, v_ref, qal_ref, ka_ref)
@@ -499,11 +549,10 @@
 ):
     core = core_ref[0]
     fetch(moves, core_ref, parts, w_ref, FIRST_ROWS)
-    moves.need(dr1_ref)
+    moves.first(dr1_ref, w_ref, o_ref)
     for qb in range(TALLS):
         rows = pl.ds(qb * TALL, TALL)
         g_ref[rows, :] = dr1_ref[rows, :].astype(BF)
-    moves.need(w_ref, o_ref)
     mix_gradient(g_ref, square(w_ref, 3), o_ref, do_ref, del_ref)
     moves.done(do_ref, EVERY, LATE)
     moves.done(del_ref)
@@ -525,7 +574,7 @@
     p_ref, s_ref, late_ref, kt_ref, dqt_ref,
 ):
     core, chip = core_ref[0], core_ref[1]
-    moves.need(q_ref, k_ref, v_ref, do_ref, qal_ref, del_ref, ka_ref)
+    moves.first(q_ref, k_ref, v_ref, do_ref, qal_ref, del_ref, ka_ref)
     attend_backward(
         q_ref, k_ref, v_ref, do_ref, qal_ref, del_ref, ka_ref, dq_ref, dk_ref, dv_ref, p_ref, s_ref, kt_ref, dqt_ref, True,
         (EARLY_PAIRS, PAIRS),
@@ -560,7 +609,7 @@
 ):
     fetch(moves, core_ref, parts, w_ref, FIRST_ROWS)
     fetch(moves, core_ref, parts2, wc_ref)
-    moves.need(w_ref, dr1_ref, dqs_ref, dks_ref, dvs_ref)
+    moves.first(w_ref, dr1_ref, dqs_ref, dks_ref, dvs_ref)
     for qb in range(TALLS):
         rows = pl.ds(qb * TALL, TALL)
         total = dr1_ref[rows, :] + nt(dqs_ref[rows, :], square(w_ref, 0))
@@ -723,7 +772,6 @@
     block3 = pick(third, first, third, chunk)
     across0 = to_corners(near0)
     pair1, near1 = to_sides(block1)
-    across0, near1 = lax.optimization_barrier((across0, near1))
     part0 = finish_block(pair0, near0, across0)
     across1 = to_corners(near1)
     pair2, near2 = to_sides(jnp.concatenate([block2, block3]))

time: 278 us -> 272 us (0.978)
  Pallas kernels: 131 us -> 126 us
    pallas_call x7, Pallas kernels: 131 us -> 126 us  [call(): pl.pallas_call(body, out_shape=sds, in_specs=[pl.BlockSpec(memory_space=s...]
  transfers between devices with their start and end apart: 34 -> 34, of which waited for: 18 -> 16; matrix products, arithmetic and copies ran while one was open for 3% -> 3% of each run, Pallas kernels for 39% -> 38%
where the time goes in v3:
time: 272 us; the launch traced here: 269 us
  Pallas kernels  126 us (46%)
  waiting for transfers between devices  65.7 us (24%)
  starting transfers between devices  44.2 us (16%)
  other arithmetic  19.2 us (7%)
  local copies, waits for them, and re-layouts  9.26 us (3%)
  between operations  4.18 us (2%)
    pallas_call x7, Pallas kernels, call(): pl.pallas_call(body, out_shape=sds, in_specs=[pl.BlockSpec(memory_space=s...  126 us
    ppermute x8, waiting for transfers between devices, along_z(): lax.ppermute(x, 'dp', [(8 * a + p, 8 * b + p) for a, b in moves for p in...  26.1 us
    ppermute x15, waiting for transfers between devices, swap(): return lax.ppermute(x, 'dp', [(i, i ^ bit) for i in range(32)])  18.7 us
    ppermute x8, starting transfers between devices, along_z(): lax.ppermute(x, 'dp', [(8 * a + p, 8 * b + p) for a, b in moves for p in...  17.8 us
    all_to_all x2, starting transfers between devices, plane_sum(): lax.all_to_all(pair, 'dp', 0, 0, tiled=True, axis_index_groups=groups_xy())  7.74 us
    ppermute x1, waiting for transfers between devices, gather_blocks(): lax.ppermute(low[share - VEC_LEN:], 'dp', [(i, (i + 1) % 32) for i in ran...  7.35 us
    ppermute x3, waiting for transfers between devices, to_corners(): return lax.ppermute(near[:near.shape[0] // 2], 'dp', sides(4, 2))  6.76 us
    all_to_all x1, waiting for transfers between devices, finish_blocks(): pieces = lax.all_to_all(pieces, 'dp', 0, 0, tiled=True)  6.75 us
  transfers between devices with their start and end apart: 34, of which 16 were waited for; matrix products, arithmetic and copies ran while one was open for 3% of the time, Pallas kernels for 38%

profile of v3, /device:TPU:0, one launch (start us, length us, event | category | flops | bytes accessed | tf_op | source)
XLA Modules:
  0.0 268.8 jit_solution(15285806591001093249)
XLA Ops:
  2.4 7.4 %collective-permute-done = bf16[8704]{0:T(1024)(128)(2,1)S(1)} collective-permute-done((bf16[8704]{0:T(1024)(128)(2,1)S(1)}, bf16[8704]{0:T(1024)(128)(2,1)S(1)}, u32[]{:S(2)}, u32[]{:S(2)}) %collective-permute-start) | collective-permute-done | bytes 17440 | tf_op jit(solution)/shard_map/ppermute | solution.py:751
  17.3 3.0 %collective-permute-start.2 = (bf16[288,512]{1,0:T(8,128)(2,1)S(1)}, bf16[288,512]{1,0:T(8,128)(2,1)S(1)}, u32[]{:S(2)}, u32[]{:S(2)}) collective-permute-start(bf16[288,512]{1,0:T(8,128)(2,1)S(1)} %broadcast_select_fusion), channel_id=1, source_target_pairs={{0,8},{1,9},{2,10},{3,11},{4,12},{5,13},{6,14},{7,15},{8,16},{9,17... | collective-permute-start | bytes 884744 | tf_op jit(solution)/shard_map/ppermute | solution.py:743
  21.7 7.0 %collective-permute-done.3 = bf16[256,512]{1,0:T(8,128)(2,1)S(1)} collective-permute-done((bf16[256,512]{1,0:T(8,128)(2,1)S(1)}, bf16[256,512]{1,0:T(8,128)(2,1)S(1)}, u32[]{:S(2)}, u32[]{:S(2)}) %collective-permute-start.3) | collective-permute-done | bytes 262176 | tf_op jit(solution)/shard_map/ppermute | solution.py:743
  33.3 8.5 %collective-permute-done.6 = bf16[256,512]{1,0:T(8,128)(2,1)S(1)} collective-permute-done((bf16[256,512]{1,0:T(8,128)(2,1)S(1)}, bf16[256,512]{1,0:T(8,128)(2,1)S(1)}, u32[]{:S(2)}, u32[]{:S(2)}) %collective-permute-start.6) | collective-permute-done | bytes 262176 | tf_op jit(solution)/shard_map/ppermute | solution.py:743
  45.1 6.8 %collective-permute-done.13.refs_4_ = bf16[288,512]{1,0:T(8,128)(2,1)S(1)} collective-permute-done((bf16[288,512]{1,0:T(8,128)(2,1)S(1)}, bf16[288,512]{1,0:T(8,128)(2,1)S(1)}, u32[]{:S(2)}, u32[]{:S(2)}) %collective-permute-start.13) | collective-permute-done | bytes 294944 | tf_op jit(solution)/shard_map/ppermute | solution.py:797
  52.0 2.3 collective-permute-start.11
  55.6 14.8 %shard_map.159 = (bf16[1024,512]{1,0:T(8,128)(2,1)}, bf16[1024,512]{1,0:T(8,128)(2,1)}, bf16[1024,512]{1,0:T(8,128)(2,1)}, bf16[1024,512]{1,0:T(8,128)(2,1)}, bf...) custom-call(s32[2]{0:T(128)} %pad_add_fusion.core_ref, bf16[288,512]{1,0:T(8,128)(2,1)} %copy-done.1, ...), custom_call_target="tpu_custom_call" | custom-call | flops 10737418240 | bytes 3997696 | tf_op jit(solution)/shard_map/pallas_call | solution.py:654
  75.5 17.9 %shard_map.160 = (bf16[1024,512]{1,0:T(8,128)(2,1)}, bf16[1024,512]{1,0:T(8,128)(2,1)}, bf16[1024,512]{1,0:T(8,128)(2,1)}, bf16[1024,512]{1,0:T(8,128)(2,1)}, bf...) custom-call(s32[2]{0:T(128)} %pad_add_fusion.core_ref, bf16[256,512]{1,0:T(8,128)(2,1)} %copy-done.4, ...), custom_call_target="tpu_custom_call" | custom-call | flops 13421772800 | bytes 5832704 | tf_op jit(solution)/shard_map/pallas_call | solution.py:654
  93.6 1.9 collective-permute-done.19.refs_5_
  96.6 23.5 %shard_map.161 = (bf16[1024,512]{1,0:T(8,128)(2,1)}, bf16[4,512,512]{2,1,0:T(8,128)(2,1)}, bf16[4,512,512]{2,1,0:T(8,128)(2,1)}, f32[1024,512]{1,0:T(8,128)}, f32[32,512]{1,0:T(8,128)}) custom-call(s32[2]{0:T(128)} %pad_add_fusion.core_ref, bf16[512,512]{1,0:T(8,128)(2,1)} %copy-done.7, bf16[512,512]{1,0:T(8,128)(2,1)} %copy-done.8, ...), custom_call_target="tpu_custom_call" | custom-call | flops 13958643712 | bytes 7929856 | tf_op jit(solution)/shard_map/pallas_call | solution.py:654
  120.3 4.2 %collective-permute-done.20 = bf16[4,512,512]{2,1,0:T(8,128)(2,1)S(1)} collective-permute-done((bf16[4,512,512]{2,1,0:T(8,128)(2,1)}, bf16[4,512,512]{2,1,0:T(8,128)(2,1)S(1)}, u32[]{:S(2)}, u32[]{:S(2)}) %collective-permute-start.20) | collective-permute-done | bytes 2097184 | tf_op jit(solution)/shard_map/ppermute | solution.py:731
  124.6 3.5 %add_convert_fusion = bf16[4,512,512]{2,1,0:T(8,128)(2,1)} fusion(bf16[4,512,512]{2,1,0:T(8,128)(2,1)S(1)} %collective-permute-done.20, bf16[4,512,512]{2,1,0:T(8,128)(2,1)} %get-tuple-element.111), kind=kLoop, calls=%fused_computation | loop fusion | flops 4194304 | bytes 6291456 | tf_op jit(solution)/shard_map/convert_element_type | solution.py:829
  128.1 3.6 %all-to-all-start = ((bf16[4,512,512]{2,1,0:T(8,128)(2,1)}), bf16[4,512,512]{2,1,0:T(8,128)(2,1)S(1)}, u32[]{:S(2)}, u32[]{:S(2)}) async-start(bf16[4,512,512]{2,1,0:T(8,128)(2,1)} %add_convert_fusion), calls=%async_computation | async-start | bytes 4194304 | tf_op jit(solution)/shard_map/all_to_all | solution.py:830
  131.7 33.6 %shard_map.162 = (bf16[4,272,512]{2,1,0:T(8,128)(2,1)}, bf16[4,272,512]{2,1,0:T(8,128)(2,1)}, f32[1024,512]{1,0:T(8,128)}, bf16[1024,512]{1,0:T(8,128)(2,1)}, bf16[1024,512]{1,0:T(8,128)(2,1)}) custom-call(s32[2]{0:T(128)} %pad_add_fusion.core_ref, bf16[256,512]{1,0:T(8,128)(2,1)} %copy-done.4, bf16[256,512]{1,0:T(8,128)(2,1)} %copy-done.10, ...), custom_call_target="tpu_custom_call" | custom-call | flops 26843545600 | bytes 12713984 | tf_op jit(solution)/shard_map/pallas_call | solution.py:654
  166.3 2.8 %collective-permute-done.21 = bf16[4,272,512]{2,1,0:T(8,128)(2,1)S(1)} collective-permute-done((bf16[4,272,512]{2,1,0:T(8,128)(2,1)}, bf16[4,272,512]{2,1,0:T(8,128)(2,1)S(1)}, u32[]{:S(2)}, u32[]{:S(2)}) %collective-permute-start.21) | collective-permute-done | bytes 1114144 | tf_op jit(solution)/shard_map/ppermute | solution.py:731
  169.1 2.6 add_convert_fusion.1
  171.6 4.1 %all-to-all-start.1 = ((bf16[4,272,512]{2,1,0:T(8,128)(2,1)}), bf16[4,272,512]{2,1,0:T(8,128)(2,1)S(1)}, u32[]{:S(2)}, u32[]{:S(2)}) async-start(bf16[4,272,512]{2,1,0:T(8,128)(2,1)} %add_convert_fusion.1), calls=%async_computation.1 | async-start | bytes 2228224 | tf_op jit(solution)/shard_map/all_to_all | solution.py:830
  175.8 18.4 %shard_map.163 = (bf16[1024,512]{1,0:T(8,128)(2,1)}, bf16[1024,128]{1,0:T(8,128)(2,1)}, bf16[1024,512]{1,0:T(8,128)(2,1)}, bf16[1024,512]{1,0:T(8,128)(2,1)}, bf...) custom-call(s32[2]{0:T(128)} %pad_add_fusion.core_ref, bf16[288,512]{1,0:T(8,128)(2,1)} %copy-done.1, ...), custom_call_target="tpu_custom_call" | custom-call | flops 13421772800 | bytes 9175040 | tf_op jit(solution)/shard_map/pallas_call | solution.py:654
  194.6 2.4 collective-permute-start.22
  197.0 9.3 %shard_map.164 = (bf16[4,272,512]{2,1,0:T(8,128)(2,1)}, bf16[4,272,512]{2,1,0:T(8,128)(2,1)}, bf16[1024,512]{1,0:T(8,128)(2,1)}, bf16[1024,512]{1,0:T(8,128)(2,1)}, bf16[1024,512]{1,0:T(8,128)(2,1)}) custom-call(s32[2]{0:T(128)} %pad_add_fusion.core_ref, bf16[1024,512]{1,0:T(8,128)(2,1)} %get-tuple-element.129.refs_8_.refs_0_, ...), custom_call_target="tpu_custom_call" | custom-call | flops 6442450944 | bytes 9699328 | tf_op jit(solution)/shard_map/pallas_call | solution.py:654
  206.4 3.0 %collective-permute-done.23 = bf16[4,272,512]{2,1,0:T(8,128)(2,1)S(1)} collective-permute-done((bf16[4,272,512]{2,1,0:T(8,128)(2,1)}, bf16[4,272,512]{2,1,0:T(8,128)(2,1)S(1)}, u32[]{:S(2)}, u32[]{:S(2)}) %collective-permute-start.23) | collective-permute-done | bytes 1114144 | tf_op jit(solution)/shard_map/ppermute | solution.py:731
  210.7 2.1 collective-permute-start.24
  214.4 8.7 %shard_map.165 = (bf16[1024,512]{1,0:T(8,128)(2,1)}, bf16[1024,512]{1,0:T(8,128)(2,1)}) custom-call(s32[2]{0:T(128)} %pad_add_fusion.core_ref, bf16[288,512]{1,0:T(8,128)(2,1)} %copy-done.1, bf16[288,512]{1,0:T(8,128)(2,1)} %copy-done.9, bf16[576,512]{1,0:T(8,128)(2,1)} %copy-done.11, bf16[576,512]{1,0:T(8,128)(2,1)} %copy-done.14, ...), custom_call_target="tpu_custom_call" | custom-call | flops 3221225472 | bytes 11796480 | tf_op jit(solution)/shard_map/pallas_call | solution.py:654
  223.1 3.9 %collective-permute-done.26 = bf16[272,512]{1,0:T(8,128)(2,1)S(1)} collective-permute-done((bf16[272,512]{1,0:T(8,128)(2,1)S(1)}, bf16[272,512]{1,0:T(8,128)(2,1)S(1)}, u32[]{:S(2)}, u32[]{:S(2)}) %collective-permute-start.26) | collective-permute-done | bytes 278560 | tf_op jit(solution)/shard_map/ppermute | solution.py:731
  231.0 4.6 %collective-permute-start.28 = (bf16[272,512]{1,0:T(8,128)(2,1)S(1)}, bf16[272,512]{1,0:T(8,128)(2,1)S(1)}, u32[]{:S(2)}, u32[]{:S(2)}) collective-permute-start(bf16[272,512]{1,0:T(8,128)(2,1)S(1)} %get-tuple-element.185), channel_id=1, source_target_pairs={{0,8},{1,9},{2,10},{3,11},{4,12},{5,13},{6,14},{7,15},{8,16},{9,17... | collective-permute-start | bytes 835592 | tf_op jit(solution)/shard_map/ppermute | solution.py:743
  235.6 2.6 collective-permute-done.27
  238.2 2.1 collective-permute-done.28
  240.5 2.5 collective-permute-start.29
  243.0 5.0 %collective-permute-done.29 = bf16[272,512]{1,0:T(8,128)(2,1)S(1)} collective-permute-done((bf16[272,512]{1,0:T(8,128)(2,1)S(1)}, bf16[272,512]{1,0:T(8,128)(2,1)S(1)}, u32[]{:S(2)}, u32[]{:S(2)}) %collective-permute-start.29) | collective-permute-done | bytes 278560 | tf_op jit(solution)/shard_map/ppermute | solution.py:743
  251.1 3.2 %all-to-all-start.2 = ((f32[32,8,128]{2,1,0:T(8,128)}), f32[32,8,128]{2,1,0:T(8,128)S(1)}, u32[]{:S(2)}, u32[]{:S(2)}) async-start(f32[32,8,128]{2,1,0:T(8,128)} %broadcast_in_dim.30), calls=%async_computation.2 | async-start | bytes 262144 | tf_op jit(solution)/shard_map/all_to_all | solution.py:873
  255.8 6.8 %all-to-all-done.2 = f32[32,8,128]{2,1,0:T(8,128)S(1)} async-done(((f32[32,8,128]{2,1,0:T(8,128)}), f32[32,8,128]{2,1,0:T(8,128)S(1)}, u32[]{:S(2)}, u32[]{:S(2)}) %all-to-all-start.2) | async-done | bytes 131104 | tf_op jit(solution)/shard_map/all_to_all | solution.py:873
  265.4 2.1 fusion.26
  (167 shorter events, 40.5 us)
Async XLA Ops:
  1.9 7.8 %collective-permute-start = (bf16[8704]{0:T(1024)(128)(2,1)S(1)}, bf16[8704]{0:T(1024)(128)(2,1)S(1)}, u32[]{:S(2)}, u32[]{:S(2)}) collective-permute-start(bf16[8704]{0:T(1024)(128)(2,1)S(1)} %slice.145), channel_id=1, source_target_pairs={{0,1},{1,2},{2,3},{3,4},{4,5},{5,6},{6,7},{7,8},{8,9},{9,10},{10,1... | collective-permute-start | bytes 52232 | tf_op jit(solution)/shard_map/ppermute | solution.py:751
  10.5 6.8 %collective-permute-start.1 = (bf16[288,512]{1,0:T(8,128)(2,1)S(1)}, bf16[288,512]{1,0:T(8,128)(2,1)S(1)}, u32[]{:S(2)}, u32[]{:S(2)}) collective-permute-start(bf16[288,512]{1,0:T(8,128)(2,1)S(1)} %fusion.9), channel_id=1, source_target_pairs={{0,16},{1,17},{2,18},{3,19},{4,20},{5,21},{6,22},{7,23},{8,0},{9,1... | collective-permute-start | bytes 884744 | tf_op jit(solution)/shard_map/ppermute | solution.py:743
  17.3 11.3 %collective-permute-start.2 = (bf16[288,512]{1,0:T(8,128)(2,1)S(1)}, bf16[288,512]{1,0:T(8,128)(2,1)S(1)}, u32[]{:S(2)}, u32[]{:S(2)}) collective-permute-start(bf16[288,512]{1,0:T(8,128)(2,1)S(1)} %broadcast_select_fusion), channel_id=1, source_target_pairs={{0,8},{1,9},{2,10},{3,11},{4,12},{5,13},{6,14},{7,15},{8,16},{9,17... | collective-permute-start | bytes 884744 | tf_op jit(solution)/shard_map/ppermute | solution.py:743
  20.4 8.3 %collective-permute-start.3 = (bf16[256,512]{1,0:T(8,128)(2,1)S(1)}, bf16[256,512]{1,0:T(8,128)(2,1)S(1)}, u32[]{:S(2)}, u32[]{:S(2)}) collective-permute-start(bf16[256,512]{1,0:T(8,128)(2,1)S(1)} %slice_select_fusion), channel_id=1, source_target_pairs={{24,16},{25,17},{26,18},{27,19},{28,20},{29,21},{30,22},{31,23},{1... | collective-permute-start | bytes 786440 | tf_op jit(solution)/shard_map/ppermute | solution.py:743
  30.5 11.3 %collective-permute-start.5 = (bf16[576,512]{1,0:T(8,128)(2,1)S(1)}, bf16[576,512]{1,0:T(8,128)(2,1)S(1)}, u32[]{:S(2)}, u32[]{:S(2)}) collective-permute-start(bf16[576,512]{1,0:T(8,128)(2,1)S(1)} %pad_maximum_fusion.1), channel_id=1, source_target_pairs={{0,2},{1,5},{2,0},{3,7},{4,6},{5,1},{6,4},{7,3},{8,10},{9,13},{10,... | collective-permute-start | bytes 1769480 | tf_op jit(solution)/shard_map/ppermute | solution.py:793
  31.8 10.0 %collective-permute-start.6 = (bf16[256,512]{1,0:T(8,128)(2,1)S(1)}, bf16[256,512]{1,0:T(8,128)(2,1)S(1)}, u32[]{:S(2)}, u32[]{:S(2)}) collective-permute-start(bf16[256,512]{1,0:T(8,128)(2,1)S(1)} %broadcast_select_fusion.2), channel_id=1, source_target_pairs={{8,0},{9,1},{10,2},{11,3},{12,4},{13,5},{14,6},{15,7},{16,24},{17,... | collective-permute-start | bytes 786440 | tf_op jit(solution)/shard_map/ppermute | solution.py:743
  42.0 9.8 %collective-permute-start.10 = (bf16[512,512]{1,0:T(8,128)(2,1)S(1)}, bf16[512,512]{1,0:T(8,128)(2,1)S(1)}, u32[]{:S(2)}, u32[]{:S(2)}) collective-permute-start(bf16[512,512]{1,0:T(8,128)(2,1)S(1)} %pad_maximum_fusion.3.refs_0_), channel_id=1, source_target_pairs={{0,1},{1,0},{2,3},{3,2},{4,5},{5,4},{6,7},{7,6},{8,9},{9,8},{10,11... | collective-permute-start | bytes 1572872 | tf_op jit(solution)/shard_map/ppermute | solution.py:731
  42.6 11.7 %collective-permute-start.12 = (bf16[576,512]{1,0:T(8,128)(2,1)S(1)}, bf16[576,512]{1,0:T(8,128)(2,1)S(1)}, u32[]{:S(2)}, u32[]{:S(2)}) collective-permute-start(bf16[576,512]{1,0:T(8,128)(2,1)S(1)} %collective-permute-done.5.refs_2_), channel_id=1, source_target_pairs={{0,1},{1,0},{2,3},{3,2},{4,5},{5,4},{6,7},{7,6},{8,9},{9,8},{10,11... | collective-permute-start | bytes 1769480 | tf_op jit(solution)/shard_map/ppermute | solution.py:731
  42.7 9.2 %collective-permute-start.13 = (bf16[288,512]{1,0:T(8,128)(2,1)S(1)}, bf16[288,512]{1,0:T(8,128)(2,1)S(1)}, u32[]{:S(2)}, u32[]{:S(2)}) collective-permute-start(bf16[288,512]{1,0:T(8,128)(2,1)S(1)} %slice.114), channel_id=1, source_target_pairs={{0,4},{1,3},{2,6},{3,1},{4,0},{5,7},{6,2},{7,5},{8,12},{9,11},{10,... | collective-permute-start | bytes 884744 | tf_op jit(solution)/shard_map/ppermute | solution.py:797
  43.6 11.5 %collective-permute-start.8 = (bf16[512,512]{1,0:T(8,128)(2,1)S(1)}, bf16[512,512]{1,0:T(8,128)(2,1)S(1)}, u32[]{:S(2)}, u32[]{:S(2)}) collective-permute-start(bf16[512,512]{1,0:T(8,128)(2,1)S(1)} %pad_maximum_fusion.2), channel_id=1, source_target_pairs={{0,2},{1,5},{2,0},{3,7},{4,6},{5,1},{6,4},{7,3},{8,10},{9,13},{10,... | collective-permute-start | bytes 1572872 | tf_op jit(solution)/shard_map/ppermute | solution.py:793
  51.9 2.5 collective-permute-start.14
  52.0 18.5 %collective-permute-start.11 = (bf16[1024,512]{1,0:T(8,128)(2,1)S(1)}, bf16[1024,512]{1,0:T(8,128)(2,1)}, u32[]{:S(2)}, u32[]{:S(2)}) collective-permute-start(bf16[1024,512]{1,0:T(8,128)(2,1)S(1)} %pad_maximum_fusion), channel_id=1, source_target_pairs={{0,2},{1,5},{2,0},{3,7},{4,6},{5,1},{6,4},{7,3},{8,10},{9,13},{10,... | collective-permute-start | bytes 3145736 | tf_op jit(solution)/shard_map/ppermute | solution.py:793
  55.2 15.3 %collective-permute-start.9 = (bf16[256,512]{1,0:T(8,128)(2,1)S(1)}, bf16[256,512]{1,0:T(8,128)(2,1)S(1)}, u32[]{:S(2)}, u32[]{:S(2)}) collective-permute-start(bf16[256,512]{1,0:T(8,128)(2,1)S(1)} %slice.148), channel_id=1, source_target_pairs={{0,4},{1,3},{2,6},{3,1},{4,0},{5,7},{6,2},{7,5},{8,12},{9,11},{10,... | collective-permute-start | bytes 786440 | tf_op jit(solution)/shard_map/ppermute | solution.py:797
  70.5 3.5 %collective-permute-start.17 = (bf16[512,512]{1,0:T(8,128)(2,1)S(1)}, bf16[512,512]{1,0:T(8,128)(2,1)S(1)}, u32[]{:S(2)}, u32[]{:S(2)}) collective-permute-start(bf16[512,512]{1,0:T(8,128)(2,1)S(1)} %collective-permute-done.8.refs_2_.refs_8_), channel_id=1, source_target_pairs={{0,1},{1,0},{2,3},{3,2},{4,5},{5,4},{6,7},{7,6},{8,9},{9,8},{10,11... | collective-permute-start | bytes 1572872 | tf_op jit(solution)/shard_map/ppermute | solution.py:731
  71.3 2.7 collective-permute-start.18
  72.5 23.0 %collective-permute-start.15 = (bf16[1024,512]{1,0:T(8,128)(2,1)}, bf16[1024,512]{1,0:T(8,128)(2,1)S(1)}, u32[]{:S(2)}, u32[]{:S(2)}) collective-permute-start(bf16[1024,512]{1,0:T(8,128)(2,1)} %collective-permute-done.11.refs_2_), channel_id=1, source_target_pairs={{0,1},{1,0},{2,3},{3,2},{4,5},{5,4},{6,7},{7,6},{8,9},{9,8},{10,11... | collective-permute-start | bytes 3145736 | tf_op jit(solution)/shard_map/ppermute | solution.py:731
  73.0 20.5 %collective-permute-start.16 = (bf16[512,512]{1,0:T(8,128)(2,1)S(1)}, bf16[512,512]{1,0:T(8,128)(2,1)S(1)}, u32[]{:S(2)}, u32[]{:S(2)}) collective-permute-start(bf16[512,512]{1,0:T(8,128)(2,1)S(1)} %slice.123), channel_id=1, source_target_pairs={{0,4},{1,3},{2,6},{3,1},{4,0},{5,7},{6,2},{7,5},{8,12},{9,11},{10,... | collective-permute-start | bytes 1572872 | tf_op jit(solution)/shard_map/ppermute | solution.py:797
  93.5 2.0 collective-permute-start.19
  120.1 4.4 %collective-permute-start.20 = (bf16[4,512,512]{2,1,0:T(8,128)(2,1)}, bf16[4,512,512]{2,1,0:T(8,128)(2,1)S(1)}, u32[]{:S(2)}, u32[]{:S(2)}) collective-permute-start(bf16[4,512,512]{2,1,0:T(8,128)(2,1)} %get-tuple-element.112), channel_id=1, source_target_pairs={{0,1},{1,0},{2,3},{3,2},{4,5},{5,4},{6,7},{7,6},{8,9},{9,8},{10,11... | collective-permute-start | bytes 6291464 | tf_op jit(solution)/shard_map/ppermute | solution.py:731
  128.1 37.3 %all-to-all-start = ((bf16[4,512,512]{2,1,0:T(8,128)(2,1)}), bf16[4,512,512]{2,1,0:T(8,128)(2,1)S(1)}, u32[]{:S(2)}, u32[]{:S(2)}) async-start(bf16[4,512,512]{2,1,0:T(8,128)(2,1)} %add_convert_fusion), calls=%async_computation | async-start | bytes 4194304 | tf_op jit(solution)/shard_map/all_to_all | solution.py:830
  166.0 3.0 %collective-permute-start.21 = (bf16[4,272,512]{2,1,0:T(8,128)(2,1)}, bf16[4,272,512]{2,1,0:T(8,128)(2,1)S(1)}, u32[]{:S(2)}, u32[]{:S(2)}) collective-permute-start(bf16[4,272,512]{2,1,0:T(8,128)(2,1)} %get-tuple-element.126), channel_id=1, source_target_pairs={{0,1},{1,0},{2,3},{3,2},{4,5},{5,4},{6,7},{7,6},{8,9},{9,8},{10,11... | collective-permute-start | bytes 3342344 | tf_op jit(solution)/shard_map/ppermute | solution.py:731
  171.6 22.6 %all-to-all-start.1 = ((bf16[4,272,512]{2,1,0:T(8,128)(2,1)}), bf16[4,272,512]{2,1,0:T(8,128)(2,1)S(1)}, u32[]{:S(2)}, u32[]{:S(2)}) async-start(bf16[4,272,512]{2,1,0:T(8,128)(2,1)} %add_convert_fusion.1), calls=%async_computation.1 | async-start | bytes 2228224 | tf_op jit(solution)/shard_map/all_to_all | solution.py:830
  194.6 11.7 %collective-permute-start.22 = (bf16[272,512]{1,0:T(8,128)(2,1)S(1)}, bf16[272,512]{1,0:T(8,128)(2,1)S(1)}, u32[]{:S(2)}, u32[]{:S(2)}) collective-permute-start(bf16[272,512]{1,0:T(8,128)(2,1)S(1)} %get-tuple-element.186), channel_id=1, source_target_pairs={{0,8},{1,9},{2,10},{3,11},{4,12},{5,13},{6,14},{7,15},{24,16},{25,... | collective-permute-start | bytes 835592 | tf_op jit(solution)/shard_map/ppermute | solution.py:743
  206.3 3.0 %collective-permute-start.23 = (bf16[4,272,512]{2,1,0:T(8,128)(2,1)}, bf16[4,272,512]{2,1,0:T(8,128)(2,1)S(1)}, u32[]{:S(2)}, u32[]{:S(2)}) collective-permute-start(bf16[4,272,512]{2,1,0:T(8,128)(2,1)} %get-tuple-element.151), channel_id=1, source_target_pairs={{0,1},{1,0},{2,3},{3,2},{4,5},{5,4},{6,7},{7,6},{8,9},{9,8},{10,11... | collective-permute-start | bytes 3342344 | tf_op jit(solution)/shard_map/ppermute | solution.py:731
  210.7 12.4 %collective-permute-start.24 = (bf16[272,512]{1,0:T(8,128)(2,1)S(1)}, bf16[272,512]{1,0:T(8,128)(2,1)S(1)}, u32[]{:S(2)}, u32[]{:S(2)}) collective-permute-start(bf16[272,512]{1,0:T(8,128)(2,1)S(1)} %get-tuple-element.175), channel_id=1, source_target_pairs={{0,2},{1,3},{2,0},{3,1},{4,6},{5,7},{6,4},{7,5},{8,10},{9,11},{10,... | collective-permute-start | bytes 835592 | tf_op jit(solution)/shard_map/ppermute | solution.py:731
  212.8 14.2 %collective-permute-start.26 = (bf16[272,512]{1,0:T(8,128)(2,1)S(1)}, bf16[272,512]{1,0:T(8,128)(2,1)S(1)}, u32[]{:S(2)}, u32[]{:S(2)}) collective-permute-start(bf16[272,512]{1,0:T(8,128)(2,1)S(1)} %get-tuple-element.176), channel_id=1, source_target_pairs={{0,6},{1,7},{2,4},{3,5},{4,2},{5,3},{6,0},{7,1},{8,14},{9,15},{10,... | collective-permute-start | bytes 835592 | tf_op jit(solution)/shard_map/ppermute | solution.py:731
  214.3 14.1 %collective-permute-start.25 = (bf16[272,512]{1,0:T(8,128)(2,1)S(1)}, bf16[272,512]{1,0:T(8,128)(2,1)S(1)}, u32[]{:S(2)}, u32[]{:S(2)}) collective-permute-start(bf16[272,512]{1,0:T(8,128)(2,1)S(1)} %get-tuple-element.177), channel_id=1, source_target_pairs={{0,4},{1,5},{2,6},{3,7},{4,0},{5,1},{6,2},{7,3},{8,12},{9,13},{10,... | collective-permute-start | bytes 835592 | tf_op jit(solution)/shard_map/ppermute | solution.py:731
  229.7 8.4 %collective-permute-start.27 = (bf16[272,512]{1,0:T(8,128)(2,1)S(1)}, bf16[272,512]{1,0:T(8,128)(2,1)S(1)}, u32[]{:S(2)}, u32[]{:S(2)}) collective-permute-start(bf16[272,512]{1,0:T(8,128)(2,1)S(1)} %get-tuple-element.173), channel_id=1, source_target_pairs={{8,0},{9,1},{10,2},{11,3},{12,4},{13,5},{14,6},{15,7},{16,8},{17,9... | collective-permute-start | bytes 835592 | tf_op jit(solution)/shard_map/ppermute | solution.py:743
  231.0 9.2 %collective-permute-start.28 = (bf16[272,512]{1,0:T(8,128)(2,1)S(1)}, bf16[272,512]{1,0:T(8,128)(2,1)S(1)}, u32[]{:S(2)}, u32[]{:S(2)}) collective-permute-start(bf16[272,512]{1,0:T(8,128)(2,1)S(1)} %get-tuple-element.185), channel_id=1, source_target_pairs={{0,8},{1,9},{2,10},{3,11},{4,12},{5,13},{6,14},{7,15},{8,16},{9,17... | collective-permute-start | bytes 835592 | tf_op jit(solution)/shard_map/ppermute | solution.py:743
  240.5 7.5 %collective-permute-start.29 = (bf16[272,512]{1,0:T(8,128)(2,1)S(1)}, bf16[272,512]{1,0:T(8,128)(2,1)S(1)}, u32[]{:S(2)}, u32[]{:S(2)}) collective-permute-start(bf16[272,512]{1,0:T(8,128)(2,1)S(1)} %fusion.15), channel_id=1, source_target_pairs={{16,0},{17,1},{18,2},{19,3},{20,4},{21,5},{22,6},{23,7},{0,8},{1,9... | collective-permute-start | bytes 835592 | tf_op jit(solution)/shard_map/ppermute | solution.py:743
  251.1 11.4 %all-to-all-start.2 = ((f32[32,8,128]{2,1,0:T(8,128)}), f32[32,8,128]{2,1,0:T(8,128)S(1)}, u32[]{:S(2)}, u32[]{:S(2)}) async-start(f32[32,8,128]{2,1,0:T(8,128)} %broadcast_in_dim.30), calls=%async_computation.2 | async-start | bytes 262144 | tf_op jit(solution)/shard_map/all_to_all | solution.py:873
  254.3 11.0 %collective-permute-start.30 = (f32[8704]{0:T(1024)S(1)}, f32[8704]{0:T(1024)S(1)}, u32[]{:S(2)}, u32[]{:S(2)}) collective-permute-start(f32[8704]{0:T(1024)S(1)} %slice.144), channel_id=1, source_target_pairs={{1,0},{2,1},{3,2},{4,3},{5,4},{6,5},{7,6},{8,7},{9,8},{10,9},{11,1... | collective-permute-start | bytes 104456 | tf_op jit(solution)/shard_map/ppermute | solution.py:864
  (27 other events, 200.4 us)

commit v4 on v3

--- a/solution.py
+++ b/solution.py
@@ -18,7 +18,6 @@
 LANES = 128
 PAIRS = D // LANES
 MASK_LANE = 32
-EARLY_PAIRS = 3
 FIRST_ROWS = ROWS + 32
 
 eps_norm = 1e-05
@@ -181,11 +180,10 @@
 
 def attend_backward(
     q_ref, k_ref, v_ref, do_ref, qal_ref, del_ref, ka_ref, dq_ref, dk_ref, dv_ref, p_ref, s_ref, kt_ref, dqt_ref,
-    causal, span=(0, PAIRS),
+    causal,
 ):
     bias = causal_bias(True) if causal else None
-    cols = pl.ds(span[0] * LANES, (span[1] - span[0]) * LANES)
-    kt_ref[cols, :] = k_ref[:, cols].T
+    kt_ref[...] = k_ref[...].T
 
     def score(head, block):
         lanes = pl.ds(head // 2 * LANES, LANES)
@@ -228,7 +226,7 @@
             dk = dk + nn(s_ref[1, rows, tail], q_pair * half_row(1))
             dk_ref[rows, lanes] = (dk * key_scale).astype(BF)
 
-    steps = [(h, b) for h in range(2 * span[0], 2 * span[1]) for b in range(BLOCKS)]
+    steps = [(h, b) for h in range(HEADS) for b in range(BLOCKS)]
     waiting = score(*steps[0])
     for place, (head, block) in enumerate(steps):
         current = waiting
@@ -239,7 +237,7 @@
             pair_end(head // 2)
     for block in range(BLOCKS):
         rows = pl.ds(block * ROWS, ROWS)
-        dq_ref[rows, cols] = (dqt_ref[cols, rows] * 0.125).T.astype(BF)
+        dq_ref[rows, :] = (dqt_ref[:, rows] * 0.125).T.astype(BF)
 
 
 def mix_gradient(g_ref, w_out, o_ref, do_ref, del_ref):
@@ -537,55 +535,26 @@
         moves.done(ref, 0)
 
 
-EARLY = pl.ds(0, EARLY_PAIRS * LANES)
-LATE = pl.ds(EARLY_PAIRS * LANES, (PAIRS - EARLY_PAIRS) * LANES)
-EVERY = slice(None)
-
-
-def self_backward_start_kernel(
-    moves, core_ref, parts, dr1_ref, o_ref, q_ref, k_ref, v_ref, qal_ref, ka_ref,
-    do_ref, del_ref, dq_ref, dk_ref, dv_ref, so_ref,
-    g_ref, p_ref, s_ref, w_ref, kt_ref, dqt_ref,
+def self_backward_kernel(
+    moves, core_ref, parts, dr1_ref, o_ref, q_ref, k_ref, v_ref, qal_ref, ka_ref, xt_ref,
+    mine_ref, other_ref, dq_ref, dk_ref, dv_ref,
+    g_ref, do_ref, del_ref, p_ref, s_ref, w_ref, late_ref, kt_ref, dqt_ref,
 ):
-    core = core_ref[0]
+    core, chip = core_ref[0], core_ref[1]
     fetch(moves, core_ref, parts, w_ref, FIRST_ROWS)
     moves.first(dr1_ref, w_ref, o_ref)
     for qb in range(TALLS):
         rows = pl.ds(qb * TALL, TALL)
         g_ref[rows, :] = dr1_ref[rows, :].astype(BF)
     mix_gradient(g_ref, square(w_ref, 3), o_ref, do_ref, del_ref)
-    moves.done(do_ref, EVERY, LATE)
-    moves.done(del_ref)
-    halves = [o_ref[:, pl.ds(pl.multiple_of(h * ROWS, ROWS), ROWS)] for h in (core, 1 - core)]
-    so_ref[...] = tn(jnp.concatenate(halves, axis=1), g_ref[...]).astype(BF).reshape(2, ROWS, D)
-    moves.done(so_ref)
+    put_square_tn(mine_ref, other_ref, core, 3, o_ref, g_ref[...], chip)
     moves.need(q_ref, k_ref, v_ref, qal_ref, ka_ref)
     attend_backward(
-        q_ref, k_ref, v_ref, do_ref, qal_ref, del_ref, ka_ref, dq_ref, dk_ref, dv_ref, p_ref, s_ref, kt_ref, dqt_ref, True,
-        (0, EARLY_PAIRS),
+        q_ref, k_ref, v_ref, do_ref, qal_ref, del_ref, ka_ref, dq_ref, dk_ref, dv_ref, p_ref, s_ref, kt_ref, dqt_ref, True
     )
     for ref in (dq_ref, dk_ref, dv_ref):
-        moves.done(ref, EVERY, EARLY)
-
-
-def self_backward_end_kernel(
-    moves, core_ref, q_ref, k_ref, v_ref, do_ref, qal_ref, del_ref, ka_ref, dqe_ref, dke_ref, dve_ref, xt_ref, so_ref,
-    mine_ref, other_ref, dq_ref, dk_ref, dv_ref,
-    p_ref, s_ref, late_ref, kt_ref, dqt_ref,
-):
-    core, chip = core_ref[0], core_ref[1]
-    moves.first(q_ref, k_ref, v_ref, do_ref, qal_ref, del_ref, ka_ref)
-    attend_backward(
-        q_ref, k_ref, v_ref, do_ref, qal_ref, del_ref, ka_ref, dq_ref, dk_ref, dv_ref, p_ref, s_ref, kt_ref, dqt_ref, True,
-        (EARLY_PAIRS, PAIRS),
-    )
-    for ref, source in ((dq_ref, dqe_ref), (dk_ref, dke_ref), (dv_ref, dve_ref)):
-        moves.need(source)
-        ref[:, EARLY] = source[:, EARLY]
         moves.done(ref)
-    moves.need(xt_ref, so_ref)
-    mine_ref[3 ^ chip, :ROWS, :] = so_ref[0]
-    other_ref[3 ^ chip, :ROWS, :] = so_ref[1]
+    moves.need(xt_ref)
     late_ref[0:1, :] = col_sum(dq_ref[...])
     late_ref[1:2, :] = col_sum(dv_ref[...])
     for ref, half in ((mine_ref, core), (other_ref, 1 - core)):
@@ -624,8 +593,7 @@
         moves.done(mg_ref, rows)
 
 
-def call(kernel, outs, scratch, flops, core, parts, args, views=None):
-    views = views or {}
+def call(kernel, outs, scratch, flops, core, parts, args):
     sds = [jax.ShapeDtypeStruct(shape, dtype) for shape, dtype in outs]
     arrays = [block for group in parts for block in group]
     moved = sum(a.size * a.dtype.itemsize for a in arrays + list(args))
@@ -641,11 +609,8 @@
         results, refs = refs[: len(outs)], refs[len(outs) :]
         held, refs = refs[: len(args)], refs[len(args) :]
         moves = Moves(refs[-1])
-        for i, (source, target) in enumerate(zip(given, held)):
-            if i in views:
-                moves.bring(source.at[views[i]], target.at[views[i]], target)
-            else:
-                moves.bring(source, target, target)
+        for source, target in zip(given, held):
+            moves.bring(source, target, target)
         for place, result in zip(refs, results):
             moves.pair(place, result)
         kernel(moves, core_ref, *groups, *held, *refs[:-1])
@@ -696,17 +661,10 @@
     return call(cross_backward_kernel, outs, scratch, 50 * unit, core, [w], args)
 
 
-def self_backward_start(core, w, *args):
-    outs = [TOKB, (STAT, BF), TOKB, TOKB, TOKB, ((2, ROWS, D), BF)]
-    scratch = [TOKB, PROBS, PROBS, (OCT, BF), TURN, TURN32]
-    return call(self_backward_start_kernel, outs, scratch, 25 * unit, core, [w], args)
-
-
-def self_backward_end(core, *args):
+def self_backward(core, w, *args):
     outs = [HALVES, HALVES, TOKB, TOKB, TOKB]
-    scratch = [PROBS, PROBS, ((8, D), F32), TURN, TURN32]
-    views = {i: (EVERY, LATE) for i in (0, 1, 2, 3)} | {i: (EVERY, EARLY) for i in (7, 8, 9)}
-    return call(self_backward_end_kernel, outs, scratch, 12 * unit, core, [], args, views)
+    scratch = [TOKB, TOKB, (STAT, BF), PROBS, PROBS, (OCT, BF), ((8, D), F32), TURN, TURN32]
+    return call(self_backward_kernel, outs, scratch, 37 * unit, core, [w], args)
 
 
 def input_grads(core, ws, wc, *args):
@@ -825,9 +783,12 @@
     return parts(mats[0], FIRST_ROWS), parts(mats[1], ROWS), parts(wide, 2 * ROWS), vec, others
 
 
-def plane_sum(mine, other):
+def plane_parts(mine, other):
     pair = (mine.astype(F32) + swap(other, 1).astype(F32)).astype(BF)
-    parts = lax.all_to_all(pair, "dp", 0, 0, tiled=True, axis_index_groups=groups_xy())
+    return lax.all_to_all(pair, "dp", 0, 0, tiled=True, axis_index_groups=groups_xy())
+
+
+def summed(parts):
     return jnp.sum(parts.astype(F32), axis=0).astype(BF)
 
 
@@ -835,11 +796,12 @@
     return (a.astype(F32) + b.astype(F32)).astype(BF)
 
 
-def first_round(part_c, part_f, z):
+def first_round(parts_c, part_f, z):
+    part_c = summed(parts_c)
     extra = part_c[ROWS:]
     part_1 = jnp.concatenate([part_f[:ROWS], extra])
     part_2 = jnp.concatenate([part_f[ROWS:], extra])
-    return part_c, part_1, part_2, along_z(jnp.where(z == 0, part_1, part_c), ((0, 1), (3, 2)))
+    return (part_c, part_1, part_2), jnp.where(z == 0, part_1, part_c)
 
 
 def finish_blocks(mine, other, blocks, grads, index):
@@ -930,19 +892,20 @@
         core, wc, dr2, oc, qc, kc, vc, qal_c, ka_cross, memory_turn, n1, vec, vg_f, r1
     )
     if blocked:
-        part_f = plane_sum(mine_f, other_f)
+        part_f = plane_parts(mine_f, other_f)
         part_f, mine_c, other_c, dr1 = lax.optimization_barrier((part_f, mine_c, other_c, dr1))
-        part_c = plane_sum(mine_c, other_c)
-    early = self_backward_start(core, ws, dr1, os, qs, ks, vs, qal_s, ka_self)
+        part_c = plane_parts(mine_c, other_c)
+        part_f, dr1 = lax.optimization_barrier((summed(part_f), dr1))
+    mine_s, other_s, dqs, dks, dvs = self_backward(
+        core, ws, dr1, os, qs, ks, vs, qal_s, ka_self, targets_turn
+    )
     if blocked:
-        part_c, early = lax.optimization_barrier((part_c, early))
-        blocks = first_round(part_c, part_f, index // 8)
-    mine_s, other_s, dqs, dks, dvs = self_backward_end(
-        core, qs, ks, vs, early[0], qal_s, early[1], ka_self, *early[2:5], targets_turn, early[5]
-    )
+        part_c, part_f, mine_s = lax.optimization_barrier((part_c, part_f, mine_s))
+        blocks, first_sent = first_round(part_c, part_f, index // 8)
+        first_sent, dr1 = lax.optimization_barrier((first_sent, dr1))
+        blocks += (along_z(first_sent, ((0, 1), (3, 2))),)
     input_grad, memory_grad = input_grads(core, ws, wc, dr1, dqs, dks, dvs, dkc, dvc)
     if blocked:
-        blocks, mine_s, other_s = lax.optimization_barrier((blocks, mine_s, other_s))
         grads = (input_grad, memory_grad)
         grad, vec_total, square, grads = finish_blocks(mine_s, other_s, blocks, grads, index)
         input_grad, memory_grad = grads

time: 272 us -> 266 us (0.978)
  Pallas kernels: 126 us -> 122 us
  waiting for transfers between devices: 65.7 us -> 62.2 us
    pallas_call x7 -> x6, Pallas kernels: 126 us -> 122 us  [call(): pl.pallas_call(body, out_shape=sds, in_specs=[pl.BlockSpec(memory_space=s...]
    ppermute x15, waiting for transfers between devices: 18.7 us -> 15.4 us  [swap(): return lax.ppermute(x, 'dp', [(i, i ^ bit) for i in range(32)])]
    unnamed x60 -> x62, local copies, waits for them, and re-layouts: 5.56 us -> 6.01 us
  transfers between devices with their start and end apart: 34 -> 34, of which waited for: 16 -> 16; matrix products, arithmetic and copies ran while one was open for 3% -> 4% of each run, Pallas kernels for 38% -> 38%
where the time goes in v4:
time: 266 us; the launch traced here: 262 us
  Pallas kernels  122 us (46%)
  waiting for transfers between devices  62.2 us (23%)
  starting transfers between devices  45.4 us (17%)
  other arithmetic  19.5 us (7%)
  local copies, waits for them, and re-layouts  8.66 us (3%)
  between operations  4.2 us (2%)
    pallas_call x6, Pallas kernels, call(): pl.pallas_call(body, out_shape=sds, in_specs=[pl.BlockSpec(memory_space=s...  122 us
    ppermute x8, waiting for transfers between devices, along_z(): lax.ppermute(x, 'dp', [(8 * a + p, 8 * b + p) for a, b in moves for p in...  25.9 us
    ppermute x8, starting transfers between devices, along_z(): lax.ppermute(x, 'dp', [(8 * a + p, 8 * b + p) for a, b in moves for p in...  18.2 us
    ppermute x15, waiting for transfers between devices, swap(): return lax.ppermute(x, 'dp', [(i, i ^ bit) for i in range(32)])  15.4 us
    all_to_all x2, starting transfers between devices, plane_parts(): lax.all_to_all(pair, 'dp', 0, 0, tiled=True, axis_index_groups=groups_xy())  7.76 us
    ppermute x1, waiting for transfers between devices, gather_blocks(): lax.ppermute(low[share - VEC_LEN:], 'dp', [(i, (i + 1) % 32) for i in ran...  7.35 us
    ppermute x15, starting transfers between devices, swap(): return lax.ppermute(x, 'dp', [(i, i ^ bit) for i in range(32)])  7.18 us
    ppermute x3, waiting for transfers between devices, to_corners(): return lax.ppermute(near[:near.shape[0] // 2], 'dp', sides(4, 2))  6.76 us
  transfers between devices with their start and end apart: 34, of which 16 were waited for; matrix products, arithmetic and copies ran while one was open for 4% of the time, Pallas kernels for 38%

profile of v4, /device:TPU:0, one launch (start us, length us, event | category | flops | bytes accessed | tf_op | source)
XLA Modules:
  0.0 262.3 jit_solution(7112660878772980040)
XLA Ops:
  2.4 7.4 %collective-permute-done = bf16[8704]{0:T(1024)(128)(2,1)S(1)} collective-permute-done((bf16[8704]{0:T(1024)(128)(2,1)S(1)}, bf16[8704]{0:T(1024)(128)(2,1)S(1)}, u32[]{:S(2)}, u32[]{:S(2)}) %collective-permute-start) | collective-permute-done | bytes 17440 | tf_op jit(solution)/shard_map/ppermute | solution.py:709
  17.3 3.0 %collective-permute-start.2 = (bf16[288,512]{1,0:T(8,128)(2,1)S(1)}, bf16[288,512]{1,0:T(8,128)(2,1)S(1)}, u32[]{:S(2)}, u32[]{:S(2)}) collective-permute-start(bf16[288,512]{1,0:T(8,128)(2,1)S(1)} %broadcast_select_fusion), channel_id=1, source_target_pairs={{0,8},{1,9},{2,10},{3,11},{4,12},{5,13},{6,14},{7,15},{8,16},{9,17... | collective-permute-start | bytes 884744 | tf_op jit(solution)/shard_map/ppermute | solution.py:701
  21.7 7.0 %collective-permute-done.3 = bf16[256,512]{1,0:T(8,128)(2,1)S(1)} collective-permute-done((bf16[256,512]{1,0:T(8,128)(2,1)S(1)}, bf16[256,512]{1,0:T(8,128)(2,1)S(1)}, u32[]{:S(2)}, u32[]{:S(2)}) %collective-permute-start.3) | collective-permute-done | bytes 262176 | tf_op jit(solution)/shard_map/ppermute | solution.py:701
  28.9 1.5 collective-permute-done.4.refs_1_
  33.3 8.5 %collective-permute-done.6 = bf16[256,512]{1,0:T(8,128)(2,1)S(1)} collective-permute-done((bf16[256,512]{1,0:T(8,128)(2,1)S(1)}, bf16[256,512]{1,0:T(8,128)(2,1)S(1)}, u32[]{:S(2)}, u32[]{:S(2)}) %collective-permute-start.6) | collective-permute-done | bytes 262176 | tf_op jit(solution)/shard_map/ppermute | solution.py:701
  43.6 1.5 collective-permute-start.8
  45.1 6.8 %collective-permute-done.13.refs_4_ = bf16[288,512]{1,0:T(8,128)(2,1)S(1)} collective-permute-done((bf16[288,512]{1,0:T(8,128)(2,1)S(1)}, bf16[288,512]{1,0:T(8,128)(2,1)S(1)}, u32[]{:S(2)}, u32[]{:S(2)}) %collective-permute-start.13) | collective-permute-done | bytes 294944 | tf_op jit(solution)/shard_map/ppermute | solution.py:755
  52.0 2.3 collective-permute-start.11
  56.4 14.8 %shard_map.159 = (bf16[1024,512]{1,0:T(8,128)(2,1)}, bf16[1024,512]{1,0:T(8,128)(2,1)}, bf16[1024,512]{1,0:T(8,128)(2,1)}, bf16[1024,512]{1,0:T(8,128)(2,1)}, bf...) custom-call(s32[2]{0:T(128)} %pad_add_fusion.core_ref, bf16[288,512]{1,0:T(8,128)(2,1)} %copy-done.1, ...), custom_call_target="tpu_custom_call" | custom-call | flops 10737418240 | bytes 3997696 | tf_op jit(solution)/shard_map/pallas_call | solution.py:619
  76.1 17.9 %shard_map.160 = (bf16[1024,512]{1,0:T(8,128)(2,1)}, bf16[1024,512]{1,0:T(8,128)(2,1)}, bf16[1024,512]{1,0:T(8,128)(2,1)}, bf16[1024,512]{1,0:T(8,128)(2,1)}, bf...) custom-call(s32[2]{0:T(128)} %pad_add_fusion.core_ref, bf16[256,512]{1,0:T(8,128)(2,1)} %copy-done.5, ...), custom_call_target="tpu_custom_call" | custom-call | flops 13421772800 | bytes 5832704 | tf_op jit(solution)/shard_map/pallas_call | solution.py:619
  94.5 1.5 collective-permute-done.19.refs_5_
  96.8 23.5 %shard_map.161 = (bf16[1024,512]{1,0:T(8,128)(2,1)}, bf16[4,512,512]{2,1,0:T(8,128)(2,1)}, bf16[4,512,512]{2,1,0:T(8,128)(2,1)}, f32[1024,512]{1,0:T(8,128)}, f32[32,512]{1,0:T(8,128)}) custom-call(s32[2]{0:T(128)} %pad_add_fusion.core_ref, bf16[512,512]{1,0:T(8,128)(2,1)} %copy-done.8, bf16[512,512]{1,0:T(8,128)(2,1)} %copy-done.9, ...), custom_call_target="tpu_custom_call" | custom-call | flops 13958643712 | bytes 7929856 | tf_op jit(solution)/shard_map/pallas_call | solution.py:619
  120.8 4.0 %collective-permute-done.20 = bf16[4,512,512]{2,1,0:T(8,128)(2,1)S(1)} collective-permute-done((bf16[4,512,512]{2,1,0:T(8,128)(2,1)}, bf16[4,512,512]{2,1,0:T(8,128)(2,1)S(1)}, u32[]{:S(2)}, u32[]{:S(2)}) %collective-permute-start.20) | collective-permute-done | bytes 2097184 | tf_op jit(solution)/shard_map/ppermute | solution.py:689
  124.8 3.5 %add_convert_fusion = bf16[4,512,512]{2,1,0:T(8,128)(2,1)} fusion(bf16[4,512,512]{2,1,0:T(8,128)(2,1)S(1)} %collective-permute-done.20, bf16[4,512,512]{2,1,0:T(8,128)(2,1)} %get-tuple-element.99), kind=kLoop, calls=%fused_computation | loop fusion | flops 4194304 | bytes 6291456 | tf_op jit(solution)/shard_map/convert_element_type | solution.py:787
  128.3 3.6 %all-to-all-start = ((bf16[4,512,512]{2,1,0:T(8,128)(2,1)}), bf16[4,512,512]{2,1,0:T(8,128)(2,1)S(1)}, u32[]{:S(2)}, u32[]{:S(2)}) async-start(bf16[4,512,512]{2,1,0:T(8,128)(2,1)} %add_convert_fusion), calls=%async_computation | async-start | bytes 4194304 | tf_op jit(solution)/shard_map/all_to_all | solution.py:788
  131.9 33.6 %shard_map.162 = (bf16[4,272,512]{2,1,0:T(8,128)(2,1)}, bf16[4,272,512]{2,1,0:T(8,128)(2,1)}, f32[1024,512]{1,0:T(8,128)}, bf16[1024,512]{1,0:T(8,128)(2,1)}, bf16[1024,512]{1,0:T(8,128)(2,1)}) custom-call(s32[2]{0:T(128)} %pad_add_fusion.core_ref, bf16[256,512]{1,0:T(8,128)(2,1)} %copy-done.5, bf16[256,512]{1,0:T(8,128)(2,1)} %copy-done.12, ...), custom_call_target="tpu_custom_call" | custom-call | flops 26843545600 | bytes 12713984 | tf_op jit(solution)/shard_map/pallas_call | solution.py:619
  166.7 2.1 collective-permute-done.21
  168.8 2.9 %add_convert_fusion.1 = bf16[4,272,512]{2,1,0:T(8,128)(2,1)} fusion(bf16[4,272,512]{2,1,0:T(8,128)(2,1)} %collective-permute-done.21, bf16[4,272,512]{2,1,0:T(8,128)(2,1)} %get-tuple-element.113), kind=kLoop, calls=%fused_computation.1 | loop fusion | flops 2228224 | bytes 3342336 | tf_op jit(solution)/shard_map/convert_element_type | solution.py:787
  171.7 4.2 %all-to-all-start.1 = ((bf16[4,272,512]{2,1,0:T(8,128)(2,1)}), bf16[4,272,512]{2,1,0:T(8,128)(2,1)S(1)}, u32[]{:S(2)}, u32[]{:S(2)}) async-start(bf16[4,272,512]{2,1,0:T(8,128)(2,1)} %add_convert_fusion.1), calls=%async_computation.1 | async-start | bytes 2228224 | tf_op jit(solution)/shard_map/all_to_all | solution.py:788
  175.8 23.7 %shard_map.163 = (bf16[4,272,512]{2,1,0:T(8,128)(2,1)}, bf16[4,272,512]{2,1,0:T(8,128)(2,1)}, bf16[1024,512]{1,0:T(8,128)(2,1)}, bf16[1024,512]{1,0:T(8,128)(2,1)}, bf16[1024,512]{1,0:T(8,128)(2,1)}) custom-call(s32[2]{0:T(128)} %pad_add_fusion.core_ref, bf16[288,512]{1,0:T(8,128)(2,1)} %copy-done.1, bf16[288,512]{1,0:T(8,128)(2,1)} %copy-done.10, ...), custom_call_target="tpu_custom_call" | custom-call | flops 19864223744 | bytes 10223616 | tf_op jit(solution)/shard_map/pallas_call | solution.py:619
  200.0 2.8 %collective-permute-start.26 = (bf16[272,512]{1,0:T(8,128)(2,1)S(1)}, bf16[272,512]{1,0:T(8,128)(2,1)S(1)}, u32[]{:S(2)}, u32[]{:S(2)}) collective-permute-start(bf16[272,512]{1,0:T(8,128)(2,1)S(1)} %broadcast_select_fusion.1), channel_id=1, source_target_pairs={{0,8},{1,9},{2,10},{3,11},{4,12},{5,13},{6,14},{7,15},{24,16},{25,... | collective-permute-start | bytes 835592 | tf_op jit(solution)/shard_map/ppermute | solution.py:701
  204.2 2.1 collective-permute-start.23
  207.8 8.7 %shard_map.164 = (bf16[1024,512]{1,0:T(8,128)(2,1)}, bf16[1024,512]{1,0:T(8,128)(2,1)}) custom-call(s32[2]{0:T(128)} %pad_add_fusion.core_ref, bf16[288,512]{1,0:T(8,128)(2,1)} %copy-done.1, bf16[288,512]{1,0:T(8,128)(2,1)} %copy-done.10, bf16[576,512]{1,0:T(8,128)(2,1)} %copy-done.13, bf16[576,512]{1,0:T(8,128)(2,1)} %copy-done.17, ...), custom_call_target="tpu_custom_call" | custom-call | flops 3221225472 | bytes 11796480 | tf_op jit(solution)/shard_map/pallas_call | solution.py:619
  216.6 4.0 %collective-permute-done.25 = bf16[272,512]{1,0:T(8,128)(2,1)S(1)} collective-permute-done((bf16[272,512]{1,0:T(8,128)(2,1)S(1)}, bf16[272,512]{1,0:T(8,128)(2,1)S(1)}, u32[]{:S(2)}, u32[]{:S(2)}) %collective-permute-start.25) | collective-permute-done | bytes 278560 | tf_op jit(solution)/shard_map/ppermute | solution.py:689
  224.7 4.6 %collective-permute-start.28 = (bf16[272,512]{1,0:T(8,128)(2,1)S(1)}, bf16[272,512]{1,0:T(8,128)(2,1)S(1)}, u32[]{:S(2)}, u32[]{:S(2)}) collective-permute-start(bf16[272,512]{1,0:T(8,128)(2,1)S(1)} %get-tuple-element.160), channel_id=1, source_target_pairs={{0,8},{1,9},{2,10},{3,11},{4,12},{5,13},{6,14},{7,15},{8,16},{9,17... | collective-permute-start | bytes 835592 | tf_op jit(solution)/shard_map/ppermute | solution.py:701
  229.2 2.6 collective-permute-done.27
  231.8 1.8 collective-permute-done.28
  233.9 2.5 collective-permute-start.29
  236.4 5.0 %collective-permute-done.29 = bf16[272,512]{1,0:T(8,128)(2,1)S(1)} collective-permute-done((bf16[272,512]{1,0:T(8,128)(2,1)S(1)}, bf16[272,512]{1,0:T(8,128)(2,1)S(1)}, u32[]{:S(2)}, u32[]{:S(2)}) %collective-permute-start.29) | collective-permute-done | bytes 278560 | tf_op jit(solution)/shard_map/ppermute | solution.py:701
  244.5 3.2 %all-to-all-start.2 = ((f32[32,8,128]{2,1,0:T(8,128)}), f32[32,8,128]{2,1,0:T(8,128)S(1)}, u32[]{:S(2)}, u32[]{:S(2)}) async-start(f32[32,8,128]{2,1,0:T(8,128)} %broadcast_in_dim.30), calls=%async_computation.2 | async-start | bytes 262144 | tf_op jit(solution)/shard_map/all_to_all | solution.py:835
  249.2 6.8 %all-to-all-done.2 = f32[32,8,128]{2,1,0:T(8,128)S(1)} async-done(((f32[32,8,128]{2,1,0:T(8,128)}), f32[32,8,128]{2,1,0:T(8,128)S(1)}, u32[]{:S(2)}, u32[]{:S(2)}) %all-to-all-start.2) | async-done | bytes 131104 | tf_op jit(solution)/shard_map/all_to_all | solution.py:835
  258.8 2.1 fusion.26
  (167 shorter events, 38.6 us)
Async XLA Ops:
  1.9 7.8 %collective-permute-start = (bf16[8704]{0:T(1024)(128)(2,1)S(1)}, bf16[8704]{0:T(1024)(128)(2,1)S(1)}, u32[]{:S(2)}, u32[]{:S(2)}) collective-permute-start(bf16[8704]{0:T(1024)(128)(2,1)S(1)} %slice.142), channel_id=1, source_target_pairs={{0,1},{1,2},{2,3},{3,4},{4,5},{5,6},{6,7},{7,8},{8,9},{9,10},{10,1... | collective-permute-start | bytes 52232 | tf_op jit(solution)/shard_map/ppermute | solution.py:709
  10.5 6.8 %collective-permute-start.1 = (bf16[288,512]{1,0:T(8,128)(2,1)S(1)}, bf16[288,512]{1,0:T(8,128)(2,1)S(1)}, u32[]{:S(2)}, u32[]{:S(2)}) collective-permute-start(bf16[288,512]{1,0:T(8,128)(2,1)S(1)} %fusion.9), channel_id=1, source_target_pairs={{0,16},{1,17},{2,18},{3,19},{4,20},{5,21},{6,22},{7,23},{8,0},{9,1... | collective-permute-start | bytes 884744 | tf_op jit(solution)/shard_map/ppermute | solution.py:701
  17.3 11.3 %collective-permute-start.2 = (bf16[288,512]{1,0:T(8,128)(2,1)S(1)}, bf16[288,512]{1,0:T(8,128)(2,1)S(1)}, u32[]{:S(2)}, u32[]{:S(2)}) collective-permute-start(bf16[288,512]{1,0:T(8,128)(2,1)S(1)} %broadcast_select_fusion), channel_id=1, source_target_pairs={{0,8},{1,9},{2,10},{3,11},{4,12},{5,13},{6,14},{7,15},{8,16},{9,17... | collective-permute-start | bytes 884744 | tf_op jit(solution)/shard_map/ppermute | solution.py:701
  20.4 8.3 %collective-permute-start.3 = (bf16[256,512]{1,0:T(8,128)(2,1)S(1)}, bf16[256,512]{1,0:T(8,128)(2,1)S(1)}, u32[]{:S(2)}, u32[]{:S(2)}) collective-permute-start(bf16[256,512]{1,0:T(8,128)(2,1)S(1)} %slice_select_fusion), channel_id=1, source_target_pairs={{24,16},{25,17},{26,18},{27,19},{28,20},{29,21},{30,22},{31,23},{1... | collective-permute-start | bytes 786440 | tf_op jit(solution)/shard_map/ppermute | solution.py:701
  30.5 11.3 %collective-permute-start.5 = (bf16[576,512]{1,0:T(8,128)(2,1)S(1)}, bf16[576,512]{1,0:T(8,128)(2,1)S(1)}, u32[]{:S(2)}, u32[]{:S(2)}) collective-permute-start(bf16[576,512]{1,0:T(8,128)(2,1)S(1)} %pad_maximum_fusion.1), channel_id=1, source_target_pairs={{0,2},{1,5},{2,0},{3,7},{4,6},{5,1},{6,4},{7,3},{8,10},{9,13},{10,... | collective-permute-start | bytes 1769480 | tf_op jit(solution)/shard_map/ppermute | solution.py:751
  31.8 10.0 %collective-permute-start.6 = (bf16[256,512]{1,0:T(8,128)(2,1)S(1)}, bf16[256,512]{1,0:T(8,128)(2,1)S(1)}, u32[]{:S(2)}, u32[]{:S(2)}) collective-permute-start(bf16[256,512]{1,0:T(8,128)(2,1)S(1)} %broadcast_select_fusion.2), channel_id=1, source_target_pairs={{8,0},{9,1},{10,2},{11,3},{12,4},{13,5},{14,6},{15,7},{16,24},{17,... | collective-permute-start | bytes 786440 | tf_op jit(solution)/shard_map/ppermute | solution.py:701
  42.0 9.8 %collective-permute-start.10 = (bf16[512,512]{1,0:T(8,128)(2,1)S(1)}, bf16[512,512]{1,0:T(8,128)(2,1)S(1)}, u32[]{:S(2)}, u32[]{:S(2)}) collective-permute-start(bf16[512,512]{1,0:T(8,128)(2,1)S(1)} %pad_maximum_fusion.3.refs_0_), channel_id=1, source_target_pairs={{0,1},{1,0},{2,3},{3,2},{4,5},{5,4},{6,7},{7,6},{8,9},{9,8},{10,11... | collective-permute-start | bytes 1572872 | tf_op jit(solution)/shard_map/ppermute | solution.py:689
  42.6 11.7 %collective-permute-start.12 = (bf16[576,512]{1,0:T(8,128)(2,1)S(1)}, bf16[576,512]{1,0:T(8,128)(2,1)S(1)}, u32[]{:S(2)}, u32[]{:S(2)}) collective-permute-start(bf16[576,512]{1,0:T(8,128)(2,1)S(1)} %collective-permute-done.5.refs_2_), channel_id=1, source_target_pairs={{0,1},{1,0},{2,3},{3,2},{4,5},{5,4},{6,7},{7,6},{8,9},{9,8},{10,11... | collective-permute-start | bytes 1769480 | tf_op jit(solution)/shard_map/ppermute | solution.py:689
  42.7 9.2 %collective-permute-start.13 = (bf16[288,512]{1,0:T(8,128)(2,1)S(1)}, bf16[288,512]{1,0:T(8,128)(2,1)S(1)}, u32[]{:S(2)}, u32[]{:S(2)}) collective-permute-start(bf16[288,512]{1,0:T(8,128)(2,1)S(1)} %slice.112), channel_id=1, source_target_pairs={{0,4},{1,3},{2,6},{3,1},{4,0},{5,7},{6,2},{7,5},{8,12},{9,11},{10,... | collective-permute-start | bytes 884744 | tf_op jit(solution)/shard_map/ppermute | solution.py:755
  43.6 11.5 %collective-permute-start.8 = (bf16[512,512]{1,0:T(8,128)(2,1)S(1)}, bf16[512,512]{1,0:T(8,128)(2,1)S(1)}, u32[]{:S(2)}, u32[]{:S(2)}) collective-permute-start(bf16[512,512]{1,0:T(8,128)(2,1)S(1)} %pad_maximum_fusion.2), channel_id=1, source_target_pairs={{0,2},{1,5},{2,0},{3,7},{4,6},{5,1},{6,4},{7,3},{8,10},{9,13},{10,... | collective-permute-start | bytes 1572872 | tf_op jit(solution)/shard_map/ppermute | solution.py:751
  51.9 2.5 collective-permute-start.14
  52.0 19.2 %collective-permute-start.11 = (bf16[1024,512]{1,0:T(8,128)(2,1)S(1)}, bf16[1024,512]{1,0:T(8,128)(2,1)S(1)}, u32[]{:S(2)}, u32[]{:S(2)}) collective-permute-start(bf16[1024,512]{1,0:T(8,128)(2,1)S(1)} %pad_maximum_fusion), channel_id=1, source_target_pairs={{0,2},{1,5},{2,0},{3,7},{4,6},{5,1},{6,4},{7,3},{8,10},{9,13},{10,... | collective-permute-start | bytes 3145736 | tf_op jit(solution)/shard_map/ppermute | solution.py:751
  56.0 15.3 %collective-permute-start.9 = (bf16[256,512]{1,0:T(8,128)(2,1)S(1)}, bf16[256,512]{1,0:T(8,128)(2,1)}, u32[]{:S(2)}, u32[]{:S(2)}) collective-permute-start(bf16[256,512]{1,0:T(8,128)(2,1)S(1)} %slice.145), channel_id=1, source_target_pairs={{0,4},{1,3},{2,6},{3,1},{4,0},{5,7},{6,2},{7,5},{8,12},{9,11},{10,... | collective-permute-start | bytes 786440 | tf_op jit(solution)/shard_map/ppermute | solution.py:755
  71.3 3.3 %collective-permute-start.17 = (bf16[512,512]{1,0:T(8,128)(2,1)S(1)}, bf16[512,512]{1,0:T(8,128)(2,1)S(1)}, u32[]{:S(2)}, u32[]{:S(2)}) collective-permute-start(bf16[512,512]{1,0:T(8,128)(2,1)S(1)} %copy-done.16), channel_id=1, source_target_pairs={{0,1},{1,0},{2,3},{3,2},{4,5},{5,4},{6,7},{7,6},{8,9},{9,8},{10,11... | collective-permute-start | bytes 1572872 | tf_op jit(solution)/shard_map/ppermute | solution.py:689
  72.0 2.5 collective-permute-start.18
  72.2 23.9 %collective-permute-start.15 = (bf16[1024,512]{1,0:T(8,128)(2,1)S(1)}, bf16[1024,512]{1,0:T(8,128)(2,1)}, u32[]{:S(2)}, u32[]{:S(2)}) collective-permute-start(bf16[1024,512]{1,0:T(8,128)(2,1)S(1)} %collective-permute-done.11.refs_2_), channel_id=1, source_target_pairs={{0,1},{1,0},{2,3},{3,2},{4,5},{5,4},{6,7},{7,6},{8,9},{9,8},{10,11... | collective-permute-start | bytes 3145736 | tf_op jit(solution)/shard_map/ppermute | solution.py:689
  72.7 21.4 %collective-permute-start.16 = (bf16[512,512]{1,0:T(8,128)(2,1)S(1)}, bf16[512,512]{1,0:T(8,128)(2,1)S(1)}, u32[]{:S(2)}, u32[]{:S(2)}) collective-permute-start(bf16[512,512]{1,0:T(8,128)(2,1)S(1)} %slice.121), channel_id=1, source_target_pairs={{0,4},{1,3},{2,6},{3,1},{4,0},{5,7},{6,2},{7,5},{8,12},{9,11},{10,... | collective-permute-start | bytes 1572872 | tf_op jit(solution)/shard_map/ppermute | solution.py:755
  94.1 2.0 collective-permute-start.19
  120.3 4.4 %collective-permute-start.20 = (bf16[4,512,512]{2,1,0:T(8,128)(2,1)}, bf16[4,512,512]{2,1,0:T(8,128)(2,1)S(1)}, u32[]{:S(2)}, u32[]{:S(2)}) collective-permute-start(bf16[4,512,512]{2,1,0:T(8,128)(2,1)} %get-tuple-element.100), channel_id=1, source_target_pairs={{0,1},{1,0},{2,3},{3,2},{4,5},{5,4},{6,7},{7,6},{8,9},{9,8},{10,11... | collective-permute-start | bytes 6291464 | tf_op jit(solution)/shard_map/ppermute | solution.py:689
  128.3 37.3 %all-to-all-start = ((bf16[4,512,512]{2,1,0:T(8,128)(2,1)}), bf16[4,512,512]{2,1,0:T(8,128)(2,1)S(1)}, u32[]{:S(2)}, u32[]{:S(2)}) async-start(bf16[4,512,512]{2,1,0:T(8,128)(2,1)} %add_convert_fusion), calls=%async_computation | async-start | bytes 4194304 | tf_op jit(solution)/shard_map/all_to_all | solution.py:788
  165.6 3.2 %collective-permute-start.21 = (bf16[4,272,512]{2,1,0:T(8,128)(2,1)}, bf16[4,272,512]{2,1,0:T(8,128)(2,1)}, u32[]{:S(2)}, u32[]{:S(2)}) collective-permute-start(bf16[4,272,512]{2,1,0:T(8,128)(2,1)} %get-tuple-element.114), channel_id=1, source_target_pairs={{0,1},{1,0},{2,3},{3,2},{4,5},{5,4},{6,7},{7,6},{8,9},{9,8},{10,11... | collective-permute-start | bytes 3342344 | tf_op jit(solution)/shard_map/ppermute | solution.py:689
  171.7 27.9 %all-to-all-start.1 = ((bf16[4,272,512]{2,1,0:T(8,128)(2,1)}), bf16[4,272,512]{2,1,0:T(8,128)(2,1)S(1)}, u32[]{:S(2)}, u32[]{:S(2)}) async-start(bf16[4,272,512]{2,1,0:T(8,128)(2,1)} %add_convert_fusion.1), calls=%async_computation.1 | async-start | bytes 2228224 | tf_op jit(solution)/shard_map/all_to_all | solution.py:788
  199.5 3.3 %collective-permute-start.22 = (bf16[4,272,512]{2,1,0:T(8,128)(2,1)}, bf16[4,272,512]{2,1,0:T(8,128)(2,1)}, u32[]{:S(2)}, u32[]{:S(2)}) collective-permute-start(bf16[4,272,512]{2,1,0:T(8,128)(2,1)} %get-tuple-element.127), channel_id=1, source_target_pairs={{0,1},{1,0},{2,3},{3,2},{4,5},{5,4},{6,7},{7,6},{8,9},{9,8},{10,11... | collective-permute-start | bytes 3342344 | tf_op jit(solution)/shard_map/ppermute | solution.py:689
  200.0 23.1 %collective-permute-start.26 = (bf16[272,512]{1,0:T(8,128)(2,1)S(1)}, bf16[272,512]{1,0:T(8,128)(2,1)S(1)}, u32[]{:S(2)}, u32[]{:S(2)}) collective-permute-start(bf16[272,512]{1,0:T(8,128)(2,1)S(1)} %broadcast_select_fusion.1), channel_id=1, source_target_pairs={{0,8},{1,9},{2,10},{3,11},{4,12},{5,13},{6,14},{7,15},{24,16},{25,... | collective-permute-start | bytes 835592 | tf_op jit(solution)/shard_map/ppermute | solution.py:701
  204.2 12.4 %collective-permute-start.23 = (bf16[272,512]{1,0:T(8,128)(2,1)S(1)}, bf16[272,512]{1,0:T(8,128)(2,1)S(1)}, u32[]{:S(2)}, u32[]{:S(2)}) collective-permute-start(bf16[272,512]{1,0:T(8,128)(2,1)S(1)} %get-tuple-element.149), channel_id=1, source_target_pairs={{0,2},{1,3},{2,0},{3,1},{4,6},{5,7},{6,4},{7,5},{8,10},{9,11},{10,... | collective-permute-start | bytes 835592 | tf_op jit(solution)/shard_map/ppermute | solution.py:689
  206.3 14.3 %collective-permute-start.25 = (bf16[272,512]{1,0:T(8,128)(2,1)S(1)}, bf16[272,512]{1,0:T(8,128)(2,1)S(1)}, u32[]{:S(2)}, u32[]{:S(2)}) collective-permute-start(bf16[272,512]{1,0:T(8,128)(2,1)S(1)} %get-tuple-element.150), channel_id=1, source_target_pairs={{0,6},{1,7},{2,4},{3,5},{4,2},{5,3},{6,0},{7,1},{8,14},{9,15},{10,... | collective-permute-start | bytes 835592 | tf_op jit(solution)/shard_map/ppermute | solution.py:689
  207.8 14.2 %collective-permute-start.24 = (bf16[272,512]{1,0:T(8,128)(2,1)S(1)}, bf16[272,512]{1,0:T(8,128)(2,1)S(1)}, u32[]{:S(2)}, u32[]{:S(2)}) collective-permute-start(bf16[272,512]{1,0:T(8,128)(2,1)S(1)} %get-tuple-element.151), channel_id=1, source_target_pairs={{0,4},{1,5},{2,6},{3,7},{4,0},{5,1},{6,2},{7,3},{8,12},{9,13},{10,... | collective-permute-start | bytes 835592 | tf_op jit(solution)/shard_map/ppermute | solution.py:689
  223.4 8.4 %collective-permute-start.27 = (bf16[272,512]{1,0:T(8,128)(2,1)S(1)}, bf16[272,512]{1,0:T(8,128)(2,1)S(1)}, u32[]{:S(2)}, u32[]{:S(2)}) collective-permute-start(bf16[272,512]{1,0:T(8,128)(2,1)S(1)} %get-tuple-element.159), channel_id=1, source_target_pairs={{8,0},{9,1},{10,2},{11,3},{12,4},{13,5},{14,6},{15,7},{16,8},{17,9... | collective-permute-start | bytes 835592 | tf_op jit(solution)/shard_map/ppermute | solution.py:701
  224.7 9.0 %collective-permute-start.28 = (bf16[272,512]{1,0:T(8,128)(2,1)S(1)}, bf16[272,512]{1,0:T(8,128)(2,1)S(1)}, u32[]{:S(2)}, u32[]{:S(2)}) collective-permute-start(bf16[272,512]{1,0:T(8,128)(2,1)S(1)} %get-tuple-element.160), channel_id=1, source_target_pairs={{0,8},{1,9},{2,10},{3,11},{4,12},{5,13},{6,14},{7,15},{8,16},{9,17... | collective-permute-start | bytes 835592 | tf_op jit(solution)/shard_map/ppermute | solution.py:701
  233.9 7.5 %collective-permute-start.29 = (bf16[272,512]{1,0:T(8,128)(2,1)S(1)}, bf16[272,512]{1,0:T(8,128)(2,1)S(1)}, u32[]{:S(2)}, u32[]{:S(2)}) collective-permute-start(bf16[272,512]{1,0:T(8,128)(2,1)S(1)} %fusion.15), channel_id=1, source_target_pairs={{16,0},{17,1},{18,2},{19,3},{20,4},{21,5},{22,6},{23,7},{0,8},{1,9... | collective-permute-start | bytes 835592 | tf_op jit(solution)/shard_map/ppermute | solution.py:701
  244.5 11.4 %all-to-all-start.2 = ((f32[32,8,128]{2,1,0:T(8,128)}), f32[32,8,128]{2,1,0:T(8,128)S(1)}, u32[]{:S(2)}, u32[]{:S(2)}) async-start(f32[32,8,128]{2,1,0:T(8,128)} %broadcast_in_dim.30), calls=%async_computation.2 | async-start | bytes 262144 | tf_op jit(solution)/shard_map/all_to_all | solution.py:835
  247.7 11.0 %collective-permute-start.30 = (f32[8704]{0:T(1024)S(1)}, f32[8704]{0:T(1024)S(1)}, u32[]{:S(2)}, u32[]{:S(2)}) collective-permute-start(f32[8704]{0:T(1024)S(1)} %slice.141), channel_id=1, source_target_pairs={{1,0},{2,1},{3,2},{4,3},{5,4},{6,5},{7,6},{8,7},{9,8},{10,9},{11,1... | collective-permute-start | bytes 104456 | tf_op jit(solution)/shard_map/ppermute | solution.py:826
  (28 other events, 225.9 us)
